TPU v7x, 32 devices: a whole 2x2x4 slice. The times are simulated.
32 devices in a mesh: pipe: 2 (over core), expert: 16 (over z, y, x).
Axes of the slice: x: 2, y: 2, z: 4, core: 2. Of those that a mesh axis runs over, the one named last changes fastest.
Arguments:
- tokens: bfloat16 [2, 1792, 4096], P(None, 'expert'), may hold values from -6 to 6
- cotangent: bfloat16 [2, 1792, 4096], P(None, 'expert'), may hold values from -6 to 6
- expert_ids: int32 [2, 2, 1792, 2], P('pipe', None, 'expert'), may hold values from 0 to 15, all different within a row; in each aligned block of 112 rows (0 to 111, 112 to 223, ..., all dimensions but the last counted through in order) at most 17 rows name the same one
- gate_prob: float32 [2, 2, 1792, 2], P('pipe', None, 'expert'), may hold values from 0.25 to 1
- up_weight: bfloat16 [2, 16, 4096, 768], P('pipe', 'expert'), may hold values from -0.09375 to 0.09375
- down_weight: bfloat16 [2, 16, 768, 4096], P('pipe', 'expert'), may hold values from -0.21875 to 0.21875
Outputs:
- input_grad: bfloat16 [2, 2, 1792, 4096], P('pipe', None, 'expert')
- down_grad: bfloat16 [2, 16, 768, 4096], P('pipe', 'expert')
Inputs may be any that keep to these rules, and one draw needn't show every extreme that they name: `expert_ids`: for each section and micro-batch, the 112 rows of one device name no expert more than 17 times, a bound that some block reaches; the two ids of a row differ.
All inputs are finite; a program needn't handle non-finite values.
Results may differ from a plain program's by a relative error of at most 0.015.
Values may be sent and summed in bfloat16 or wider, within the bound.
No kernel may reach another device: no remote copies, remote signals or barrier semaphores. Data moves between devices by JAX's collectives and lax.ppermute only.
A program may use at most 192 MiB of HBM per device.

v0:
```python
import jax
import jax.numpy as jnp
from jax import lax
from jax.sharding import PartitionSpec as P

EPSILON = 1e-06
ROOT_HALF = 0.7071067811865476
INV_ROOT_TAU = 0.3989422804014327


def from_behind(value, axis, steps):
    count = lax.axis_size(axis)
    leading, last = (max(0, -steps), min(count, count - steps))
    return lax.ppermute(value, axis, [(source, source + steps) for source in range(leading, last)])


def gelu_value(values):
    return 0.5 * values * (1.0 + jax.scipy.special.erf(values * ROOT_HALF))


def gelu_slope(values):
    return (
        0.5 * (1.0 + jax.scipy.special.erf(values * ROOT_HALF))
        + values * jnp.exp(-0.5 * values * values) * INV_ROOT_TAU
    )


def normalize(carried):
    widened = carried.astype(jnp.float32)
    inverse_rms = lax.rsqrt(jnp.mean(widened * widened, axis=-1, keepdims=True) + EPSILON)
    return ((widened * inverse_rms).astype(jnp.bfloat16), inverse_rms)


def norm_back(carried, inverse_rms, upstream):
    widened = carried.astype(jnp.float32)
    inner = jnp.mean(widened * upstream, axis=-1, keepdims=True)
    return inverse_rms * upstream - widened * (inverse_rms * inverse_rms * inverse_rms) * inner


def slot_targets(chosen_ids, expert_count, capacity):
    flattened = chosen_ids.reshape(-1)
    onehot = (flattened[:, None] == jnp.arange(expert_count, dtype=jnp.int32)[None, :]).astype(
        jnp.int32
    )
    before = jnp.cumsum(onehot, axis=0) - onehot
    slot_index = jnp.sum(before * onehot, axis=1)
    return flattened * capacity + slot_index


def place_rows(values, targets, slot_total):
    return jnp.zeros((slot_total, values.shape[1]), values.dtype).at[targets].set(values)


def routing(id_block, prob_block, micro_index, expert_count, capacity):
    chosen_ids = lax.dynamic_index_in_dim(id_block, micro_index, 0, keepdims=False)
    weights = lax.dynamic_index_in_dim(prob_block, micro_index, 0, keepdims=False)
    return (slot_targets(chosen_ids, expert_count, capacity), weights)


def forward_step(carried, targets, weights, up_matrix, down_matrix, expert_count, capacity):
    row_count = carried.shape[0]
    feature_count = carried.shape[1]
    slot_total = expert_count * capacity
    normed, inverse_rms = normalize(carried)
    outgoing = place_rows(jnp.repeat(normed, 2, axis=0), targets, slot_total).reshape(
        expert_count, capacity, feature_count
    )
    received = lax.all_to_all(outgoing, "expert", split_axis=0, concat_axis=0, tiled=True)
    flattened = received.reshape(-1, feature_count)
    hidden = jnp.dot(flattened, up_matrix, preferred_element_type=jnp.float32)
    activated = gelu_value(hidden).astype(jnp.bfloat16)
    answer = jnp.dot(activated, down_matrix, preferred_element_type=jnp.float32).astype(
        jnp.bfloat16
    )
    returned = lax.all_to_all(
        answer.reshape(received.shape), "expert", split_axis=0, concat_axis=0, tiled=True
    )
    received = None
    picked = returned.reshape(slot_total, feature_count)[targets].reshape(
        row_count, 2, feature_count
    )
    mixed_sum = carried.astype(jnp.float32) + jnp.sum(
        weights[:, :, None] * picked.astype(jnp.float32), axis=1
    )
    return (mixed_sum.astype(jnp.bfloat16), received)


def backward_step(
    carried, incoming, targets, weights, up_matrix, down_matrix, expert_count, capacity
):
    row_count = carried.shape[0]
    feature_count = carried.shape[1]
    slot_total = expert_count * capacity
    normed, inverse_rms = normalize(carried)
    weighted = (weights[:, :, None] * incoming.astype(jnp.float32)[:, None, :]).astype(jnp.bfloat16)
    grad_out = place_rows(
        weighted.reshape(2 * row_count, feature_count), targets, slot_total
    ).reshape(expert_count, capacity, feature_count)
    outgoing = place_rows(jnp.repeat(normed, 2, axis=0), targets, slot_total).reshape(
        expert_count, capacity, feature_count
    )
    received, grad_in = (
        lax.all_to_all(outgoing, "expert", split_axis=0, concat_axis=0, tiled=True),
        lax.all_to_all(grad_out, "expert", split_axis=0, concat_axis=0, tiled=True),
    )
    row_block = received.reshape(slot_total, feature_count)
    grad_block = grad_in.reshape(slot_total, feature_count)
    hidden = jnp.dot(row_block, up_matrix, preferred_element_type=jnp.float32)
    activated = gelu_value(hidden).astype(jnp.bfloat16)
    back_act = lax.dot_general(
        grad_block, down_matrix, (((1,), (1,)), ((), ())), preferred_element_type=jnp.float32
    )
    back_hidden = (back_act * gelu_slope(hidden)).astype(jnp.bfloat16)
    back_pick = lax.dot_general(
        back_hidden, up_matrix, (((1,), (1,)), ((), ())), preferred_element_type=jnp.float32
    ).astype(jnp.bfloat16)
    down_part = lax.dot_general(
        activated, grad_block, (((0,), (0,)), ((), ())), preferred_element_type=jnp.float32
    )
    back_home = lax.all_to_all(
        back_pick.reshape(expert_count, capacity, feature_count),
        "expert",
        split_axis=0,
        concat_axis=0,
        tiled=True,
    )
    picked = back_home.reshape(slot_total, feature_count)[targets].reshape(
        row_count, 2, feature_count
    )
    back_normed = jnp.sum(picked.astype(jnp.float32), axis=1)
    previous = (incoming.astype(jnp.float32) + norm_back(carried, inverse_rms, back_normed)).astype(
        jnp.bfloat16
    )
    return (previous, down_part)


def shards(tokens, cotangent, expert_ids, gate_prob, up_weight, down_weight):
    segment_count = lax.axis_size("pipe")
    segment_index = lax.axis_index("pipe")
    expert_count = lax.axis_size("expert")
    micro_count = tokens.shape[0]
    row_count = tokens.shape[1]
    feature_count = tokens.shape[2]
    capacity = 5 * row_count // (2 * expert_count)
    hidden_count = up_weight.shape[3]
    up_matrix = up_weight[0, 0]
    down_matrix = down_weight[0, 0]
    tick_total = micro_count + segment_count - 1
    saved_in = jnp.zeros((micro_count, row_count, feature_count), jnp.bfloat16)
    arriving = jnp.zeros((row_count, feature_count), jnp.bfloat16)
    for tick_number in range(tick_total):
        offset = tick_number - segment_index
        micro_index = jnp.clip(offset, 0, micro_count - 1)
        is_valid = (offset >= 0) & (offset < micro_count)
        own_input = tokens[min(tick_number, micro_count - 1)]
        carried = jnp.where(segment_index == 0, own_input, arriving)
        targets, weights = routing(expert_ids[0], gate_prob[0], micro_index, expert_count, capacity)
        mixed, received = forward_step(
            carried, targets, weights, up_matrix, down_matrix, expert_count, capacity
        )
        saved_in = jnp.where(
            is_valid, lax.dynamic_update_index_in_dim(saved_in, carried, micro_index, 0), saved_in
        )
        if tick_number + 1 < tick_total:
            arriving = from_behind(mixed, "pipe", 1)
    grad_store = jnp.zeros((micro_count, row_count, feature_count), jnp.bfloat16)
    down_total = jnp.zeros((hidden_count, feature_count), jnp.float32)
    coming = jnp.zeros((row_count, feature_count), jnp.bfloat16)
    for tick_number in range(tick_total):
        offset = tick_number - (segment_count - 1 - segment_index)
        micro_index = jnp.clip(offset, 0, micro_count - 1)
        is_valid = (offset >= 0) & (offset < micro_count)
        own_input = cotangent[min(tick_number, micro_count - 1)]
        incoming = jnp.where(segment_index == segment_count - 1, own_input, coming)
        carried = lax.dynamic_index_in_dim(saved_in, micro_index, 0, keepdims=False)
        targets, weights = routing(expert_ids[0], gate_prob[0], micro_index, expert_count, capacity)
        previous, down_part = backward_step(
            carried, incoming, targets, weights, up_matrix, down_matrix, expert_count, capacity
        )
        down_total = jnp.where(is_valid, down_total + down_part, down_total)
        grad_store = jnp.where(
            is_valid,
            lax.dynamic_update_index_in_dim(grad_store, previous, micro_index, 0),
            grad_store,
        )
        if tick_number + 1 < tick_total:
            coming = from_behind(previous, "pipe", -1)
    return (grad_store[None], down_total.astype(jnp.bfloat16)[None, None])


def solution(mesh):
    placed = (
        P(None, "expert", None),
        P(None, "expert", None),
        P("pipe", None, "expert", None),
        P("pipe", None, "expert", None),
        P("pipe", "expert", None, None),
        P("pipe", "expert", None, None),
    )
    return jax.shard_map(
        shards,
        mesh=mesh,
        in_specs=placed,
        out_specs=(P("pipe", None, "expert", None), P("pipe", "expert", None, None)),
        check_vma=False,
    )
```

profile of v0, /device:TPU:13, one launch (start us, length us, event | category | flops | bytes accessed | tf_op | source)
XLA Modules:
  0.0 1204.9 jit_solution(338176688165180363)
XLA Ops:
  17.0 76.1 %all_to_all.65 = bf16[16,17,4096]{2,1,0:T(8,128)(2,1)} all-to-all(bf16[16,17,4096]{2,1,0:T(8,128)(2,1)S(1)} %reshape.509), channel_id=1, replica_groups=mesh['pipe'=2,'expert'=16] {'expert'}, dimensions={0} | all-to-all | bytes 4456448 | tf_op jit(solution)/shard_map/all_to_all | solution.py:68
  95.4 10.8 fusion.37
  117.0 68.3 %all-to-all-done.1 = bf16[16,17,4096]{2,1,0:T(8,128)(2,1)} async-done(((bf16[16,17,4096]{2,1,0:T(8,128)(2,1)}), bf16[16,17,4096]{2,1,0:T(8,128)(2,1)}, u32[]{:S(2)}, u32[]{:S(2)}) %all-to-all-start.1) | async-done | bytes 2228256 | tf_op jit(solution)/shard_map/all_to_all | solution.py:75
  195.6 7.9 multiply_reduce_fusion.1
  222.8 75.0 %all_to_all.66 = bf16[16,17,4096]{2,1,0:T(8,128)(2,1)} all-to-all(bf16[16,17,4096]{2,1,0:T(8,128)(2,1)} %reshape.516), channel_id=1, replica_groups=mesh['pipe'=2,'expert'=16] {'expert'}, dimensions={0} | all-to-all | bytes 4456448 | tf_op jit(solution)/shard_map/all_to_all | solution.py:68
  301.2 11.5 fusion.40
  342.2 49.6 %all-to-all-done.3 = bf16[16,17,4096]{2,1,0:T(8,128)(2,1)} async-done(((bf16[16,17,4096]{2,1,0:T(8,128)(2,1)}), bf16[16,17,4096]{2,1,0:T(8,128)(2,1)}, u32[]{:S(2)}, u32[]{:S(2)}) %all-to-all-start.3) | async-done | bytes 2228256 | tf_op jit(solution)/shard_map/all_to_all | solution.py:75
  443.4 23.9 %all-to-all-done.4 = bf16[16,17,4096]{2,1,0:T(8,128)(2,1)} async-done(((bf16[16,17,4096]{2,1,0:T(8,128)(2,1)}), bf16[16,17,4096]{2,1,0:T(8,128)(2,1)}, u32[]{:S(2)}, u32[]{:S(2)}) %all-to-all-start.4) | async-done | bytes 2228256 | tf_op jit(solution)/shard_map/all_to_all | solution.py:104
  475.2 66.9 %all-to-all-done.5 = bf16[16,17,4096]{2,1,0:T(8,128)(2,1)} async-done(((bf16[16,17,4096]{2,1,0:T(8,128)(2,1)}), bf16[16,17,4096]{2,1,0:T(8,128)(2,1)}, u32[]{:S(2)}, u32[]{:S(2)}) %all-to-all-start.5) | async-done | bytes 2228256 | tf_op jit(solution)/shard_map/all_to_all | solution.py:103
  550.8 11.8 fusion.28
  571.8 68.9 %all-to-all-done.6 = bf16[16,17,4096]{2,1,0:T(8,128)(2,1)} async-done(((bf16[16,17,4096]{2,1,0:T(8,128)(2,1)}), bf16[16,17,4096]{2,1,0:T(8,128)(2,1)}, u32[]{:S(2)}, u32[]{:S(2)}) %all-to-all-start.6) | async-done | bytes 2228256 | tf_op jit(solution)/shard_map/all_to_all | solution.py:120
  655.9 7.9 reduce_sum.185
  718.1 42.6 %all-to-all-done.8 = bf16[16,17,4096]{2,1,0:T(8,128)(2,1)} async-done(((bf16[16,17,4096]{2,1,0:T(8,128)(2,1)}), bf16[16,17,4096]{2,1,0:T(8,128)(2,1)}, u32[]{:S(2)}, u32[]{:S(2)}) %all-to-all-start.8) | async-done | bytes 2228256 | tf_op jit(solution)/shard_map/all_to_all | solution.py:103
  775.0 60.6 %all-to-all-done.7 = bf16[16,17,4096]{2,1,0:T(8,128)(2,1)} async-done(((bf16[16,17,4096]{2,1,0:T(8,128)(2,1)}), bf16[16,17,4096]{2,1,0:T(8,128)(2,1)}, u32[]{:S(2)}, u32[]{:S(2)}) %all-to-all-start.7) | async-done | bytes 2228256 | tf_op jit(solution)/shard_map/all_to_all | solution.py:104
  838.9 11.7 fusion.31
  877.1 51.7 %all-to-all-done.9 = bf16[16,17,4096]{2,1,0:T(8,128)(2,1)} async-done(((bf16[16,17,4096]{2,1,0:T(8,128)(2,1)}), bf16[16,17,4096]{2,1,0:T(8,128)(2,1)}, u32[]{:S(2)}, u32[]{:S(2)}) %all-to-all-start.9) | async-done | bytes 2228256 | tf_op jit(solution)/shard_map/all_to_all | solution.py:120
  953.6 7.9 reduce_sum.191
  967.0 14.7 %collective-permute-start.3 = (bf16[112,4096]{1,0:T(8,128)(2,1)S(1)}, bf16[112,4096]{1,0:T(8,128)(2,1)}, u32[]{:S(2)}, u32[]{:S(2)}) collective-permute-start(bf16[112,4096]{1,0:T(8,128)(2,1)S(1)} %get-tuple-element.8), channel_id=1, source_target_pairs={{16,0},{17,1},{18,2},{19,3},{20,4},{21,5},{22,6},{23,7},{24,8},{25... | collective-permute-start | bytes 2752520 | tf_op jit(solution)/shard_map/ppermute | solution.py:14
  1018.5 62.9 %all-to-all-done.10 = bf16[16,17,4096]{2,1,0:T(8,128)(2,1)} async-done(((bf16[16,17,4096]{2,1,0:T(8,128)(2,1)}), bf16[16,17,4096]{2,1,0:T(8,128)(2,1)}, u32[]{:S(2)}, u32[]{:S(2)}) %all-to-all-start.10) | async-done | bytes 2228256 | tf_op jit(solution)/shard_map/all_to_all | solution.py:104
  1084.8 11.5 fusion.34
  1105.9 8.2 fusion.151
  1123.6 12.8 %fusion.27 = bf16[1,1,768,4096]{3,2,1,0:T(8,128)(2,1)} fusion(bf16[272,4096]{1,0:T(8,128)(2,1)S(1)} %copy-done.10, f32[768,4096]{1,0:T(8,128)} %fusion.152, f32[768,4096]{1,0:T(8,128)} %fusion.151, pred[]{:T(512)S(6)} %and.19, pred[]{:T(512)S(6)} %and.23, pred[]{:T(512)S(6)} %and.24, f32[272,768]{1,0:T(8,128)S(1)} %fusion.13), kind=kOutput, calls=%fused_computation.42 | convolution fusion | flops 1731194880 | bytes 34521092 | tf_op jit(solution)/shard_map/dot_general | solution.py:117
  1136.4 39.5 %all-to-all-done.12 = bf16[16,17,4096]{2,1,0:T(8,128)(2,1)} async-done(((bf16[16,17,4096]{2,1,0:T(8,128)(2,1)}), bf16[16,17,4096]{2,1,0:T(8,128)(2,1)}, u32[]{:S(2)}, u32[]{:S(2)}) %all-to-all-start.12) | async-done | bytes 2228256 | tf_op jit(solution)/shard_map/all_to_all | solution.py:120
  1191.1 7.9 reduce_sum.196
  (227 shorter events, 392.3 us)
Async XLA Ops:
  109.6 7.1 copy-start.15
  109.6 75.7 %all-to-all-start.1 = ((bf16[16,17,4096]{2,1,0:T(8,128)(2,1)}), bf16[16,17,4096]{2,1,0:T(8,128)(2,1)}, u32[]{:S(2)}, u32[]{:S(2)}) async-start(bf16[16,17,4096]{2,1,0:T(8,128)(2,1)} %reshape.511), calls=%async_computation.1 | async-start | bytes 6291456 | tf_op jit(solution)/shard_map/all_to_all | solution.py:75
  195.6 7.9 copy-start.4
  203.7 4.8 collective-permute-start
  315.9 5.5 copy-start.8
  315.9 75.9 %all-to-all-start.3 = ((bf16[16,17,4096]{2,1,0:T(8,128)(2,1)}), bf16[16,17,4096]{2,1,0:T(8,128)(2,1)}, u32[]{:S(2)}, u32[]{:S(2)}) async-start(bf16[16,17,4096]{2,1,0:T(8,128)(2,1)} %reshape.518), calls=%async_computation.3 | async-start | bytes 6291456 | tf_op jit(solution)/shard_map/all_to_all | solution.py:75
  391.8 75.4 %all-to-all-start.4 = ((bf16[16,17,4096]{2,1,0:T(8,128)(2,1)}), bf16[16,17,4096]{2,1,0:T(8,128)(2,1)}, u32[]{:S(2)}, u32[]{:S(2)}) async-start(bf16[16,17,4096]{2,1,0:T(8,128)(2,1)} %reshape.522), calls=%async_computation.4 | async-start | bytes 6291456 | tf_op jit(solution)/shard_map/all_to_all | solution.py:104
  420.0 5.4 copy-start.5
  420.0 5.3 collective-permute-start.1
  467.3 74.9 %all-to-all-start.5 = ((bf16[16,17,4096]{2,1,0:T(8,128)(2,1)}), bf16[16,17,4096]{2,1,0:T(8,128)(2,1)}, u32[]{:S(2)}, u32[]{:S(2)}) async-start(bf16[16,17,4096]{2,1,0:T(8,128)(2,1)} %reshape.525), calls=%async_computation.5 | async-start | bytes 6291456 | tf_op jit(solution)/shard_map/all_to_all | solution.py:103
  550.8 11.8 copy-start.12
  565.9 74.8 %all-to-all-start.6 = ((bf16[16,17,4096]{2,1,0:T(8,128)(2,1)}), bf16[16,17,4096]{2,1,0:T(8,128)(2,1)}, u32[]{:S(2)}, u32[]{:S(2)}) async-start(bf16[16,17,4096]{2,1,0:T(8,128)(2,1)} %reshape.527), calls=%async_computation.6 | async-start | bytes 6291456 | tf_op jit(solution)/shard_map/all_to_all | solution.py:120
  685.9 74.8 %all-to-all-start.8 = ((bf16[16,17,4096]{2,1,0:T(8,128)(2,1)}), bf16[16,17,4096]{2,1,0:T(8,128)(2,1)}, u32[]{:S(2)}, u32[]{:S(2)}) async-start(bf16[16,17,4096]{2,1,0:T(8,128)(2,1)} %reshape.534), calls=%async_computation.8 | async-start | bytes 6291456 | tf_op jit(solution)/shard_map/all_to_all | solution.py:103
  690.3 6.2 collective-permute-start.2
  760.7 74.9 %all-to-all-start.7 = ((bf16[16,17,4096]{2,1,0:T(8,128)(2,1)}), bf16[16,17,4096]{2,1,0:T(8,128)(2,1)}, u32[]{:S(2)}, u32[]{:S(2)}) async-start(bf16[16,17,4096]{2,1,0:T(8,128)(2,1)} %reshape.531), calls=%async_computation.7 | async-start | bytes 6291456 | tf_op jit(solution)/shard_map/all_to_all | solution.py:104
  853.9 74.9 %all-to-all-start.9 = ((bf16[16,17,4096]{2,1,0:T(8,128)(2,1)}), bf16[16,17,4096]{2,1,0:T(8,128)(2,1)}, u32[]{:S(2)}, u32[]{:S(2)}) async-start(bf16[16,17,4096]{2,1,0:T(8,128)(2,1)} %reshape.536), calls=%async_computation.9 | async-start | bytes 6291456 | tf_op jit(solution)/shard_map/all_to_all | solution.py:120
  928.8 75.0 %all-to-all-start.11 = ((bf16[16,17,4096]{2,1,0:T(8,128)(2,1)}), bf16[16,17,4096]{2,1,0:T(8,128)(2,1)}, u32[]{:S(2)}, u32[]{:S(2)}) async-start(bf16[16,17,4096]{2,1,0:T(8,128)(2,1)} %reshape.543), calls=%async_computation.11 | async-start | bytes 6291456 | tf_op jit(solution)/shard_map/all_to_all | solution.py:103
  967.0 15.0 %collective-permute-start.3 = (bf16[112,4096]{1,0:T(8,128)(2,1)S(1)}, bf16[112,4096]{1,0:T(8,128)(2,1)}, u32[]{:S(2)}, u32[]{:S(2)}) collective-permute-start(bf16[112,4096]{1,0:T(8,128)(2,1)S(1)} %get-tuple-element.8), channel_id=1, source_target_pairs={{16,0},{17,1},{18,2},{19,3},{20,4},{21,5},{22,6},{23,7},{24,8},{25... | collective-permute-start | bytes 2752520 | tf_op jit(solution)/shard_map/ppermute | solution.py:14
  1003.9 77.6 %all-to-all-start.10 = ((bf16[16,17,4096]{2,1,0:T(8,128)(2,1)}), bf16[16,17,4096]{2,1,0:T(8,128)(2,1)}, u32[]{:S(2)}, u32[]{:S(2)}) async-start(bf16[16,17,4096]{2,1,0:T(8,128)(2,1)} %reshape.540), calls=%async_computation.10 | async-start | bytes 6291456 | tf_op jit(solution)/shard_map/all_to_all | solution.py:104
  1099.6 6.2 copy-start.13
  1099.6 76.2 %all-to-all-start.12 = ((bf16[16,17,4096]{2,1,0:T(8,128)(2,1)}), bf16[16,17,4096]{2,1,0:T(8,128)(2,1)}, u32[]{:S(2)}, u32[]{:S(2)}) async-start(bf16[16,17,4096]{2,1,0:T(8,128)(2,1)} %reshape.545), calls=%async_computation.12 | async-start | bytes 6291456 | tf_op jit(solution)/shard_map/all_to_all | solution.py:120
  1105.8 8.2 copy-start.11
  1105.9 8.2 copy-start.14
  1120.5 3.1 copy-start.10
  (7 other events, 13.8 us)
where the time goes:
time: 1220 us; the launch traced here: 1200 us
  waiting for transfers between devices  542 us (44%)
  local copies, waits for them, and re-layouts  239 us (20%)
  blocking collectives  151 us (12%)
  matrix products  102 us (8%)
  other arithmetic  91.2 us (7%)
  starting transfers between devices  78.1 us (6%)
    all_to_all x3, waiting for transfers between devices, backward_step(): lax.all_to_all(back_pick.reshape(expert_count, capacity, feature_count),...  160 us
    all_to_all x2, blocking collectives, forward_step(): lax.all_to_all(outgoing, 'expert', split_axis=0, concat_axis=0, tiled=True)  151 us
    all_to_all x3, waiting for transfers between devices, backward_step(): lax.all_to_all(grad_out, 'expert', split_axis=0, concat_axis=0, tiled=True)  147 us
    all_to_all x2, waiting for transfers between devices, forward_step(): lax.all_to_all(answer.reshape(received.shape), 'expert', split_axis=0, co...  118 us
    all_to_all x3, waiting for transfers between devices, backward_step(): lax.all_to_all(outgoing, 'expert', split_axis=0, concat_axis=0, tiled=True)  110 us
    dot_general x3, matrix products, backward_step(): lax.dot_general(back_hidden, up_matrix, (((1,), (1,)), ((), ())), preferr...  35 us
    mul x9, local copies, waits for them, and re-layouts, backward_step(): weights[:, :, None] * incoming.astype(jnp.float32)[:, None, :]  28.6 us
    scatter x5, local copies, waits for them, and re-layouts, place_rows(): jnp.zeros((slot_total, values.shape[1]), values.dtype).at[targets]  28.5 us
  transfers between devices with their start and end apart: 15, of which 14 were waited for; matrix products, arithmetic and copies ran while one was open for 17% of the time, Pallas kernels for 0%

commit v1 on v0

v1 whole, which is shorter than its diff:
```python
import functools

import jax
import jax.numpy as jnp
from jax import lax
from jax.experimental import pallas as pl
from jax.experimental.pallas import tpu as pltpu
from jax.sharding import PartitionSpec as P

EPSILON = 1e-06
ROOT_HALF = 0.7071067811865476
INV_ROOT_TAU = 0.3989422804014327
BF16 = jnp.bfloat16
F32 = jnp.float32
FEATURE_BLOCKS = 8
SLOT_TILE = 16
VMEM_BYTES = 56 * 1024 * 1024


class Sizes:
    def __init__(self, experts, rows, features, hidden):
        self.experts, self.rows, self.features, self.hidden = experts, rows, features, hidden
        self.capacity = 5 * rows // (2 * experts)
        self.lanes = features // FEATURE_BLOCKS
        self.tiled = self.capacity // SLOT_TILE * SLOT_TILE
        self.rest = self.capacity - self.tiled
        self.tiled_rows = experts * self.tiled
        self.rest_rows = experts * self.rest
        self.slots = experts * self.capacity
        self.message = (experts, FEATURE_BLOCKS * self.capacity, self.lanes)


def iota(shape, axis):
    return lax.broadcasted_iota(jnp.int32, shape, axis)


def dot(left, right):
    return jnp.dot(left, right, preferred_element_type=F32)


def dot_last(left, right):
    return lax.dot_general(left, right, (((1,), (1,)), ((), ())), preferred_element_type=F32)


def gelu_value(values):
    return 0.5 * values * (1.0 + lax.erf(values * ROOT_HALF))


def gelu_slope(values):
    return (
        0.5 * (1.0 + lax.erf(values * ROOT_HALF))
        + values * jnp.exp(-0.5 * values * values) * INV_ROOT_TAU
    )


def halves(values):
    high = values.astype(BF16)
    return high, (values - high.astype(F32)).astype(BF16)


def slot_parts(sizes):
    parts = []
    if sizes.tiled:
        parts.append((sizes.tiled, 0))
    if sizes.rest:
        parts.append((sizes.rest, sizes.tiled))
    return parts


def expansion(sizes, width):
    count = sizes.experts * width
    shape = (count, sizes.experts)
    first = iota(shape, 1) * width
    row = iota(shape, 0)
    return ((row >= first) & (row < first + width)).astype(BF16)


def expansion_across(sizes, width):
    count = sizes.experts * width
    shape = (sizes.experts, count)
    first = iota(shape, 0) * width
    column = iota(shape, 1)
    return ((column >= first) & (column < first + width)).astype(BF16)


def slots_by_token(sizes, table_across, gated):
    rows = sizes.rows
    names = iota((sizes.experts, rows), 0).astype(F32)
    first = table_across[0:1, :] == names
    second = table_across[1:2, :] == names
    chosen = jnp.where(first | second, 1.0, 0.0)
    earlier = (iota((rows, rows), 0) < iota((rows, rows), 1)).astype(BF16)
    rank = jnp.where(chosen > 0.0, dot(chosen.astype(BF16), earlier), -1.0).astype(BF16)
    if gated:
        gate = jnp.where(first, table_across[2:3, :], 0.0) + jnp.where(
            second, table_across[3:4, :], 0.0
        )
        high, low = halves(gate)
    ones, highs, lows = [], [], []
    for width, start in slot_parts(sizes):
        spread = expansion(sizes, width)
        ranks = dot(spread, rank)
        place = iota(ranks.shape, 0) % width + start
        here = ranks == place.astype(F32)
        if gated:
            highs.append(jnp.where(here, dot(spread, high), 0.0).astype(BF16))
            lows.append(jnp.where(here, dot(spread, low), 0.0).astype(BF16))
        else:
            ones.append(jnp.where(here, 1.0, 0.0).astype(BF16))
    if gated:
        return jnp.concatenate(highs, axis=0), jnp.concatenate(lows, axis=0)
    return jnp.concatenate(ones, axis=0)


def tokens_by_slot(sizes, table, gated):
    rows = sizes.rows
    names = iota((rows, sizes.experts), 1).astype(F32)
    first = table[:, 0:1] == names
    second = table[:, 1:2] == names
    chosen = jnp.where(first | second, 1.0, 0.0)
    earlier = (iota((rows, rows), 1) < iota((rows, rows), 0)).astype(BF16)
    rank = jnp.where(chosen > 0.0, dot(earlier, chosen.astype(BF16)), -1.0).astype(BF16)
    if gated:
        gate = jnp.where(first, table[:, 2:3], 0.0) + jnp.where(second, table[:, 3:4], 0.0)
        high, low = halves(gate)
    ones, highs, lows = [], [], []
    for width, start in slot_parts(sizes):
        spread = expansion_across(sizes, width)
        ranks = dot(rank, spread)
        place = iota(ranks.shape, 1) % width + start
        here = ranks == place.astype(F32)
        if gated:
            highs.append(jnp.where(here, dot(high, spread), 0.0).astype(BF16))
            lows.append(jnp.where(here, dot(low, spread), 0.0).astype(BF16))
        else:
            ones.append(jnp.where(here, 1.0, 0.0).astype(BF16))
    if gated:
        return jnp.concatenate(highs, axis=1), jnp.concatenate(lows, axis=1)
    return jnp.concatenate(ones, axis=1)


def write_tiled(sizes, message, block, values):
    if sizes.tiled:
        message[:, block * sizes.tiled : (block + 1) * sizes.tiled, :] = (
            values[: sizes.tiled_rows].astype(BF16).reshape(sizes.experts, sizes.tiled, sizes.lanes)
        )
    return values[sizes.tiled_rows :].astype(BF16)


def rest_places(sizes, block):
    shape = (sizes.rest_rows * FEATURE_BLOCKS, sizes.rest_rows)
    return (iota(shape, 0) == iota(shape, 1) * FEATURE_BLOCKS + block).astype(BF16)


def rest_places_across(sizes, block):
    shape = (sizes.rest_rows, sizes.rest_rows * FEATURE_BLOCKS)
    return (iota(shape, 1) == iota(shape, 0) * FEATURE_BLOCKS + block).astype(BF16)


def write_message(sizes, message, block_values):
    rest = None
    for block in range(FEATURE_BLOCKS):
        other = write_tiled(sizes, message, block, block_values(block))
        if sizes.rest:
            part = dot(rest_places(sizes, block), other)
            rest = part if rest is None else rest + part
    if sizes.rest:
        first = FEATURE_BLOCKS * sizes.tiled
        message[:, first:, :] = rest.reshape(
            sizes.experts, FEATURE_BLOCKS * sizes.rest, sizes.lanes
        ).astype(BF16)


def read_rest(sizes, message):
    if not sizes.rest:
        return None
    first = FEATURE_BLOCKS * sizes.tiled
    return (
        message[:, first:, :]
        .astype(F32)
        .reshape(sizes.rest_rows * FEATURE_BLOCKS, sizes.lanes)
        .astype(BF16)
    )


def read_block(sizes, message, rest, block):
    parts = []
    if sizes.tiled:
        parts.append(
            message[:, block * sizes.tiled : (block + 1) * sizes.tiled, :].reshape(
                sizes.tiled_rows, sizes.lanes
            )
        )
    if sizes.rest:
        parts.append(dot(rest_places_across(sizes, block), rest).astype(BF16))
    return jnp.concatenate(parts, axis=0)


def span(sizes, block):
    return slice(block * sizes.lanes, (block + 1) * sizes.lanes)


def inverse_rms(sizes, read):
    total = jnp.zeros((sizes.rows, 1), F32)
    for block in range(FEATURE_BLOCKS):
        wide = read(block).astype(F32)
        total = total + jnp.sum(wide * wide, axis=1, keepdims=True)
    return lax.rsqrt(total / sizes.features + EPSILON)


def send_normed(sizes, carried, across, message):
    scale = inverse_rms(sizes, lambda block: carried[:, span(sizes, block)])
    select = slots_by_token(sizes, across, False)

    def values(block):
        normed = (carried[:, span(sizes, block)].astype(F32) * scale).astype(BF16)
        return dot(select, normed)

    write_message(sizes, message, values)


def send_weighted(sizes, incoming, across, message):
    high, low = slots_by_token(sizes, across, True)

    def values(block):
        rows = incoming[:, span(sizes, block)]
        return dot(high, rows) + dot(low, rows)

    write_message(sizes, message, values)


def first_kernel(sizes, which, carried, across, message):
    send_normed(sizes, carried.at[0], across, message)


def cotangent_kernel(sizes, which, incoming, across, message):
    send_weighted(sizes, incoming.at[0], across, message)


def middle_kernel(sizes, which, before, answer, table, across, carried, message):
    high, low = tokens_by_slot(sizes, table, True)
    rest = read_rest(sizes, answer)
    for block in range(FEATURE_BLOCKS):
        rows = read_block(sizes, answer, rest, block)
        mixed = before[0, :, span(sizes, block)].astype(F32) + (dot(high, rows) + dot(low, rows))
        carried[:, span(sizes, block)] = mixed.astype(BF16)
    send_normed(sizes, carried, across, message)


def norm_back(sizes, carried, incoming, answer, table, upstream, result):
    select = tokens_by_slot(sizes, table, False)
    rest = read_rest(sizes, answer)
    inner = jnp.zeros((sizes.rows, 1), F32)
    squares = jnp.zeros((sizes.rows, 1), F32)
    for block in range(FEATURE_BLOCKS):
        here = span(sizes, block)
        back = dot(select, read_block(sizes, answer, rest, block))
        wide = carried[:, here].astype(F32)
        upstream[:, here] = back
        inner = inner + jnp.sum(wide * back, axis=1, keepdims=True)
        squares = squares + jnp.sum(wide * wide, axis=1, keepdims=True)
    scale = lax.rsqrt(squares / sizes.features + EPSILON)
    pull = scale * scale * scale * (inner / sizes.features)
    for block in range(FEATURE_BLOCKS):
        here = span(sizes, block)
        wide = carried[:, here].astype(F32)
        result[:, here] = (
            incoming[:, here].astype(F32) + (scale * upstream[:, here] - wide * pull)
        ).astype(BF16)


def turn_kernel(
    sizes, which, carried, incoming, answer, table, across, result, message, upstream
):
    norm_back(sizes, carried, incoming.at[0], answer, table, upstream, result)
    send_weighted(sizes, result, across, message)


def last_kernel(sizes, which, carried, incoming, answer, table, result, upstream):
    norm_back(sizes, carried.at[0], incoming, answer, table, upstream, result)


def fetch(which, wanted, own, other, place, semaphores, pieces):
    def begin(source):
        for number, piece in enumerate(pieces):
            pltpu.make_async_copy(
                source.at[piece], place.at[piece], semaphores.at[number]
            ).start()

    @pl.when(which[0] == wanted)
    def _():
        begin(own)

    @pl.when(which[0] != wanted)
    def _():
        begin(other)

    def wait(number):
        piece = pieces[number]
        pltpu.make_async_copy(own.at[piece], place.at[piece], semaphores.at[number]).wait()

    return wait


def up_pieces(sizes):
    return [
        (pl.ds(block * sizes.lanes, sizes.lanes), slice(None)) for block in range(FEATURE_BLOCKS)
    ]


def down_pieces(sizes):
    return [
        (slice(None), pl.ds(block * sizes.lanes, sizes.lanes)) for block in range(FEATURE_BLOCKS)
    ]


def forward_kernel(
    sizes, section, which, received, up, up_other, down, down_other,
    hidden_out, activated_out, message, up_here, down_here, up_done, down_done,
):
    up_wait = fetch(which, section, up, up_other, up_here, up_done, up_pieces(sizes))
    down_wait = fetch(which, section, down, down_other, down_here, down_done, down_pieces(sizes))
    rest = read_rest(sizes, received)
    hidden = jnp.zeros((sizes.slots, sizes.hidden), F32)
    for block in range(FEATURE_BLOCKS):
        rows = read_block(sizes, received, rest, block)
        up_wait(block)
        hidden = hidden + dot(rows, up_here[span(sizes, block), :])
    hidden_out[...] = hidden
    activated = gelu_value(hidden).astype(BF16)
    activated_out[...] = activated

    def values(block):
        down_wait(block)
        return dot(activated, down_here[:, span(sizes, block)])

    write_message(sizes, message, values)


def hidden_back_kernel(
    sizes, section, which, received, down, down_other, back_out, down_here, down_done
):
    down_wait = fetch(which, section, down, down_other, down_here, down_done, down_pieces(sizes))
    rest = read_rest(sizes, received)
    back = jnp.zeros((sizes.slots, sizes.hidden), F32)
    for block in range(FEATURE_BLOCKS):
        rows = read_block(sizes, received, rest, block)
        down_wait(block)
        back = back + dot_last(rows, down_here[:, span(sizes, block)])
    back_out[...] = back


def back_message(sizes, back_hidden, up_here, message):
    write_message(
        sizes, message, lambda block: dot_last(back_hidden, up_here[span(sizes, block), :])
    )


def turn_expert_kernel(
    sizes, section, which, received, back, up, up_other,
    activated_out, message, up_here, up_done,
):
    up_wait = fetch(which, section, up, up_other, up_here, up_done, up_pieces(sizes))
    rest = read_rest(sizes, received)
    hidden = jnp.zeros((sizes.slots, sizes.hidden), F32)
    for block in range(FEATURE_BLOCKS):
        rows = read_block(sizes, received, rest, block)
        up_wait(block)
        hidden = hidden + dot(rows, up_here[span(sizes, block), :])
    activated_out[...] = gelu_value(hidden).astype(BF16)
    back_hidden = (back[...] * gelu_slope(hidden)).astype(BF16)
    back_message(sizes, back_hidden, up_here, message)


def backward_kernel(
    sizes, section, which, received, hidden, up, up_other, down, down_other,
    message, up_here, down_here, up_done, down_done,
):
    down_wait = fetch(which, section, down, down_other, down_here, down_done, down_pieces(sizes))
    up_wait = fetch(which, section, up, up_other, up_here, up_done, up_pieces(sizes))
    slope = gelu_slope(hidden[...])
    rest = read_rest(sizes, received)
    back = jnp.zeros((sizes.slots, sizes.hidden), F32)
    for block in range(FEATURE_BLOCKS):
        rows = read_block(sizes, received, rest, block)
        down_wait(block)
        back = back + dot_last(rows, down_here[:, span(sizes, block)])
    back_hidden = (back * slope).astype(BF16)
    for block in range(FEATURE_BLOCKS):
        up_wait(block)
    back_message(sizes, back_hidden, up_here, message)


def down_grad_kernel(
    sizes, which, activated_0, grad_0, activated_1, grad_1, activated_far, grad_far,
    result, activated_here, grad_here, done,
):
    everything = (slice(None), slice(None))
    whole = (slice(None), slice(None), slice(None))
    activated_wait = fetch(
        which, 0, activated_0, activated_1, activated_here, done.at[pl.ds(0, 1)], [everything]
    )
    grad_wait = fetch(which, 0, grad_0, grad_1, grad_here, done.at[pl.ds(1, 1)], [whole])
    activated_wait(0)
    grad_wait(0)
    near, far = activated_here[...], activated_far[...]
    rest_near, rest_far = read_rest(sizes, grad_here), read_rest(sizes, grad_far)
    over_rows = (((0,), (0,)), ((), ()))
    for block in range(FEATURE_BLOCKS):
        rows_near = read_block(sizes, grad_here, rest_near, block)
        rows_far = read_block(sizes, grad_far, rest_far, block)
        total = lax.dot_general(near, rows_near, over_rows, preferred_element_type=F32)
        total = total + lax.dot_general(far, rows_far, over_rows, preferred_element_type=F32)
        result[:, span(sizes, block)] = total.astype(BF16)


VMEM = pl.BlockSpec(memory_space=pltpu.VMEM)
HBM = pl.BlockSpec(memory_space=pl.ANY)


def call(kernel, name, which, operands, specs, outs, scratch=()):
    def chosen(shape):
        return pl.BlockSpec((1,) + shape[1:], lambda step, pick: (pick[0], 0, 0))

    in_specs = [
        chosen(operand.shape) if spec == "clip" else spec for operand, spec in zip(operands, specs)
    ]
    return pl.pallas_call(
        kernel,
        name=name,
        grid_spec=pltpu.PrefetchScalarGridSpec(
            num_scalar_prefetch=1,
            grid=(1,),
            in_specs=in_specs,
            out_specs=[VMEM] * len(outs),
            scratch_shapes=list(scratch),
        ),
        out_shape=[jax.ShapeDtypeStruct(shape, kind) for shape, kind in outs],
        compiler_params=pltpu.CompilerParams(vmem_limit_bytes=VMEM_BYTES),
    )(which, *operands)


def exchange(message):
    return lax.all_to_all(message, "expert", split_axis=0, concat_axis=0, tiled=True)


def shards(tokens, cotangent, expert_ids, gate_prob, up_weight, down_weight):
    core = lax.axis_index("pipe")
    rows, features = tokens.shape[1], tokens.shape[2]
    hidden = up_weight.shape[3]
    sizes = Sizes(lax.axis_size("expert"), rows, features, hidden)
    swap = [(0, 1), (1, 0)]
    which = jnp.reshape(core, (1,)).astype(jnp.int32)

    tables = jnp.concatenate([expert_ids[0].astype(F32), gate_prob[0]], axis=-1)
    mine = lax.dynamic_index_in_dim(tables, core, 0, keepdims=False)
    theirs = lax.dynamic_index_in_dim(tables, 1 - core, 0, keepdims=False)
    theirs = lax.ppermute(theirs, "pipe", swap)
    table_0 = jnp.where(core == 0, mine, theirs)
    table_1 = jnp.where(core == 0, theirs, mine)
    across_0, across_1 = table_0.T, table_1.T

    up, down = up_weight[0, 0], down_weight[0, 0]
    up_other = lax.ppermute(up, "pipe", swap)
    down_other = lax.ppermute(down, "pipe", swap)

    up_scratch = pltpu.VMEM((features, hidden), BF16)
    down_scratch = pltpu.VMEM((hidden, features), BF16)
    done_scratch = pltpu.SemaphoreType.DMA((FEATURE_BLOCKS,))
    upstream_scratch = pltpu.VMEM((rows, features), F32)
    message = (sizes.message, BF16)
    home_rows = ((rows, features), BF16)
    activated = ((sizes.slots, hidden), BF16)
    wide_hidden = ((sizes.slots, hidden), F32)

    def kernel(body, *more):
        return functools.partial(body, sizes, *more)

    (out_0,) = call(
        kernel(first_kernel), "send_tokens", which, [tokens, across_0], ["clip", VMEM], [message]
    )
    in_0 = exchange(out_0)
    (grad_out_1,) = call(
        kernel(cotangent_kernel), "send_cotangent", which, [cotangent, across_1],
        ["clip", VMEM], [message],
    )
    grad_in_1 = exchange(grad_out_1)
    hidden_0, activated_0, answer_0 = call(
        kernel(forward_kernel, 0), "expert_forward", which,
        [in_0, up, up_other, down, down_other], [VMEM, HBM, HBM, HBM, HBM],
        [wide_hidden, activated, message],
        [up_scratch, down_scratch, done_scratch, done_scratch],
    )
    returned_0 = exchange(answer_0)
    carried_1, out_1 = call(
        kernel(middle_kernel), "combine_send", which,
        [tokens, returned_0, table_0, across_1], ["clip", VMEM, VMEM, VMEM], [home_rows, message],
    )
    in_1 = exchange(out_1)
    (back_1,) = call(
        kernel(hidden_back_kernel, 1), "hidden_back", which,
        [grad_in_1, down, down_other], [VMEM, HBM, HBM], [wide_hidden],
        [down_scratch, done_scratch],
    )
    activated_1, picks_1 = call(
        kernel(turn_expert_kernel, 1), "expert_turn", which,
        [in_1, back_1, up, up_other], [VMEM, VMEM, HBM, HBM], [activated, message],
        [up_scratch, done_scratch],
    )
    back_home_1 = exchange(picks_1)
    grad_1, grad_out_0 = call(
        kernel(turn_kernel), "norm_back_send", which,
        [carried_1, cotangent, back_home_1, table_1, across_0],
        [VMEM, "clip", VMEM, VMEM, VMEM], [home_rows, message], [upstream_scratch],
    )
    grad_in_0 = exchange(grad_out_0)
    (picks_0,) = call(
        kernel(backward_kernel, 0), "expert_backward", which,
        [grad_in_0, hidden_0, up, up_other, down, down_other],
        [VMEM, VMEM, HBM, HBM, HBM, HBM], [message],
        [up_scratch, down_scratch, done_scratch, done_scratch],
    )
    back_home_0 = exchange(picks_0)

    to_first, to_second = [(1, 0)], [(0, 1)]
    activated_far = jnp.where(
        core == 0,
        lax.ppermute(activated_0, "pipe", to_first),
        lax.ppermute(activated_1, "pipe", to_second),
    )
    grad_far = jnp.where(
        core == 0,
        lax.ppermute(grad_in_0, "pipe", to_first),
        lax.ppermute(grad_in_1, "pipe", to_second),
    )
    (down_grad,) = call(
        kernel(down_grad_kernel), "down_grad", which,
        [activated_0, grad_in_0, activated_1, grad_in_1, activated_far, grad_far],
        [HBM, HBM, HBM, HBM, VMEM, VMEM], [((hidden, features), BF16)],
        [
            pltpu.VMEM((sizes.slots, hidden), BF16),
            pltpu.VMEM(sizes.message, BF16),
            pltpu.SemaphoreType.DMA((2,)),
        ],
    )

    (grad_0,) = call(
        kernel(last_kernel), "norm_back_last", which,
        [tokens, grad_1, back_home_0, table_0], ["clip", VMEM, VMEM, VMEM], [home_rows],
        [upstream_scratch],
    )
    far_1 = lax.ppermute(grad_1, "pipe", to_second)
    far_0 = lax.ppermute(grad_0, "pipe", to_first)
    input_grad = jnp.where(
        core == 0, jnp.stack([grad_0, far_0]), jnp.stack([far_1, grad_1])
    )
    return input_grad[None], down_grad[None, None]


def solution(mesh):
    placed = (
        P(None, "expert", None),
        P(None, "expert", None),
        P("pipe", None, "expert", None),
        P("pipe", None, "expert", None),
        P("pipe", "expert", None, None),
        P("pipe", "expert", None, None),
    )
    return jax.shard_map(
        shards,
        mesh=mesh,
        in_specs=placed,
        out_specs=(P("pipe", None, "expert", None), P("pipe", "expert", None, None)),
        check_vma=False,
    )
```

time: 1220 us -> 483 us (0.40); the launches traced: 1200 us -> 482 us
  waiting for transfers between devices: 542 us -> 178 us
  local copies, waits for them, and re-layouts: 239 us -> 4.26 us
  matrix products: 102 us -> 0 us
  Pallas kernels: 0 us -> 86.1 us
  other arithmetic: 91.2 us -> 9.2 us
  starting transfers between devices: 78.1 us -> 37.7 us
  blocking collectives: 151 us -> 166 us
    all_to_all x11 -> x4, waiting for transfers between devices: 536 us -> 170 us  [exchange(): lax.all_to_all(message, 'expert', split_axis=0, concat_axis=0, tiled=True)]
    dot_general x11 -> x0, matrix products: 102 us -> none  [the longest x3 35 us: backward_step(): lax.dot_general(back_hidden, up_matrix, (((1,), (1,)), ((), ())), preferr...]
    reshape x31 -> x0, local copies, waits for them, and re-layouts: 101 us -> none  [the longest x3 14.9 us: backward_step(): jnp.repeat(normed, 2, axis=0)]
    pallas_call x0 -> x10, Pallas kernels: none -> 86.1 us  [call(): pl.pallas_call(kernel, name=name, grid_spec=pltpu.PrefetchScalarGridSpec(...]
    reduce_sum x16 -> x0, other arithmetic: 49.1 us -> none  [the longest x3 23.7 us: backward_step(): back_normed = jnp.sum(picked.astype(jnp.float32), axis=1)]
    all_to_all x11 -> x4, starting transfers between devices: 55.1 us -> 19.5 us  [exchange(): lax.all_to_all(message, 'expert', split_axis=0, concat_axis=0, tiled=True)]
    mul x21 -> x0, local copies, waits for them, and re-layouts: 30 us -> none  [the longest x9 28.6 us: backward_step(): weights[:, :, None] * incoming.astype(jnp.float32)[:, None, :]]
    gather x5 -> x0, local copies, waits for them, and re-layouts: 29.4 us -> none  [the longest x3 19.8 us: backward_step(): back_home.reshape(slot_total, feature_count)[targets]]
  transfers between devices with their start and end apart: 15 -> 13, of which waited for: 14 -> 5; matrix products, arithmetic and copies ran while one was open for 17% -> 2% of each run, Pallas kernels for 0% -> 9%
where the time goes in v1:
time: 483 us; the launch traced here: 482 us
  waiting for transfers between devices  178 us (37%)
  blocking collectives  166 us (34%)
  Pallas kernels  86.1 us (18%)
  starting transfers between devices  37.7 us (8%)
  other arithmetic  9.2 us (2%)
    all_to_all x4, waiting for transfers between devices, exchange(): lax.all_to_all(message, 'expert', split_axis=0, concat_axis=0, tiled=True)  170 us
    all_to_all x3, blocking collectives, exchange(): lax.all_to_all(message, 'expert', split_axis=0, concat_axis=0, tiled=True)  166 us
    pallas_call x10, Pallas kernels, call(): pl.pallas_call(kernel, name=name, grid_spec=pltpu.PrefetchScalarGridSpec(...  86.1 us
    all_to_all x4, starting transfers between devices, exchange(): lax.all_to_all(message, 'expert', split_axis=0, concat_axis=0, tiled=True)  19.5 us
  transfers between devices with their start and end apart: 13, of which 5 were waited for; matrix products, arithmetic and copies ran while one was open for 2% of the time, Pallas kernels for 9%

profile of v1, /device:TPU:13, one launch (start us, length us, event | category | flops | bytes accessed | tf_op | source)
XLA Modules:
  0.0 482.0 jit_solution(10975609579560214332)
XLA Ops:
  3.5 7.8 %collective-permute-done = f32[112,4]{1,0:T(8,128)S(1)} collective-permute-done((f32[112,4]{1,0:T(8,128)S(1)}, f32[112,4]{1,0:T(8,128)S(1)}, u32[]{:S(2)}, u32[]{:S(2)}) %collective-permute-start) | collective-permute-done | bytes 1824 | tf_op jit(solution)/shard_map/ppermute | solution.py:458
  12.0 4.7 send_tokens.1
  16.7 57.0 %all_to_all.35.received = bf16[16,136,512]{2,1,0:T(8,128)(2,1)} all-to-all(bf16[16,136,512]{2,1,0:T(8,128)(2,1)} %send_tokens.1), channel_id=1, replica_groups=mesh['pipe'=2,'expert'=16] {'expert'}, dimensions={0} | all-to-all | bytes 4456448 | tf_op jit(solution)/shard_map/all_to_all | solution.py:444
  73.7 12.0 %expert_forward.1 = (f32[272,768]{1,0:T(8,128)}, bf16[272,768]{1,0:T(8,128)(2,1)}, bf16[16,136,512]{2,1,0:T(8,128)(2,1)}) custom-call(s32[1]{0:T(128)} %bitcast.which, bf16[16,136,512]{2,1,0:T(8,128)(2,1)} %all_to_all.35.received, bf16[4096,768]{1,0:T(8,128)(2,1)} %bitcast.18, bf16[4096,768]{1,0:T(8,128)(2,1)} %collective-permute-done.1.up_other, ...), custom_call_target="tpu_custom_call" | custom-call | tf_op jit(solution)/shard_map/expert_forward/pallas_call | solution.py:428
  85.7 4.9 %all-to-all-start.1 = ((bf16[16,136,512]{2,1,0:T(8,128)(2,1)}), bf16[16,136,512]{2,1,0:T(8,128)(2,1)S(1)}, u32[]{:S(2)}, u32[]{:S(2)}) async-start(bf16[16,136,512]{2,1,0:T(8,128)(2,1)} %get-tuple-element.11), calls=%async_computation.1 | async-start | bytes 4456448 | tf_op jit(solution)/shard_map/all_to_all | solution.py:444
  91.3 5.3 %send_cotangent.1 = bf16[16,136,512]{2,1,0:T(8,128)(2,1)} custom-call(s32[1]{0:T(128)} %bitcast.which, bf16[2,112,4096]{2,1,0:T(8,128)(2,1)} %incoming.3, f32[4,112]{1,0:T(4,128)} %copy.11.across), custom_call_target="tpu_custom_call" | custom-call | tf_op jit(solution)/shard_map/send_cotangent/pallas_call | solution.py:428
  96.6 44.9 %all-to-all-done.1.answer = bf16[16,136,512]{2,1,0:T(8,128)(2,1)S(1)} async-done(((bf16[16,136,512]{2,1,0:T(8,128)(2,1)}), bf16[16,136,512]{2,1,0:T(8,128)(2,1)S(1)}, u32[]{:S(2)}, u32[]{:S(2)}) %all-to-all-start.1) | async-done | bytes 2228256 | tf_op jit(solution)/shard_map/all_to_all | solution.py:444
  142.8 4.1 all-to-all-start.3
  147.0 7.2 %combine_send.1 = (bf16[112,4096]{1,0:T(8,128)(2,1)}, bf16[16,136,512]{2,1,0:T(8,128)(2,1)}) custom-call(s32[1]{0:T(128)} %bitcast.which, bf16[2,112,4096]{2,1,0:T(8,128)(2,1)} %carried.3, bf16[16,136,512]{2,1,0:T(8,128)(2,1)} %copy-done.2, f32[112,4]{1,0:T(8,128)} %copy-done.6, f32[4,112]{1,0:T(4,128)} %copy.11.across), custom_call_target="tpu_custom_call" | custom-call | tf_op jit(solution)/shard_map/combine_send/pallas_call | solution.py:428
  154.2 43.7 %all-to-all-done.3.received.grad_1 = bf16[16,136,512]{2,1,0:T(8,128)(2,1)S(1)} async-done(((bf16[16,136,512]{2,1,0:T(8,128)(2,1)}), bf16[16,136,512]{2,1,0:T(8,128)(2,1)S(1)}, u32[]{:S(2)}, u32[]{:S(2)}) %all-to-all-start.3) | async-done | bytes 2228256 | tf_op jit(solution)/shard_map/all_to_all | solution.py:444
  199.2 4.5 all-to-all-start.2
  203.8 7.2 %hidden_back.1.back = f32[272,768]{1,0:T(8,128)} custom-call(s32[1]{0:T(128)} %bitcast.which, bf16[16,136,512]{2,1,0:T(8,128)(2,1)} %copy-done.1, bf16[768,4096]{1,0:T(8,128)(2,1)} %bitcast.23, bf16[768,4096]{1,0:T(8,128)(2,1)} %collective-permute-done.2.down_other), custom_call_target="tpu_custom_call" | custom-call | tf_op jit(solution)/shard_map/hidden_back/pallas_call | solution.py:428
  211.0 43.4 %all-to-all-done.2.received = bf16[16,136,512]{2,1,0:T(8,128)(2,1)} async-done(((bf16[16,136,512]{2,1,0:T(8,128)(2,1)}), bf16[16,136,512]{2,1,0:T(8,128)(2,1)}, u32[]{:S(2)}, u32[]{:S(2)}) %all-to-all-start.2) | async-done | bytes 2228256 | tf_op jit(solution)/shard_map/all_to_all | solution.py:444
  254.4 11.1 %expert_turn.1 = (bf16[272,768]{1,0:T(8,128)(2,1)}, bf16[16,136,512]{2,1,0:T(8,128)(2,1)}) custom-call(s32[1]{0:T(128)} %bitcast.which, bf16[16,136,512]{2,1,0:T(8,128)(2,1)} %all-to-all-done.2.received, f32[272,768]{1,0:T(8,128)} %hidden_back.1.back, bf16[4096,768]{1,0:T(8,128)(2,1)} %bitcast.19, bf16[4096,768]{1,0:T(8,128)(2,1)} %collective-permute-done.1.up_other), custom_call_target="tpu_custom_call" | custom-call | tf_op jit(solution)/shard_map/expert_turn/pallas_call | solution.py:428
  265.5 54.0 %all_to_all.36.answer = bf16[16,136,512]{2,1,0:T(8,128)(2,1)} all-to-all(bf16[16,136,512]{2,1,0:T(8,128)(2,1)} %get-tuple-element.14), channel_id=1, replica_groups=mesh['pipe'=2,'expert'=16] {'expert'}, dimensions={0} | all-to-all | bytes 4456448 | tf_op jit(solution)/shard_map/all_to_all | solution.py:444
  319.6 8.2 %norm_back_send.1 = (bf16[112,4096]{1,0:T(8,128)(2,1)}, bf16[16,136,512]{2,1,0:T(8,128)(2,1)}) custom-call(s32[1]{0:T(128)} %bitcast.which, bf16[112,4096]{1,0:T(8,128)(2,1)} %get-tuple-element.12.carried, bf16[2,112,4096]{2,1,0:T(8,128)(2,1)} %incoming.3, bf16[16,136,512]{2,1,0:T(8,128)(2,1)} %all_to_all.36.answer, f32[112,4]{1,0:T(8,128)} %copy-done.7, ...), custom_call_target="tpu_custom_call" | custom-call | tf_op jit(solution)/shard_map/norm_back_send/pallas_call | solution.py:428
  327.8 55.2 %all_to_all.37.received.grad_0 = bf16[16,136,512]{2,1,0:T(8,128)(2,1)} all-to-all(bf16[16,136,512]{2,1,0:T(8,128)(2,1)} %get-tuple-element.16), channel_id=1, replica_groups=mesh['pipe'=2,'expert'=16] {'expert'}, dimensions={0} | all-to-all | bytes 4456448 | tf_op jit(solution)/shard_map/all_to_all | solution.py:444
  383.0 11.5 %expert_backward.1 = bf16[16,136,512]{2,1,0:T(8,128)(2,1)} custom-call(s32[1]{0:T(128)} %bitcast.which, bf16[16,136,512]{2,1,0:T(8,128)(2,1)} %all_to_all.37.received.grad_0, f32[272,768]{1,0:T(8,128)} %get-tuple-element.17.hidden, bf16[4096,768]{1,0:T(8,128)(2,1)} %bitcast.20, bf16[4096,768]{1,0:T(8,128)(2,1)} %collective-permute-done.1.up_other, ...), custom_call_target="tpu_custom_call" | custom-call | tf_op jit(solution)/shard_map/expert_backward/pallas_call | solution.py:428
  394.6 6.0 %all-to-all-start.6 = ((bf16[16,136,512]{2,1,0:T(8,128)(2,1)}), bf16[16,136,512]{2,1,0:T(8,128)(2,1)}, u32[]{:S(2)}, u32[]{:S(2)}) async-start(bf16[16,136,512]{2,1,0:T(8,128)(2,1)} %expert_backward.1), calls=%async_computation.6 | async-start | bytes 4456448 | tf_op jit(solution)/shard_map/all_to_all | solution.py:444
  401.9 7.3 %collective-permute-start.7 = (bf16[16,136,512]{2,1,0:T(8,128)(2,1)S(1)}, bf16[16,136,512]{2,1,0:T(8,128)(2,1)}, u32[]{:S(2)}, u32[]{:S(2)}) collective-permute-start(bf16[16,136,512]{2,1,0:T(8,128)(2,1)S(1)} %copy-done), channel_id=1, source_target_pairs={{16,0},{17,1},{18,2},{19,3},{20,4},{21,5},{22,6},{23,7},{24,8},{25... | collective-permute-start | bytes 6684680 | tf_op jit(solution)/shard_map/ppermute | solution.py:533
  413.8 37.8 %all-to-all-done.6.answer = bf16[16,136,512]{2,1,0:T(8,128)(2,1)} async-done(((bf16[16,136,512]{2,1,0:T(8,128)(2,1)}), bf16[16,136,512]{2,1,0:T(8,128)(2,1)}, u32[]{:S(2)}, u32[]{:S(2)}) %all-to-all-start.6) | async-done | bytes 2228256 | tf_op jit(solution)/shard_map/all_to_all | solution.py:444
  451.6 5.1 %norm_back_last.1 = bf16[112,4096]{1,0:T(8,128)(2,1)} custom-call(s32[1]{0:T(128)} %bitcast.which, bf16[2,112,4096]{2,1,0:T(8,128)(2,1)} %carried.3, bf16[112,4096]{1,0:T(8,128)(2,1)} %get-tuple-element.15.incoming, bf16[16,136,512]{2,1,0:T(8,128)(2,1)} %all-to-all-done.6.answer, f32[112,4]{1,0:T(8,128)} %copy-done.6), custom_call_target="tpu_custom_call" | custom-call | tf_op jit(solution)/shard_map/norm_back_last/pallas_call | solution.py:428
  456.8 3.7 collective-permute-start.3
  465.6 13.6 %down_grad.1 = bf16[768,4096]{1,0:T(8,128)(2,1)} custom-call(s32[1]{0:T(128)} %bitcast.which, bf16[272,768]{1,0:T(8,128)(2,1)} %get-tuple-element.18.activated_0, bf16[16,136,512]{2,1,0:T(8,128)(2,1)} %all_to_all.37.received.grad_0, bf16[272,768]{1,0:T(8,128)(2,1)} %get-tuple-element.19.activated_1, bf16[16,136,512]{2,1,0:T(8,128)(2,1)} %copy-done.1, ...), custom_call_target="tpu_custom_call" | custom-call | tf_op jit(solution)/shard_map/down_grad/pallas_call | solution.py:428
  (41 shorter events, 20.7 us)
Async XLA Ops:
  0.6 73.1 %collective-permute-start.1 = (bf16[4096,768]{1,0:T(8,128)(2,1)}, bf16[4096,768]{1,0:T(8,128)(2,1)}, u32[]{:S(2)}, u32[]{:S(2)}) collective-permute-start(bf16[4096,768]{1,0:T(8,128)(2,1)} %bitcast.17), channel_id=1, source_target_pairs={{0,16},{16,0},{1,17},{17,1},{2,18},{18,2},{3,19},{19,3},{4,20},{20... | collective-permute-start | bytes 18874376 | tf_op jit(solution)/shard_map/ppermute | solution.py:464
  1.4 72.4 %collective-permute-start.2 = (bf16[768,4096]{1,0:T(8,128)(2,1)}, bf16[768,4096]{1,0:T(8,128)(2,1)}, u32[]{:S(2)}, u32[]{:S(2)}) collective-permute-start(bf16[768,4096]{1,0:T(8,128)(2,1)} %bitcast.21), channel_id=1, source_target_pairs={{0,16},{16,0},{1,17},{17,1},{2,18},{18,2},{3,19},{19,3},{4,20},{20... | collective-permute-start | bytes 18874376 | tf_op jit(solution)/shard_map/ppermute | solution.py:465
  3.0 8.4 %collective-permute-start = (f32[112,4]{1,0:T(8,128)S(1)}, f32[112,4]{1,0:T(8,128)S(1)}, u32[]{:S(2)}, u32[]{:S(2)}) collective-permute-start(f32[112,4]{1,0:T(8,128)S(1)} %bitcast.31), channel_id=1, source_target_pairs={{0,16},{16,0},{1,17},{17,1},{2,18},{18,2},{3,19},{19,3},{4,20},{20... | collective-permute-start | bytes 5384 | tf_op jit(solution)/shard_map/ppermute | solution.py:458
  11.3 62.4 %copy-start.6 = (f32[112,4]{1,0:T(8,128)}, f32[112,4]{1,0:T(8,128)S(1)}, u32[]{:S(2)}) copy-start(f32[112,4]{1,0:T(8,128)S(1)} %get-tuple-element.21.table) | copy-start | bytes 5380
  11.3 79.3 %copy-start.7 = (f32[112,4]{1,0:T(8,128)}, f32[112,4]{1,0:T(8,128)S(1)}, u32[]{:S(2)}) copy-start(f32[112,4]{1,0:T(8,128)S(1)} %get-tuple-element.20.table) | copy-start | bytes 5380
  85.7 55.8 %all-to-all-start.1 = ((bf16[16,136,512]{2,1,0:T(8,128)(2,1)}), bf16[16,136,512]{2,1,0:T(8,128)(2,1)S(1)}, u32[]{:S(2)}, u32[]{:S(2)}) async-start(bf16[16,136,512]{2,1,0:T(8,128)(2,1)} %get-tuple-element.11), calls=%async_computation.1 | async-start | bytes 4456448 | tf_op jit(solution)/shard_map/all_to_all | solution.py:444
  141.5 1.4 copy-start.2
  142.8 55.0 %all-to-all-start.3 = ((bf16[16,136,512]{2,1,0:T(8,128)(2,1)}), bf16[16,136,512]{2,1,0:T(8,128)(2,1)S(1)}, u32[]{:S(2)}, u32[]{:S(2)}) async-start(bf16[16,136,512]{2,1,0:T(8,128)(2,1)} %send_cotangent.1), calls=%async_computation.3 | async-start | bytes 4456448 | tf_op jit(solution)/shard_map/all_to_all | solution.py:444
  197.9 1.3 copy-start.1
  199.2 55.2 %all-to-all-start.2 = ((bf16[16,136,512]{2,1,0:T(8,128)(2,1)}), bf16[16,136,512]{2,1,0:T(8,128)(2,1)}, u32[]{:S(2)}, u32[]{:S(2)}) async-start(bf16[16,136,512]{2,1,0:T(8,128)(2,1)} %get-tuple-element.13), calls=%async_computation.2 | async-start | bytes 4456448 | tf_op jit(solution)/shard_map/all_to_all | solution.py:444
  394.6 7.3 %copy-start = (bf16[16,136,512]{2,1,0:T(8,128)(2,1)S(1)}, bf16[16,136,512]{2,1,0:T(8,128)(2,1)}, u32[]{:S(2)}) copy-start(bf16[16,136,512]{2,1,0:T(8,128)(2,1)} %all_to_all.37.received.grad_0) | copy-start | bytes 6684676
  394.6 17.9 %copy-start.3 = (bf16[112,4096]{1,0:T(8,128)(2,1)S(1)}, bf16[112,4096]{1,0:T(8,128)(2,1)}, u32[]{:S(2)}) copy-start(bf16[112,4096]{1,0:T(8,128)(2,1)} %get-tuple-element.15.incoming) | copy-start | bytes 2752516
  394.6 57.1 %all-to-all-start.6 = ((bf16[16,136,512]{2,1,0:T(8,128)(2,1)}), bf16[16,136,512]{2,1,0:T(8,128)(2,1)}, u32[]{:S(2)}, u32[]{:S(2)}) async-start(bf16[16,136,512]{2,1,0:T(8,128)(2,1)} %expert_backward.1), calls=%async_computation.6 | async-start | bytes 4456448 | tf_op jit(solution)/shard_map/all_to_all | solution.py:444
  400.6 61.7 %collective-permute-start.8 = (bf16[16,136,512]{2,1,0:T(8,128)(2,1)}, bf16[16,136,512]{2,1,0:T(8,128)(2,1)}, u32[]{:S(2)}, u32[]{:S(2)}) collective-permute-start(bf16[16,136,512]{2,1,0:T(8,128)(2,1)} %copy-done.1), channel_id=1, source_target_pairs={{0,16},{1,17},{2,18},{3,19},{4,20},{5,21},{6,22},{7,23},{8,24},{9,... | collective-permute-start | bytes 6684680 | tf_op jit(solution)/shard_map/ppermute | solution.py:534
  401.9 60.4 %collective-permute-start.7 = (bf16[16,136,512]{2,1,0:T(8,128)(2,1)S(1)}, bf16[16,136,512]{2,1,0:T(8,128)(2,1)}, u32[]{:S(2)}, u32[]{:S(2)}) collective-permute-start(bf16[16,136,512]{2,1,0:T(8,128)(2,1)S(1)} %copy-done), channel_id=1, source_target_pairs={{16,0},{17,1},{18,2},{19,3},{20,4},{21,5},{22,6},{23,7},{24,8},{25... | collective-permute-start | bytes 6684680 | tf_op jit(solution)/shard_map/ppermute | solution.py:533
  409.2 47.6 %collective-permute-start.5 = (bf16[272,768]{1,0:T(8,128)(2,1)}, bf16[272,768]{1,0:T(8,128)(2,1)}, u32[]{:S(2)}, u32[]{:S(2)}) collective-permute-start(bf16[272,768]{1,0:T(8,128)(2,1)} %get-tuple-element.18.activated_0), channel_id=1, source_target_pairs={{16,0},{17,1},{18,2},{19,3},{20,4},{21,5},{22,6},{23,7},{24,8},{25... | collective-permute-start | bytes 1253384 | tf_op jit(solution)/shard_map/ppermute | solution.py:528
  411.2 49.3 %collective-permute-start.6 = (bf16[272,768]{1,0:T(8,128)(2,1)}, bf16[272,768]{1,0:T(8,128)(2,1)}, u32[]{:S(2)}, u32[]{:S(2)}) collective-permute-start(bf16[272,768]{1,0:T(8,128)(2,1)} %get-tuple-element.19.activated_1), channel_id=1, source_target_pairs={{0,16},{1,17},{2,18},{3,19},{4,20},{5,21},{6,22},{7,23},{8,24},{9,... | collective-permute-start | bytes 1253384 | tf_op jit(solution)/shard_map/ppermute | solution.py:529
  412.5 66.7 %collective-permute-start.4 = (bf16[112,4096]{1,0:T(8,128)(2,1)S(1)}, bf16[112,4096]{1,0:T(8,128)(2,1)}, u32[]{:S(2)}, u32[]{:S(2)}) collective-permute-start(bf16[112,4096]{1,0:T(8,128)(2,1)S(1)} %copy-done.3), channel_id=1, source_target_pairs={{0,16},{1,17},{2,18},{3,19},{4,20},{5,21},{6,22},{7,23},{8,24},{9,... | collective-permute-start | bytes 2752520 | tf_op jit(solution)/shard_map/ppermute | solution.py:552
  456.8 22.4 %collective-permute-start.3 = (bf16[112,4096]{1,0:T(8,128)(2,1)}, bf16[112,4096]{1,0:T(8,128)(2,1)S(1)}, u32[]{:S(2)}, u32[]{:S(2)}) collective-permute-start(bf16[112,4096]{1,0:T(8,128)(2,1)} %norm_back_last.1), channel_id=1, source_target_pairs={{16,0},{17,1},{18,2},{19,3},{20,4},{21,5},{22,6},{23,7},{24,8},{25... | collective-permute-start | bytes 2752520 | tf_op jit(solution)/shard_map/ppermute | solution.py:553
  465.6 13.7 %copy-start.4 = (bf16[112,4096]{1,0:T(8,128)(2,1)S(1)}, bf16[112,4096]{1,0:T(8,128)(2,1)}, u32[]{:S(2)}) copy-start(bf16[112,4096]{1,0:T(8,128)(2,1)} %get-tuple-element.15.incoming) | copy-start | bytes 2752516
  465.6 13.7 %copy-start.5 = (bf16[112,4096]{1,0:T(8,128)(2,1)S(1)}, bf16[112,4096]{1,0:T(8,128)(2,1)}, u32[]{:S(2)}) copy-start(bf16[112,4096]{1,0:T(8,128)(2,1)} %norm_back_last.1) | copy-start | bytes 2752516

commit v2 on v1

v2 whole, which is shorter than its diff:
```python
import functools

import jax
import jax.numpy as jnp
from jax import lax
from jax.experimental import pallas as pl
from jax.experimental.pallas import tpu as pltpu
from jax.sharding import PartitionSpec as P

EPSILON = 1e-06
ROOT_HALF = 0.7071067811865476
INV_ROOT_TAU = 0.3989422804014327
BF16 = jnp.bfloat16
F32 = jnp.float32
FEATURE_BLOCKS = 8
SLOT_TILE = 16
VMEM_BYTES = 20 * 1024 * 1024


class Sizes:
    def __init__(self, experts, rows, features, hidden):
        self.experts, self.rows, self.features, self.hidden = experts, rows, features, hidden
        self.capacity = 5 * rows // (2 * experts)
        self.lanes = features // FEATURE_BLOCKS
        self.tiled = self.capacity // SLOT_TILE * SLOT_TILE
        self.rest = self.capacity - self.tiled
        self.tiled_rows = experts * self.tiled
        self.rest_rows = experts * self.rest
        self.slots = experts * self.capacity
        self.message = (experts, FEATURE_BLOCKS * self.capacity, self.lanes)


def iota(shape, axis):
    return lax.broadcasted_iota(jnp.int32, shape, axis)


def dot(left, right):
    return jnp.dot(left, right, preferred_element_type=F32)


def dot_last(left, right):
    return lax.dot_general(left, right, (((1,), (1,)), ((), ())), preferred_element_type=F32)


def gelu_value(values):
    return 0.5 * values * (1.0 + lax.erf(values * ROOT_HALF))


def gelu_slope(values):
    return (
        0.5 * (1.0 + lax.erf(values * ROOT_HALF))
        + values * jnp.exp(-0.5 * values * values) * INV_ROOT_TAU
    )


def halves(values):
    high = values.astype(BF16)
    return high, (values - high.astype(F32)).astype(BF16)


def slot_parts(sizes):
    parts = []
    if sizes.tiled:
        parts.append((sizes.tiled, 0))
    if sizes.rest:
        parts.append((sizes.rest, sizes.tiled))
    return parts


def expansion(sizes, width):
    count = sizes.experts * width
    shape = (count, sizes.experts)
    first = iota(shape, 1) * width
    row = iota(shape, 0)
    return ((row >= first) & (row < first + width)).astype(BF16)


def expansion_across(sizes, width):
    count = sizes.experts * width
    shape = (sizes.experts, count)
    first = iota(shape, 0) * width
    column = iota(shape, 1)
    return ((column >= first) & (column < first + width)).astype(BF16)


def slots_by_token(sizes, table_across, gated):
    rows = sizes.rows
    names = iota((sizes.experts, rows), 0).astype(F32)
    first = table_across[0:1, :] == names
    second = table_across[1:2, :] == names
    chosen = jnp.where(first | second, 1.0, 0.0)
    earlier = (iota((rows, rows), 0) < iota((rows, rows), 1)).astype(BF16)
    rank = jnp.where(chosen > 0.0, dot(chosen.astype(BF16), earlier), -1.0).astype(BF16)
    if gated:
        gate = jnp.where(first, table_across[2:3, :], 0.0) + jnp.where(
            second, table_across[3:4, :], 0.0
        )
        high, low = halves(gate)
    ones, highs, lows = [], [], []
    for width, start in slot_parts(sizes):
        spread = expansion(sizes, width)
        ranks = dot(spread, rank)
        place = iota(ranks.shape, 0) % width + start
        here = ranks == place.astype(F32)
        if gated:
            highs.append(jnp.where(here, dot(spread, high), 0.0).astype(BF16))
            lows.append(jnp.where(here, dot(spread, low), 0.0).astype(BF16))
        else:
            ones.append(jnp.where(here, 1.0, 0.0).astype(BF16))
    if gated:
        return jnp.concatenate(highs, axis=0), jnp.concatenate(lows, axis=0)
    return jnp.concatenate(ones, axis=0)


def tokens_by_slot(sizes, table, gated):
    rows = sizes.rows
    names = iota((rows, sizes.experts), 1).astype(F32)
    first = table[:, 0:1] == names
    second = table[:, 1:2] == names
    chosen = jnp.where(first | second, 1.0, 0.0)
    earlier = (iota((rows, rows), 1) < iota((rows, rows), 0)).astype(BF16)
    rank = jnp.where(chosen > 0.0, dot(earlier, chosen.astype(BF16)), -1.0).astype(BF16)
    if gated:
        gate = jnp.where(first, table[:, 2:3], 0.0) + jnp.where(second, table[:, 3:4], 0.0)
        high, low = halves(gate)
    ones, highs, lows = [], [], []
    for width, start in slot_parts(sizes):
        spread = expansion_across(sizes, width)
        ranks = dot(rank, spread)
        place = iota(ranks.shape, 1) % width + start
        here = ranks == place.astype(F32)
        if gated:
            highs.append(jnp.where(here, dot(high, spread), 0.0).astype(BF16))
            lows.append(jnp.where(here, dot(low, spread), 0.0).astype(BF16))
        else:
            ones.append(jnp.where(here, 1.0, 0.0).astype(BF16))
    if gated:
        return jnp.concatenate(highs, axis=1), jnp.concatenate(lows, axis=1)
    return jnp.concatenate(ones, axis=1)


def write_tiled(sizes, message, block, values):
    if sizes.tiled:
        message[:, block * sizes.tiled : (block + 1) * sizes.tiled, :] = (
            values[: sizes.tiled_rows].astype(BF16).reshape(sizes.experts, sizes.tiled, sizes.lanes)
        )
    return values[sizes.tiled_rows :].astype(BF16)


def rest_places(sizes, block):
    shape = (sizes.rest_rows * FEATURE_BLOCKS, sizes.rest_rows)
    return (iota(shape, 0) == iota(shape, 1) * FEATURE_BLOCKS + block).astype(BF16)


def rest_places_across(sizes, block):
    shape = (sizes.rest_rows, sizes.rest_rows * FEATURE_BLOCKS)
    return (iota(shape, 1) == iota(shape, 0) * FEATURE_BLOCKS + block).astype(BF16)


def write_message(sizes, message, block_values):
    rest = None
    for block in range(FEATURE_BLOCKS):
        other = write_tiled(sizes, message, block, block_values(block))
        if sizes.rest:
            part = dot(rest_places(sizes, block), other)
            rest = part if rest is None else rest + part
    if sizes.rest:
        first = FEATURE_BLOCKS * sizes.tiled
        message[:, first:, :] = rest.reshape(
            sizes.experts, FEATURE_BLOCKS * sizes.rest, sizes.lanes
        ).astype(BF16)


def read_rest(sizes, message):
    if not sizes.rest:
        return None
    first = FEATURE_BLOCKS * sizes.tiled
    return (
        message[:, first:, :]
        .astype(F32)
        .reshape(sizes.rest_rows * FEATURE_BLOCKS, sizes.lanes)
        .astype(BF16)
    )


def read_block(sizes, message, rest, block):
    parts = []
    if sizes.tiled:
        parts.append(
            message[:, block * sizes.tiled : (block + 1) * sizes.tiled, :].reshape(
                sizes.tiled_rows, sizes.lanes
            )
        )
    if sizes.rest:
        parts.append(dot(rest_places_across(sizes, block), rest).astype(BF16))
    return jnp.concatenate(parts, axis=0)


def span(sizes, block):
    return slice(block * sizes.lanes, (block + 1) * sizes.lanes)


def inverse_rms(sizes, read):
    total = jnp.zeros((sizes.rows, 1), F32)
    for block in range(FEATURE_BLOCKS):
        wide = read(block).astype(F32)
        total = total + jnp.sum(wide * wide, axis=1, keepdims=True)
    return lax.rsqrt(total / sizes.features + EPSILON)


def clip_copy(pick, clips, place, done):
    copy = pltpu.make_async_copy(clips.at[pick[0]], place, done)
    copy.start()
    return copy


def first_kernel(sizes, pick, clips, across, message, clip, done):
    clip_copy(pick, clips, clip, done.at[0]).wait()
    send_normed(sizes, clip, across, message)


def cotangent_kernel(sizes, pick, clips, across, message, clip, done):
    clip_copy(pick, clips, clip, done.at[0]).wait()
    send_weighted(sizes, clip, across, message)


def send_normed(sizes, carried, across, message):
    scale = inverse_rms(sizes, lambda block: carried[:, span(sizes, block)])
    select = slots_by_token(sizes, across[...], False)

    def values(block):
        normed = (carried[:, span(sizes, block)].astype(F32) * scale).astype(BF16)
        return dot(select, normed)

    write_message(sizes, message, values)


def send_weighted(sizes, incoming, across, message):
    high, low = slots_by_token(sizes, across[...], True)

    def values(block):
        rows = incoming[:, span(sizes, block)]
        return dot(high, rows) + dot(low, rows)

    write_message(sizes, message, values)


def middle_kernel(sizes, pick, clips, answer, table, across, carried, message, before, done):
    copy = clip_copy(pick, clips, before, done.at[0])
    high, low = tokens_by_slot(sizes, table[...], True)
    rest = read_rest(sizes, answer)
    copy.wait()
    for block in range(FEATURE_BLOCKS):
        rows = read_block(sizes, answer, rest, block)
        mixed = before[:, span(sizes, block)].astype(F32) + (dot(high, rows) + dot(low, rows))
        carried[:, span(sizes, block)] = mixed.astype(BF16)
    send_normed(sizes, carried, across, message)


def norm_back(sizes, carried, incoming, answer, table, result, upstream, copies):
    select = tokens_by_slot(sizes, table[...], False)
    rest = read_rest(sizes, answer)
    copies[0].wait()
    inner = jnp.zeros((sizes.rows, 1), F32)
    squares = jnp.zeros((sizes.rows, 1), F32)
    for block in range(FEATURE_BLOCKS):
        here = span(sizes, block)
        back = dot(select, read_block(sizes, answer, rest, block))
        wide = carried[:, here].astype(F32)
        upstream[:, here] = back
        inner = inner + jnp.sum(wide * back, axis=1, keepdims=True)
        squares = squares + jnp.sum(wide * wide, axis=1, keepdims=True)
    scale = lax.rsqrt(squares / sizes.features + EPSILON)
    pull = scale * scale * scale * (inner / sizes.features)
    copies[1].wait()
    for block in range(FEATURE_BLOCKS):
        here = span(sizes, block)
        wide = carried[:, here].astype(F32)
        result[:, here] = (
            incoming[:, here].astype(F32) + (scale * upstream[:, here] - wide * pull)
        ).astype(BF16)


def last_kernel(
    sizes, pick, clips, incoming, answer, table, far, result, whole, upstream, clip, grad, done
):
    copies = [
        clip_copy(pick, clips, clip, done.at[0]),
        pltpu.make_async_copy(incoming, grad, done.at[1]),
    ]
    copies[1].start()
    near_first = pltpu.make_async_copy(result, whole.at[0], done.at[2])
    far_first = pltpu.make_async_copy(far, whole.at[0], done.at[2])
    near_last = pltpu.make_async_copy(incoming, whole.at[1], done.at[3])

    @pl.when(pick[0] != 0)
    def _():
        far_first.start()
        near_last.start()

    norm_back(sizes, clip, grad, answer, table, result, upstream, copies)

    @pl.when(pick[0] == 0)
    def _():
        near_first.start()
        near_first.wait()

    @pl.when(pick[0] != 0)
    def _():
        far_first.wait()
        near_last.wait()


def turn_kernel(
    sizes, pick, carried, clips, answer, table, across, result, message, upstream, held, grad, done
):
    copies = [
        pltpu.make_async_copy(carried, held, done.at[0]),
        clip_copy(pick, clips, grad, done.at[1]),
    ]
    copies[0].start()
    norm_back(sizes, held, grad, answer, table, result, upstream, copies)
    send_weighted(sizes, result, across, message)


def through_up(sizes, received, up):
    rest = read_rest(sizes, received)
    hidden = jnp.zeros((sizes.slots, sizes.hidden), F32)
    for block in range(FEATURE_BLOCKS):
        rows = read_block(sizes, received, rest, block)
        hidden = hidden + dot(rows, up[span(sizes, block), :])
    return hidden


def through_down_back(sizes, received, down):
    rest = read_rest(sizes, received)
    back = jnp.zeros((sizes.slots, sizes.hidden), F32)
    for block in range(FEATURE_BLOCKS):
        rows = read_block(sizes, received, rest, block)
        back = back + dot_last(rows, down[:, span(sizes, block)])
    return back


def back_message(sizes, back_hidden, up, message):
    write_message(sizes, message, lambda block: dot_last(back_hidden, up[span(sizes, block), :]))


def forward_kernel(sizes, received, up, down, hidden_out, activated_out, message):
    hidden = through_up(sizes, received, up)
    hidden_out[...] = hidden
    activated = gelu_value(hidden).astype(BF16)
    activated_out[...] = activated
    write_message(sizes, message, lambda block: dot(activated, down[:, span(sizes, block)]))


def hidden_back_kernel(sizes, received, down, back_out):
    back_out[...] = through_down_back(sizes, received, down)


def turn_expert_kernel(sizes, received, back, up, activated_out, message):
    hidden = through_up(sizes, received, up)
    activated_out[...] = gelu_value(hidden).astype(BF16)
    back_hidden = (back[...] * gelu_slope(hidden)).astype(BF16)
    back_message(sizes, back_hidden, up, message)


def backward_kernel(sizes, received, hidden, up, down, message):
    slope = gelu_slope(hidden[...])
    back = through_down_back(sizes, received, down)
    back_message(sizes, (back * slope).astype(BF16), up, message)


def choose(pick, wanted, sources, places, semaphores):
    count = len(places)

    def begin(chosen):
        for number in range(count):
            pltpu.make_async_copy(chosen[number], places[number], semaphores.at[number]).start()

    @pl.when(pick[0] == wanted)
    def _():
        begin(sources[:count])

    @pl.when(pick[0] != wanted)
    def _():
        begin(sources[count:])

    for number in range(count):
        pltpu.make_async_copy(sources[number], places[number], semaphores.at[number]).wait()


def weights_kernel(pick, up, down, up_other, down_other, up_0, down_0, up_1, down_1, done):
    mine, others = (up, down), (up_other, down_other)
    choose(pick, 0, mine + others + others + mine, (up_0, down_0, up_1, down_1), done)


def assemble_kernel(pick, far, mine, whole, done):
    @pl.when(pick[0] == 0)
    def _():
        copy = pltpu.make_async_copy(far, whole.at[1], done.at[0])
        copy.start()
        copy.wait()


def down_grad_kernel(sizes, pick, *refs):
    sources, result, here, done = refs[:8], refs[8], refs[9:13], refs[13]
    choose(pick, 0, sources, here, done)
    near, near_grad, far, far_grad = here
    rest_near, rest_far = read_rest(sizes, near_grad), read_rest(sizes, far_grad)
    over_rows = (((0,), (0,)), ((), ()))
    for block in range(FEATURE_BLOCKS):
        rows_near = read_block(sizes, near_grad, rest_near, block)
        rows_far = read_block(sizes, far_grad, rest_far, block)
        total = lax.dot_general(near[...], rows_near, over_rows, preferred_element_type=F32)
        total = total + lax.dot_general(far[...], rows_far, over_rows, preferred_element_type=F32)
        result[:, span(sizes, block)] = total.astype(BF16)


VMEM = pl.BlockSpec(memory_space=pltpu.VMEM)
SMEM = pl.BlockSpec(memory_space=pltpu.SMEM)
HBM = pl.BlockSpec(memory_space=pltpu.HBM)


def call(kernel, name, operands, outs, scratch=(), specs=None, out_specs=None, aliases=None):
    return pl.pallas_call(
        kernel,
        name=name,
        in_specs=specs or [VMEM] * len(operands),
        out_specs=out_specs or [VMEM] * len(outs),
        out_shape=[
            jax.ShapeDtypeStruct(*out) if isinstance(out, tuple) else out for out in outs
        ],
        scratch_shapes=list(scratch),
        input_output_aliases=aliases or {},
        compiler_params=pltpu.CompilerParams(vmem_limit_bytes=VMEM_BYTES),
    )(*operands)


def exchange(message):
    return lax.all_to_all(message, "expert", split_axis=0, concat_axis=0, tiled=True)


def shards(tokens, cotangent, expert_ids, gate_prob, up_weight, down_weight):
    core = lax.axis_index("pipe")
    rows, features = tokens.shape[1], tokens.shape[2]
    hidden = up_weight.shape[3]
    sizes = Sizes(lax.axis_size("expert"), rows, features, hidden)
    swap = [(0, 1), (1, 0)]
    pick = jnp.reshape(core, (1,)).astype(jnp.int32)

    tables = jnp.concatenate([expert_ids[0].astype(F32), gate_prob[0]], axis=-1).swapaxes(1, 2)
    mine = lax.dynamic_index_in_dim(tables, core, 0, keepdims=False)
    theirs = lax.dynamic_index_in_dim(tables, 1 - core, 0, keepdims=False)
    theirs = lax.ppermute(theirs, "pipe", swap)
    across_0 = jnp.where(core == 0, mine, theirs)
    across_1 = jnp.where(core == 0, theirs, mine)
    table_0, table_1 = across_0.T, across_1.T
    up, down, theirs = lax.optimization_barrier((up_weight[0, 0], down_weight[0, 0], theirs))
    up_other = lax.ppermute(up, "pipe", swap)
    down_other = lax.ppermute(down, "pipe", swap)

    upstream_scratch = pltpu.VMEM((rows, features), F32)
    message = (sizes.message, BF16)
    home_rows = ((rows, features), BF16)
    activated = ((sizes.slots, hidden), BF16)
    wide_hidden = ((sizes.slots, hidden), F32)
    rows_scratch = pltpu.VMEM(*home_rows)
    up_shape, down_shape = ((features, hidden), BF16), ((hidden, features), BF16)

    def kernel(body, *more):
        return functools.partial(body, sizes, *more)

    def done(count):
        return pltpu.SemaphoreType.DMA((count,))

    up_0, down_0, up_1, down_1 = call(
        weights_kernel, "weights", [pick, up, down, up_other, down_other],
        [up_shape, down_shape] * 2, [done(4)], [SMEM] + [HBM] * 4, [HBM] * 4,
    )
    (out_0,) = call(
        kernel(first_kernel), "send_tokens", [pick, tokens, across_0], [message],
        [rows_scratch, done(1)], [SMEM, HBM, VMEM],
    )
    in_0 = exchange(out_0)
    (grad_out_1,) = call(
        kernel(cotangent_kernel), "send_cotangent", [pick, cotangent, across_1], [message],
        [rows_scratch, done(1)], [SMEM, HBM, VMEM],
    )
    grad_out_1, in_0 = lax.optimization_barrier((grad_out_1, in_0))
    grad_in_1 = exchange(grad_out_1)
    hidden_0, activated_0, answer_0 = call(
        kernel(forward_kernel), "expert_forward", [in_0, up_0, down_0],
        [wide_hidden, activated, message],
    )
    answer_0, grad_in_1 = lax.optimization_barrier((answer_0, grad_in_1))
    returned_0 = exchange(answer_0)
    (back_1,) = call(kernel(hidden_back_kernel), "hidden_back", [grad_in_1, down_1], [wide_hidden])
    returned_0, back_1 = lax.optimization_barrier((returned_0, back_1))
    carried_1, out_1 = call(
        kernel(middle_kernel), "combine_send", [pick, tokens, returned_0, table_0, across_1],
        [home_rows, message], [rows_scratch, done(1)], [SMEM, HBM, VMEM, VMEM, VMEM],
    )
    in_1 = exchange(out_1)
    activated_1, picks_1 = call(
        kernel(turn_expert_kernel), "expert_turn", [in_1, back_1, up_1], [activated, message]
    )
    back_home_1 = exchange(picks_1)
    grad_1, grad_out_0 = call(
        kernel(turn_kernel), "norm_back_send",
        [pick, carried_1, cotangent, back_home_1, table_1, across_0],
        [home_rows, message], [upstream_scratch, rows_scratch, rows_scratch, done(2)],
        [SMEM, HBM, HBM, VMEM, VMEM, VMEM],
    )
    grad_in_0 = exchange(grad_out_0)
    (picks_0,) = call(
        kernel(backward_kernel), "expert_backward", [grad_in_0, hidden_0, up_0, down_0], [message]
    )
    back_home_0 = exchange(picks_0)

    to_first, to_second = [(1, 0)], [(0, 1)]
    operands = []
    for near, way in (
        ([activated_0, grad_in_0], to_first), ([activated_1, grad_in_1], to_second)
    ):
        operands += near + [lax.ppermute(array, "pipe", way) for array in near]
    (down_grad,) = call(
        kernel(down_grad_kernel), "down_grad", [pick] + operands, [((hidden, features), BF16)],
        [pltpu.VMEM(*activated), pltpu.VMEM(*message)] * 2 + [pltpu.SemaphoreType.DMA((4,))],
        [SMEM] + [HBM] * 8,
    )
    far_1 = lax.ppermute(grad_1, "pipe", to_second)
    down_grad, far_1, back_home_0 = lax.optimization_barrier((down_grad, far_1, back_home_0))
    held = (tokens.shape, BF16)
    grad_0, input_grad = call(
        kernel(last_kernel), "norm_back_last", [pick, tokens, grad_1, back_home_0, table_0, far_1],
        [home_rows, held], [upstream_scratch, rows_scratch, rows_scratch, done(4)],
        [SMEM, HBM, HBM, VMEM, VMEM, HBM], [VMEM, HBM],
    )
    far_0 = lax.ppermute(grad_0, "pipe", to_first)
    (input_grad,) = call(
        assemble_kernel, "assemble", [pick, far_0, input_grad], [held], [pltpu.SemaphoreType.DMA((1,))],
        [SMEM, HBM, HBM], [HBM], {2: 0},
    )
    return input_grad[None], down_grad[None, None]


def solution(mesh):
    placed = (
        P(None, "expert", None),
        P(None, "expert", None),
        P("pipe", None, "expert", None),
        P("pipe", None, "expert", None),
        P("pipe", "expert", None, None),
        P("pipe", "expert", None, None),
    )
    return jax.shard_map(
        shards,
        mesh=mesh,
        in_specs=placed,
        out_specs=(P("pipe", None, "expert", None), P("pipe", "expert", None, None)),
        check_vma=False,
    )
```

time: 483 us -> 442 us (0.915)
  waiting for transfers between devices: 178 us -> 140 us
  local copies, waits for them, and re-layouts: 4.26 us -> 34.4 us
  Pallas kernels: 86.1 us -> 60.6 us
  other arithmetic: 9.2 us -> 1.4 us
    all_to_all x4, waiting for transfers between devices: 170 us -> 134 us  [exchange(): lax.all_to_all(message, 'expert', split_axis=0, concat_axis=0, tiled=True)]
    unnamed x16 -> x58, local copies, waits for them, and re-layouts: 2.73 us -> 34.3 us
    pallas_call x10 -> x12, Pallas kernels: 86.1 us -> 60.6 us  [call(): pl.pallas_call(kernel, name=name, in_specs=specs or [VMEM] * len(operands...]
    select_n x4 -> x1, other arithmetic: 7.82 us -> 0.01 us  [shards(): across_0 = jnp.where(core == 0, mine, theirs)]
    ppermute x1, waiting for transfers between devices: 7.77 us -> 0.78 us  [shards(): theirs = lax.ppermute(theirs, 'pipe', swap)]
  transfers between devices with their start and end apart: 13 -> 13, of which waited for: 5 -> 7; matrix products, arithmetic and copies ran while one was open for 2% -> 0% of each run, Pallas kernels for 9% -> 7%
where the time goes in v2:
time: 442 us; the launch traced here: 440 us
  blocking collectives  164 us (37%)
  waiting for transfers between devices  140 us (32%)
  Pallas kernels  60.6 us (14%)
  starting transfers between devices  39 us (9%)
  local copies, waits for them, and re-layouts  34.4 us (8%)
    all_to_all x3, blocking collectives, exchange(): lax.all_to_all(message, 'expert', split_axis=0, concat_axis=0, tiled=True)  164 us
    all_to_all x4, waiting for transfers between devices, exchange(): lax.all_to_all(message, 'expert', split_axis=0, concat_axis=0, tiled=True)  134 us
    pallas_call x12, Pallas kernels, call(): pl.pallas_call(kernel, name=name, in_specs=specs or [VMEM] * len(operands...  60.6 us
    unnamed x58, local copies, waits for them, and re-layouts  34.3 us
    all_to_all x4, starting transfers between devices, exchange(): lax.all_to_all(message, 'expert', split_axis=0, concat_axis=0, tiled=True)  21.4 us
    ppermute x4, starting transfers between devices, shards(): operands += near + [lax.ppermute(array, 'pipe', way) for array in near]  10.2 us
  transfers between devices with their start and end apart: 13, of which 7 were waited for; matrix products, arithmetic and copies ran while one was open for 0% of the time, Pallas kernels for 7%

profile of v2, /device:TPU:13, one launch (start us, length us, event | category | flops | bytes accessed | tf_op | source)
XLA Modules:
  0.0 440.3 jit_solution(15691538307181150655)
XLA Ops:
  9.2 6.6 %all-to-all-start = ((bf16[16,136,512]{2,1,0:T(8,128)(2,1)}), bf16[16,136,512]{2,1,0:T(8,128)(2,1)S(1)}, u32[]{:S(2)}, u32[]{:S(2)}) async-start(bf16[16,136,512]{2,1,0:T(8,128)(2,1)} %copy-done.7), calls=%async_computation | async-start | bytes 4456448 | tf_op jit(solution)/shard_map/all_to_all | solution.py:440
  18.3 3.0 send_cotangent.1
  22.7 43.6 %all-to-all-done.received = bf16[16,136,512]{2,1,0:T(8,128)(2,1)S(1)} async-done(((bf16[16,136,512]{2,1,0:T(8,128)(2,1)}), bf16[16,136,512]{2,1,0:T(8,128)(2,1)S(1)}, u32[]{:S(2)}, u32[]{:S(2)}) %all-to-all-start) | async-done | bytes 2228256 | tf_op jit(solution)/shard_map/all_to_all | solution.py:440
  66.3 4.7 %all-to-all-start.1 = ((bf16[16,136,512]{2,1,0:T(8,128)(2,1)}), bf16[16,136,512]{2,1,0:T(8,128)(2,1)}, u32[]{:S(2)}, u32[]{:S(2)}) async-start(bf16[16,136,512]{2,1,0:T(8,128)(2,1)} %copy-done.6), calls=%async_computation.1 | async-start | bytes 4456448 | tf_op jit(solution)/shard_map/all_to_all | solution.py:440
  73.8 6.5 %weights.1 = (bf16[4096,768]{1,0:T(8,128)(2,1)S(1)}, bf16[768,4096]{1,0:T(8,128)(2,1)S(1)}, bf16[4096,768]{1,0:T(8,128)(2,1)S(1)}, bf16[768,4096]{1,0:T(8,128)(2,1)S(1)}) custom-call(s32[1]{0:T(128)} %bitcast.pick, bf16[4096,768]{1,0:T(8,128)(2,1)S(1)} %bitcast.23, bf16[768,4096]{1,0:T(8,128)(2,1)} %bitcast.29, ...), custom_call_target="tpu_custom_call" | custom-call | tf_op jit(solution)/shard_map/weights/pallas_call | solution.py:425
  85.8 5.7 %expert_forward.1 = (f32[272,768]{1,0:T(8,128)S(1)}, bf16[272,768]{1,0:T(8,128)(2,1)S(1)}, bf16[16,136,512]{2,1,0:T(8,128)(2,1)S(1)}) custom-call(bf16[16,136,512]{2,1,0:T(8,128)(2,1)S(1)} %all-to-all-done.received, bf16[4096,768]{1,0:T(8,128)(2,1)S(1)} %get-tuple-element.31.up, bf16[768,4096]{1,0:T(8,128)(2,1)S(1)} %get-tuple-element.32.down), custom_call_target="tpu_custom_call" | custom-call | tf_op jit(solution)/shard_map/expert_forward/pallas_call | solution.py:425
  99.1 22.9 %all-to-all-done.1.received.refs_5_ = bf16[16,136,512]{2,1,0:T(8,128)(2,1)} async-done(((bf16[16,136,512]{2,1,0:T(8,128)(2,1)}), bf16[16,136,512]{2,1,0:T(8,128)(2,1)}, u32[]{:S(2)}, u32[]{:S(2)}) %all-to-all-start.1) | async-done | bytes 2228256 | tf_op jit(solution)/shard_map/all_to_all | solution.py:440
  122.1 4.5 %all-to-all-start.2 = ((bf16[16,136,512]{2,1,0:T(8,128)(2,1)}), bf16[16,136,512]{2,1,0:T(8,128)(2,1)}, u32[]{:S(2)}, u32[]{:S(2)}) async-start(bf16[16,136,512]{2,1,0:T(8,128)(2,1)} %copy-done.15), calls=%async_computation.2 | async-start | bytes 4456448 | tf_op jit(solution)/shard_map/all_to_all | solution.py:440
  129.4 4.3 hidden_back.1.back
  133.7 43.5 %all-to-all-done.2.answer = bf16[16,136,512]{2,1,0:T(8,128)(2,1)} async-done(((bf16[16,136,512]{2,1,0:T(8,128)(2,1)}), bf16[16,136,512]{2,1,0:T(8,128)(2,1)}, u32[]{:S(2)}, u32[]{:S(2)}) %all-to-all-start.2) | async-done | bytes 2228256 | tf_op jit(solution)/shard_map/all_to_all | solution.py:440
  177.2 6.0 %combine_send.1 = (bf16[112,4096]{1,0:T(8,128)(2,1)S(1)}, bf16[16,136,512]{2,1,0:T(8,128)(2,1)S(1)}) custom-call(s32[1]{0:T(128)} %bitcast.pick, bf16[2,112,4096]{2,1,0:T(8,128)(2,1)S(1)} %copy-done.3, bf16[16,136,512]{2,1,0:T(8,128)(2,1)} %all-to-all-done.2.answer, f32[112,4]{1,0:T(8,128)S(1)} %bitcast.24, f32[4,112]{1,0:T(4,128)S(1)} %copy.17.across), custom_call_target="tpu_custom_call" | custom-call | tf_op jit(solution)/shard_map/combine_send/pallas_call | solution.py:425
  183.3 53.8 %all_to_all.35.received = bf16[16,136,512]{2,1,0:T(8,128)(2,1)S(1)} all-to-all(bf16[16,136,512]{2,1,0:T(8,128)(2,1)S(1)} %get-tuple-element.40), channel_id=1, replica_groups=mesh['pipe'=2,'expert'=16] {'expert'}, dimensions={0} | all-to-all | bytes 4456448 | tf_op jit(solution)/shard_map/all_to_all | solution.py:440
  239.9 6.0 %expert_turn.1 = (bf16[272,768]{1,0:T(8,128)(2,1)S(1)}, bf16[16,136,512]{2,1,0:T(8,128)(2,1)S(1)}) custom-call(bf16[16,136,512]{2,1,0:T(8,128)(2,1)S(1)} %all_to_all.35.received, f32[272,768]{1,0:T(8,128)S(1)} %hidden_back.1.back, bf16[4096,768]{1,0:T(8,128)(2,1)S(1)} %copy-done.11), custom_call_target="tpu_custom_call" | custom-call | tf_op jit(solution)/shard_map/expert_turn/pallas_call | solution.py:425
  246.6 55.2 %all_to_all.36.answer = bf16[16,136,512]{2,1,0:T(8,128)(2,1)S(1)} all-to-all(bf16[16,136,512]{2,1,0:T(8,128)(2,1)S(1)} %get-tuple-element.43), channel_id=1, replica_groups=mesh['pipe'=2,'expert'=16] {'expert'}, dimensions={0} | all-to-all | bytes 4456448 | tf_op jit(solution)/shard_map/all_to_all | solution.py:440
  301.8 5.1 %norm_back_send.1 = (bf16[112,4096]{1,0:T(8,128)(2,1)S(1)}, bf16[16,136,512]{2,1,0:T(8,128)(2,1)S(1)}) custom-call(s32[1]{0:T(128)} %bitcast.pick, bf16[112,4096]{1,0:T(8,128)(2,1)S(1)} %get-tuple-element.39.carried, bf16[2,112,4096]{2,1,0:T(8,128)(2,1)S(1)} %copy-done.9, bf16[16,136,512]{2,1,0:T(8,128)(2,1)S(1)} %all_to_all.36.answer, ...), custom_call_target="tpu_custom_call" | custom-call | tf_op jit(solution)/shard_map/norm_back_send/pallas_call | solution.py:425
  307.0 55.1 %all_to_all.37.refs_1_.received = bf16[16,136,512]{2,1,0:T(8,128)(2,1)S(1)} all-to-all(bf16[16,136,512]{2,1,0:T(8,128)(2,1)S(1)} %get-tuple-element.46), channel_id=1, replica_groups=mesh['pipe'=2,'expert'=16] {'expert'}, dimensions={0} | all-to-all | bytes 4456448 | tf_op jit(solution)/shard_map/all_to_all | solution.py:440
  362.2 5.5 %expert_backward.1 = bf16[16,136,512]{2,1,0:T(8,128)(2,1)S(1)} custom-call(bf16[16,136,512]{2,1,0:T(8,128)(2,1)S(1)} %all_to_all.37.refs_1_.received, f32[272,768]{1,0:T(8,128)S(1)} %copy-done.21, bf16[4096,768]{1,0:T(8,128)(2,1)S(1)} %bitcast.19, bf16[768,4096]{1,0:T(8,128)(2,1)S(1)} %bitcast.21), custom_call_target="tpu_custom_call" | custom-call | tf_op jit(solution)/shard_map/expert_backward/pallas_call | solution.py:425
  369.0 5.6 %all-to-all-start.6 = ((bf16[16,136,512]{2,1,0:T(8,128)(2,1)}), bf16[16,136,512]{2,1,0:T(8,128)(2,1)}, u32[]{:S(2)}, u32[]{:S(2)}) async-start(bf16[16,136,512]{2,1,0:T(8,128)(2,1)} %copy-done.5), calls=%async_computation.6 | async-start | bytes 4456448 | tf_op jit(solution)/shard_map/all_to_all | solution.py:440
  375.9 4.5 %collective-permute-start.4 = (bf16[16,136,512]{2,1,0:T(8,128)(2,1)S(1)}, bf16[16,136,512]{2,1,0:T(8,128)(2,1)S(1)}, u32[]{:S(2)}, u32[]{:S(2)}) collective-permute-start(bf16[16,136,512]{2,1,0:T(8,128)(2,1)S(1)} %all_to_all.37.refs_1_.received), channel_id=1, source_target_pairs={{16,0},{17,1},{18,2},{19,3},{20,4},{21,5},{22,6},{23,7},{24,8},{25... | collective-permute-start | bytes 6684680 | tf_op jit(solution)/shard_map/ppermute | solution.py:525
  381.7 3.1 collective-permute-start.3
  388.5 11.9 %down_grad.1 = bf16[768,4096]{1,0:T(8,128)(2,1)} custom-call(s32[1]{0:T(128)} %bitcast.pick, bf16[272,768]{1,0:T(8,128)(2,1)S(1)} %get-tuple-element.45.refs_0_, bf16[16,136,512]{2,1,0:T(8,128)(2,1)S(1)} %all_to_all.37.refs_1_.received, bf16[272,768]{1,0:T(8,128)(2,1)S(1)} %collective-permute-done.3.refs_2_, ...), custom_call_target="tpu_custom_call" | custom-call | tf_op jit(solution)/shard_map/down_grad/pallas_call | solution.py:425
  401.4 24.3 %all-to-all-done.6.answer = bf16[16,136,512]{2,1,0:T(8,128)(2,1)} async-done(((bf16[16,136,512]{2,1,0:T(8,128)(2,1)}), bf16[16,136,512]{2,1,0:T(8,128)(2,1)}, u32[]{:S(2)}, u32[]{:S(2)}) %all-to-all-start.6) | async-done | bytes 2228256 | tf_op jit(solution)/shard_map/all_to_all | solution.py:440
  429.6 4.1 norm_back_last.1
  433.7 4.4 collective-permute-start.8
  (82 shorter events, 49.0 us)
Async XLA Ops:
  2.1 1.6 collective-permute-start
  9.2 57.2 %all-to-all-start = ((bf16[16,136,512]{2,1,0:T(8,128)(2,1)}), bf16[16,136,512]{2,1,0:T(8,128)(2,1)S(1)}, u32[]{:S(2)}, u32[]{:S(2)}) async-start(bf16[16,136,512]{2,1,0:T(8,128)(2,1)} %copy-done.7), calls=%async_computation | async-start | bytes 4456448 | tf_op jit(solution)/shard_map/all_to_all | solution.py:440
  15.8 55.3 %collective-permute-start.1 = (bf16[4096,768]{1,0:T(8,128)(2,1)}, bf16[4096,768]{1,0:T(8,128)(2,1)}, u32[]{:S(2)}, u32[]{:S(2)}) collective-permute-start(bf16[4096,768]{1,0:T(8,128)(2,1)} %bitcast.22), channel_id=1, source_target_pairs={{0,16},{16,0},{1,17},{17,1},{2,18},{18,2},{3,19},{19,3},{4,20},{20... | collective-permute-start | bytes 18874376 | tf_op jit(solution)/shard_map/ppermute | solution.py:459
  16.7 54.4 %collective-permute-start.2 = (bf16[768,4096]{1,0:T(8,128)(2,1)}, bf16[768,4096]{1,0:T(8,128)(2,1)}, u32[]{:S(2)}, u32[]{:S(2)}) collective-permute-start(bf16[768,4096]{1,0:T(8,128)(2,1)} %bitcast.28), channel_id=1, source_target_pairs={{0,16},{16,0},{1,17},{17,1},{2,18},{18,2},{3,19},{19,3},{4,20},{20... | collective-permute-start | bytes 18874376 | tf_op jit(solution)/shard_map/ppermute | solution.py:460
  66.3 55.7 %all-to-all-start.1 = ((bf16[16,136,512]{2,1,0:T(8,128)(2,1)}), bf16[16,136,512]{2,1,0:T(8,128)(2,1)}, u32[]{:S(2)}, u32[]{:S(2)}) async-start(bf16[16,136,512]{2,1,0:T(8,128)(2,1)} %copy-done.6), calls=%async_computation.1 | async-start | bytes 4456448 | tf_op jit(solution)/shard_map/all_to_all | solution.py:440
  71.1 2.8 copy-start.14
  122.1 55.2 %all-to-all-start.2 = ((bf16[16,136,512]{2,1,0:T(8,128)(2,1)}), bf16[16,136,512]{2,1,0:T(8,128)(2,1)}, u32[]{:S(2)}, u32[]{:S(2)}) async-start(bf16[16,136,512]{2,1,0:T(8,128)(2,1)} %copy-done.15), calls=%async_computation.2 | async-start | bytes 4456448 | tf_op jit(solution)/shard_map/all_to_all | solution.py:440
  126.6 2.8 copy-start.13
  129.4 47.9 %copy-start.3 = (bf16[2,112,4096]{2,1,0:T(8,128)(2,1)S(1)}, bf16[2,112,4096]{2,1,0:T(8,128)(2,1)}, u32[]{:S(2)}) copy-start(bf16[2,112,4096]{2,1,0:T(8,128)(2,1)} %clips.9) | copy-start | bytes 5505028
  239.9 62.0 %copy-start.9 = (bf16[2,112,4096]{2,1,0:T(8,128)(2,1)S(1)}, bf16[2,112,4096]{2,1,0:T(8,128)(2,1)}, u32[]{:S(2)}) copy-start(bf16[2,112,4096]{2,1,0:T(8,128)(2,1)} %clips.8) | copy-start | bytes 5505028
  239.9 122.2 %slice-start.2 = ((s8[6291456]{0:T(1024)(128)(4,1)}), s8[4194304]{0:T(1024)(128)(4,1)S(1)}, s32[]{:S(2)}) async-start(s8[6291456]{0:T(1024)(128)(4,1)} %bitcast.20), calls=%async_computation.9 | async-start | bytes 8388608
  246.6 115.5 %slice-start = ((s8[6291456]{0:T(1024)(128)(4,1)}), s8[4194304]{0:T(1024)(128)(4,1)S(1)}, s32[]{:S(2)}) async-start(s8[6291456]{0:T(1024)(128)(4,1)} %bitcast.18), calls=%async_computation.7 | async-start | bytes 8388608
  246.6 115.5 %slice-start.3 = ((s8[6291456]{0:T(1024)(128)(4,1)}), s8[2097152]{0:T(1024)(128)(4,1)S(1)}, s32[]{:S(2)}) async-start(s8[6291456]{0:T(1024)(128)(4,1)} %bitcast.20), calls=%async_computation.10 | async-start | bytes 4194304
  301.8 60.3 %slice-start.1 = ((s8[6291456]{0:T(1024)(128)(4,1)}), s8[2097152]{0:T(1024)(128)(4,1)S(1)}, s32[]{:S(2)}) async-start(s8[6291456]{0:T(1024)(128)(4,1)} %bitcast.18), calls=%async_computation.8 | async-start | bytes 4194304
  307.0 55.2 %copy-start.16 = (bf16[112,4096]{1,0:T(8,128)(2,1)}, bf16[112,4096]{1,0:T(8,128)(2,1)S(1)}, u32[]{:S(2)}) copy-start(bf16[112,4096]{1,0:T(8,128)(2,1)S(1)} %get-tuple-element.44.incoming) | copy-start | bytes 2752516
  307.0 55.2 %copy-start.21 = (f32[272,768]{1,0:T(8,128)S(1)}, f32[272,768]{1,0:T(8,128)}, u32[]{:S(2)}) copy-start(f32[272,768]{1,0:T(8,128)} %copy-done.20) | copy-start | bytes 2506756
  369.0 15.8 %copy-start.23 = (bf16[272,768]{1,0:T(8,128)(2,1)S(1)}, bf16[272,768]{1,0:T(8,128)(2,1)}, u32[]{:S(2)}) copy-start(bf16[272,768]{1,0:T(8,128)(2,1)} %copy-done.22) | copy-start | bytes 1253380
  369.0 56.7 %all-to-all-start.6 = ((bf16[16,136,512]{2,1,0:T(8,128)(2,1)}), bf16[16,136,512]{2,1,0:T(8,128)(2,1)}, u32[]{:S(2)}, u32[]{:S(2)}) async-start(bf16[16,136,512]{2,1,0:T(8,128)(2,1)} %copy-done.5), calls=%async_computation.6 | async-start | bytes 4456448 | tf_op jit(solution)/shard_map/all_to_all | solution.py:440
  374.6 11.6 %collective-permute-start.6 = (bf16[16,136,512]{2,1,0:T(8,128)(2,1)}, bf16[16,136,512]{2,1,0:T(8,128)(2,1)S(1)}, u32[]{:S(2)}, u32[]{:S(2)}) collective-permute-start(bf16[16,136,512]{2,1,0:T(8,128)(2,1)} %all-to-all-done.1.received.refs_5_), channel_id=1, source_target_pairs={{0,16},{1,17},{2,18},{3,19},{4,20},{5,21},{6,22},{7,23},{8,24},{9,... | collective-permute-start | bytes 6684680 | tf_op jit(solution)/shard_map/ppermute | solution.py:525
  375.9 12.6 %collective-permute-start.4 = (bf16[16,136,512]{2,1,0:T(8,128)(2,1)S(1)}, bf16[16,136,512]{2,1,0:T(8,128)(2,1)S(1)}, u32[]{:S(2)}, u32[]{:S(2)}) collective-permute-start(bf16[16,136,512]{2,1,0:T(8,128)(2,1)S(1)} %all_to_all.37.refs_1_.received), channel_id=1, source_target_pairs={{16,0},{17,1},{18,2},{19,3},{20,4},{21,5},{22,6},{23,7},{24,8},{25... | collective-permute-start | bytes 6684680 | tf_op jit(solution)/shard_map/ppermute | solution.py:525
  380.4 20.0 %collective-permute-start.7 = (bf16[112,4096]{1,0:T(8,128)(2,1)}, bf16[112,4096]{1,0:T(8,128)(2,1)S(1)}, u32[]{:S(2)}, u32[]{:S(2)}) collective-permute-start(bf16[112,4096]{1,0:T(8,128)(2,1)} %copy-done.16), channel_id=1, source_target_pairs={{0,16},{1,17},{2,18},{3,19},{4,20},{5,21},{6,22},{7,23},{8,24},{9,... | collective-permute-start | bytes 2752520 | tf_op jit(solution)/shard_map/ppermute | solution.py:531
  381.7 4.5 %collective-permute-start.3 = (bf16[272,768]{1,0:T(8,128)(2,1)S(1)}, bf16[272,768]{1,0:T(8,128)(2,1)S(1)}, u32[]{:S(2)}, u32[]{:S(2)}) collective-permute-start(bf16[272,768]{1,0:T(8,128)(2,1)S(1)} %get-tuple-element.45.refs_0_), channel_id=1, source_target_pairs={{16,0},{17,1},{18,2},{19,3},{20,4},{21,5},{22,6},{23,7},{24,8},{25... | collective-permute-start | bytes 1253384 | tf_op jit(solution)/shard_map/ppermute | solution.py:525
  384.8 3.7 collective-permute-start.5
  433.7 6.4 %collective-permute-start.8 = (bf16[112,4096]{1,0:T(8,128)(2,1)S(1)}, bf16[112,4096]{1,0:T(8,128)(2,1)S(1)}, u32[]{:S(2)}, u32[]{:S(2)}) collective-permute-start(bf16[112,4096]{1,0:T(8,128)(2,1)S(1)} %get-tuple-element.51), channel_id=1, source_target_pairs={{16,0},{17,1},{18,2},{19,3},{20,4},{21,5},{22,6},{23,7},{24,8},{25... | collective-permute-start | bytes 2752520 | tf_op jit(solution)/shard_map/ppermute | solution.py:539
  (17 other events, 28.6 us)

commit v3 on v2

--- a/solution.py
+++ b/solution.py
@@ -13,8 +13,10 @@
 BF16 = jnp.bfloat16
 F32 = jnp.float32
 FEATURE_BLOCKS = 8
+PLANES = 4
 SLOT_TILE = 16
 VMEM_BYTES = 20 * 1024 * 1024
+WHOLE_VMEM_BYTES = 60 * 1024 * 1024
 
 
 class Sizes:
@@ -28,6 +30,7 @@
         self.rest_rows = experts * self.rest
         self.slots = experts * self.capacity
         self.message = (experts, FEATURE_BLOCKS * self.capacity, self.lanes)
+        self.in_plane = experts // PLANES
 
 
 def iota(shape, axis):
@@ -83,9 +86,9 @@
     return ((column >= first) & (column < first + width)).astype(BF16)
 
 
-def slots_by_token(sizes, table_across, gated):
+def slots_by_token(sizes, table_across, gated, base=0):
     rows = sizes.rows
-    names = iota((sizes.experts, rows), 0).astype(F32)
+    names = (iota((sizes.experts, rows), 0) ^ base).astype(F32)
     first = table_across[0:1, :] == names
     second = table_across[1:2, :] == names
     chosen = jnp.where(first | second, 1.0, 0.0)
@@ -139,14 +142,6 @@
     return jnp.concatenate(ones, axis=1)
 
 
-def write_tiled(sizes, message, block, values):
-    if sizes.tiled:
-        message[:, block * sizes.tiled : (block + 1) * sizes.tiled, :] = (
-            values[: sizes.tiled_rows].astype(BF16).reshape(sizes.experts, sizes.tiled, sizes.lanes)
-        )
-    return values[sizes.tiled_rows :].astype(BF16)
-
-
 def rest_places(sizes, block):
     shape = (sizes.rest_rows * FEATURE_BLOCKS, sizes.rest_rows)
     return (iota(shape, 0) == iota(shape, 1) * FEATURE_BLOCKS + block).astype(BF16)
@@ -157,18 +152,29 @@
     return (iota(shape, 1) == iota(shape, 0) * FEATURE_BLOCKS + block).astype(BF16)
 
 
-def write_message(sizes, message, block_values):
+def write_pieces(sizes, pieces, block_values):
+    tile, each = sizes.tiled, sizes.experts // len(pieces)
     rest = None
     for block in range(FEATURE_BLOCKS):
-        other = write_tiled(sizes, message, block, block_values(block))
+        values = block_values(block)
+        if tile:
+            for number, piece in enumerate(pieces):
+                rows = values[number * each * tile : (number + 1) * each * tile].astype(BF16)
+                piece[:, block * tile : (block + 1) * tile, :] = rows.reshape(
+                    each, tile, sizes.lanes
+                )
         if sizes.rest:
-            part = dot(rest_places(sizes, block), other)
+            part = dot(rest_places(sizes, block), values[sizes.tiled_rows :].astype(BF16))
             rest = part if rest is None else rest + part
     if sizes.rest:
-        first = FEATURE_BLOCKS * sizes.tiled
-        message[:, first:, :] = rest.reshape(
-            sizes.experts, FEATURE_BLOCKS * sizes.rest, sizes.lanes
-        ).astype(BF16)
+        first, each_rest = FEATURE_BLOCKS * tile, FEATURE_BLOCKS * sizes.rest
+        for number, piece in enumerate(pieces):
+            rows = rest[number * each * each_rest : (number + 1) * each * each_rest]
+            piece[:, first:, :] = rows.reshape(each, each_rest, sizes.lanes).astype(BF16)
+
+
+def write_message(sizes, message, block_values):
+    write_pieces(sizes, [message], block_values)
 
 
 def read_rest(sizes, message):
@@ -219,9 +225,23 @@
     send_normed(sizes, clip, across, message)
 
 
-def cotangent_kernel(sizes, pick, clips, across, message, clip, done):
+def cotangent_kernel(sizes, pick, clips, across, *refs):
+    planes, (clip, done) = refs[:PLANES], refs[PLANES:]
     clip_copy(pick, clips, clip, done.at[0]).wait()
-    send_weighted(sizes, clip, across, message)
+    send_weighted(sizes, clip, across, planes, pick[1])
+
+
+def regroup_kernel(sizes, *refs):
+    planes, places = refs[:PLANES], refs[PLANES:]
+    for number, place in enumerate(places):
+        for plane_number, plane in enumerate(planes):
+            place[plane_number] = plane[number]
+
+
+def far_kernel(*refs):
+    *places, plane = refs
+    for number, place in enumerate(places):
+        plane[number] = place[PLANES - 1]
 
 
 def send_normed(sizes, carried, across, message):
@@ -235,21 +255,19 @@
     write_message(sizes, message, values)
 
 
-def send_weighted(sizes, incoming, across, message):
-    high, low = slots_by_token(sizes, across[...], True)
+def send_weighted(sizes, incoming, across, pieces, base=0):
+    high, low = slots_by_token(sizes, across[...], True, base)
 
     def values(block):
         rows = incoming[:, span(sizes, block)]
         return dot(high, rows) + dot(low, rows)
 
-    write_message(sizes, message, values)
-
-
-def middle_kernel(sizes, pick, clips, answer, table, across, carried, message, before, done):
-    copy = clip_copy(pick, clips, before, done.at[0])
+    write_pieces(sizes, pieces, values)
+
+
+def middle_kernel(sizes, before, answer, table, across, carried, message):
     high, low = tokens_by_slot(sizes, table[...], True)
     rest = read_rest(sizes, answer)
-    copy.wait()
     for block in range(FEATURE_BLOCKS):
         rows = read_block(sizes, answer, rest, block)
         mixed = before[:, span(sizes, block)].astype(F32) + (dot(high, rows) + dot(low, rows))
@@ -257,10 +275,11 @@
     send_normed(sizes, carried, across, message)
 
 
-def norm_back(sizes, carried, incoming, answer, table, result, upstream, copies):
+def norm_back(sizes, carried, incoming, answer, table, result, upstream, copies=()):
     select = tokens_by_slot(sizes, table[...], False)
     rest = read_rest(sizes, answer)
-    copies[0].wait()
+    for copy in copies[:1]:
+        copy.wait()
     inner = jnp.zeros((sizes.rows, 1), F32)
     squares = jnp.zeros((sizes.rows, 1), F32)
     for block in range(FEATURE_BLOCKS):
@@ -272,7 +291,8 @@
         squares = squares + jnp.sum(wide * wide, axis=1, keepdims=True)
     scale = lax.rsqrt(squares / sizes.features + EPSILON)
     pull = scale * scale * scale * (inner / sizes.features)
-    copies[1].wait()
+    for copy in copies[1:]:
+        copy.wait()
     for block in range(FEATURE_BLOCKS):
         here = span(sizes, block)
         wide = carried[:, here].astype(F32)
@@ -282,45 +302,39 @@
 
 
 def last_kernel(
-    sizes, pick, clips, incoming, answer, table, far, result, whole, upstream, clip, grad, done
+    sizes, pick, before, incoming, answer, table, far,
+    result, whole, upstream, clip, grad, apart, done,
 ):
     copies = [
-        clip_copy(pick, clips, clip, done.at[0]),
+        pltpu.make_async_copy(before, clip, done.at[0]),
         pltpu.make_async_copy(incoming, grad, done.at[1]),
     ]
-    copies[1].start()
-    near_first = pltpu.make_async_copy(result, whole.at[0], done.at[2])
-    far_first = pltpu.make_async_copy(far, whole.at[0], done.at[2])
-    near_last = pltpu.make_async_copy(incoming, whole.at[1], done.at[3])
+    for copy in copies:
+        copy.start()
+    far_copy = pltpu.make_async_copy(far, apart, done.at[2])
+    far_copy.start()
+    norm_back(sizes, clip, grad, answer, table, result, upstream, copies)
+    far_copy.wait()
+
+    @pl.when(pick[0] == 0)
+    def _():
+        near_first = pltpu.make_async_copy(result, whole.at[0], done.at[2])
+        near_first.start()
+        near_first.wait()
 
     @pl.when(pick[0] != 0)
     def _():
+        far_first = pltpu.make_async_copy(apart, whole.at[0], done.at[2])
+        near_last = pltpu.make_async_copy(grad, whole.at[1], done.at[3])
         far_first.start()
         near_last.start()
-
-    norm_back(sizes, clip, grad, answer, table, result, upstream, copies)
-
-    @pl.when(pick[0] == 0)
-    def _():
-        near_first.start()
-        near_first.wait()
-
-    @pl.when(pick[0] != 0)
-    def _():
         far_first.wait()
         near_last.wait()
 
 
-def turn_kernel(
-    sizes, pick, carried, clips, answer, table, across, result, message, upstream, held, grad, done
-):
-    copies = [
-        pltpu.make_async_copy(carried, held, done.at[0]),
-        clip_copy(pick, clips, grad, done.at[1]),
-    ]
-    copies[0].start()
-    norm_back(sizes, held, grad, answer, table, result, upstream, copies)
-    send_weighted(sizes, result, across, message)
+def turn_kernel(sizes, carried, incoming, answer, table, across, result, message, upstream):
+    norm_back(sizes, carried, incoming, answer, table, result, upstream)
+    send_weighted(sizes, result, across, [message])
 
 
 def through_up(sizes, received, up):
@@ -353,7 +367,25 @@
     write_message(sizes, message, lambda block: dot(activated, down[:, span(sizes, block)]))
 
 
-def hidden_back_kernel(sizes, received, down, back_out):
+def hidden_back_kernel(sizes, pick, down, *refs):
+    count, last = sizes.in_plane, PLANES - 1
+    places, far, (back_out, received, here, done) = refs[:count], refs[count], refs[count + 1 :]
+    copies = []
+    for number, place in enumerate(places):
+        first = number * PLANES
+        copies += [
+            pltpu.make_async_copy(
+                place.at[pl.ds(0, last)], here.at[pl.ds(first, last)], done.at[number]
+            ),
+            pltpu.make_async_copy(far.at[number], here.at[first + last], done.at[count + number]),
+        ]
+    for copy in copies:
+        copy.start()
+    for copy in copies:
+        copy.wait()
+    for sender in range(sizes.experts):
+        partner = pick[1] ^ sender
+        received[sender] = here[(partner % count) * PLANES + partner // count]
     back_out[...] = through_down_back(sizes, received, down)
 
 
@@ -416,12 +448,23 @@
         result[:, span(sizes, block)] = total.astype(BF16)
 
 
+TOOK = {
+    "weights": 7, "send_tokens": 3, "send_cotangent": 4, "expert_forward": 6, "hidden_back": 5,
+    "combine_send": 4, "expert_turn": 6, "norm_back_send": 5, "expert_backward": 6,
+    "down_grad": 11, "norm_back_last": 6, "assemble": 1, "regroup": 2, "far_plane": 1,
+}
+FLOPS_PER_MICROSECOND = 1_150_000_000
+
+
 VMEM = pl.BlockSpec(memory_space=pltpu.VMEM)
 SMEM = pl.BlockSpec(memory_space=pltpu.SMEM)
 HBM = pl.BlockSpec(memory_space=pltpu.HBM)
 
 
-def call(kernel, name, operands, outs, scratch=(), specs=None, out_specs=None, aliases=None):
+def call(
+    kernel, name, operands, outs, scratch=(), specs=None, out_specs=None, aliases=None,
+    vmem=VMEM_BYTES,
+):
     return pl.pallas_call(
         kernel,
         name=name,
@@ -432,12 +475,22 @@
         ],
         scratch_shapes=list(scratch),
         input_output_aliases=aliases or {},
-        compiler_params=pltpu.CompilerParams(vmem_limit_bytes=VMEM_BYTES),
+        cost_estimate=pl.CostEstimate(
+            flops=TOOK[name] * FLOPS_PER_MICROSECOND, transcendentals=0, bytes_accessed=0
+        ),
+        compiler_params=pltpu.CompilerParams(vmem_limit_bytes=vmem),
     )(*operands)
 
 
 def exchange(message):
     return lax.all_to_all(message, "expert", split_axis=0, concat_axis=0, tiled=True)
+
+
+def to_partner(piece, number):
+    if number == 0:
+        return piece
+    count = lax.axis_size("expert")
+    return lax.ppermute(piece, "expert", [(source, source ^ number) for source in range(count)])
 
 
 def shards(tokens, cotangent, expert_ids, gate_prob, up_weight, down_weight):
@@ -446,7 +499,7 @@
     hidden = up_weight.shape[3]
     sizes = Sizes(lax.axis_size("expert"), rows, features, hidden)
     swap = [(0, 1), (1, 0)]
-    pick = jnp.reshape(core, (1,)).astype(jnp.int32)
+    pick = jnp.stack([core, lax.axis_index("expert")]).astype(jnp.int32)
 
     tables = jnp.concatenate([expert_ids[0].astype(F32), gate_prob[0]], axis=-1).swapaxes(1, 2)
     mine = lax.dynamic_index_in_dim(tables, core, 0, keepdims=False)
@@ -477,39 +530,52 @@
         weights_kernel, "weights", [pick, up, down, up_other, down_other],
         [up_shape, down_shape] * 2, [done(4)], [SMEM] + [HBM] * 4, [HBM] * 4,
     )
-    (out_0,) = call(
-        kernel(first_kernel), "send_tokens", [pick, tokens, across_0], [message],
-        [rows_scratch, done(1)], [SMEM, HBM, VMEM],
-    )
+    out_0, clip = call(
+        kernel(first_kernel), "send_tokens", [pick, tokens, across_0], [message, home_rows],
+        [done(1)], [SMEM, HBM, VMEM],
+    )
+    across_1_late, _, _ = lax.optimization_barrier((across_1, out_0, up_1))
     in_0 = exchange(out_0)
-    (grad_out_1,) = call(
-        kernel(cotangent_kernel), "send_cotangent", [pick, cotangent, across_1], [message],
-        [rows_scratch, done(1)], [SMEM, HBM, VMEM],
-    )
-    grad_out_1, in_0 = lax.optimization_barrier((grad_out_1, in_0))
-    grad_in_1 = exchange(grad_out_1)
+    plane = ((sizes.in_plane,) + sizes.message[1:], BF16)
+    place = ((PLANES,) + sizes.message[1:], BF16)
+    *planes, clip_grad = call(
+        kernel(cotangent_kernel), "send_cotangent", [pick, cotangent, across_1_late],
+        [plane] * PLANES + [home_rows], [done(1)], [SMEM, HBM, VMEM],
+    )
+    last = PLANES - 1
+    near = [to_partner(planes[number], number * sizes.in_plane) for number in range(last)]
     hidden_0, activated_0, answer_0 = call(
         kernel(forward_kernel), "expert_forward", [in_0, up_0, down_0],
         [wide_hidden, activated, message],
     )
-    answer_0, grad_in_1 = lax.optimization_barrier((answer_0, grad_in_1))
+    *near, answer_0 = lax.optimization_barrier((*near, answer_0))
     returned_0 = exchange(answer_0)
-    (back_1,) = call(kernel(hidden_back_kernel), "hidden_back", [grad_in_1, down_1], [wide_hidden])
-    returned_0, back_1 = lax.optimization_barrier((returned_0, back_1))
+    places = call(
+        kernel(regroup_kernel), "regroup", near + [planes[last]], [place] * sizes.in_plane
+    )
+    places = [to_partner(piece, number) for number, piece in enumerate(places)]
+    (far,) = call(far_kernel, "far_plane", places, [plane])
+    _, returned_0 = lax.optimization_barrier((far, returned_0))
+    far = to_partner(far, last * sizes.in_plane)
     carried_1, out_1 = call(
-        kernel(middle_kernel), "combine_send", [pick, tokens, returned_0, table_0, across_1],
-        [home_rows, message], [rows_scratch, done(1)], [SMEM, HBM, VMEM, VMEM, VMEM],
-    )
+        kernel(middle_kernel), "combine_send", [clip, returned_0, table_0, across_1],
+        [home_rows, message],
+    )
+    far, out_1 = lax.optimization_barrier((far, out_1))
     in_1 = exchange(out_1)
+    back_1, grad_in_1 = call(
+        kernel(hidden_back_kernel), "hidden_back", [pick, down_1] + places + [far],
+        [wide_hidden, message], [pltpu.VMEM(*message), done(2 * sizes.in_plane)],
+        [SMEM, VMEM] + [HBM] * (sizes.in_plane + 1),
+    )
     activated_1, picks_1 = call(
         kernel(turn_expert_kernel), "expert_turn", [in_1, back_1, up_1], [activated, message]
     )
     back_home_1 = exchange(picks_1)
     grad_1, grad_out_0 = call(
         kernel(turn_kernel), "norm_back_send",
-        [pick, carried_1, cotangent, back_home_1, table_1, across_0],
-        [home_rows, message], [upstream_scratch, rows_scratch, rows_scratch, done(2)],
-        [SMEM, HBM, HBM, VMEM, VMEM, VMEM],
+        [carried_1, clip_grad, back_home_1, table_1, across_0],
+        [home_rows, message], [upstream_scratch],
     )
     grad_in_0 = exchange(grad_out_0)
     (picks_0,) = call(
@@ -532,9 +598,9 @@
     down_grad, far_1, back_home_0 = lax.optimization_barrier((down_grad, far_1, back_home_0))
     held = (tokens.shape, BF16)
     grad_0, input_grad = call(
-        kernel(last_kernel), "norm_back_last", [pick, tokens, grad_1, back_home_0, table_0, far_1],
-        [home_rows, held], [upstream_scratch, rows_scratch, rows_scratch, done(4)],
-        [SMEM, HBM, HBM, VMEM, VMEM, HBM], [VMEM, HBM],
+        kernel(last_kernel), "norm_back_last", [pick, clip, grad_1, back_home_0, table_0, far_1],
+        [home_rows, held], [upstream_scratch] + [rows_scratch] * 3 + [done(4)],
+        [SMEM, HBM, HBM, VMEM, VMEM, HBM], [VMEM, HBM], vmem=WHOLE_VMEM_BYTES,
     )
     far_0 = lax.ppermute(grad_0, "pipe", to_first)
     (input_grad,) = call(

time: 442 us -> 431 us (0.975)
  blocking collectives: 164 us -> 109 us
  local copies, waits for them, and re-layouts: 34.4 us -> 50.4 us
  waiting for transfers between devices: 140 us -> 152 us
  starting transfers between devices: 39 us -> 46.9 us
  Pallas kernels: 60.6 us -> 68.3 us
    all_to_all x3 -> x2, blocking collectives: 164 us -> 109 us  [exchange(): lax.all_to_all(message, 'expert', split_axis=0, concat_axis=0, tiled=True)]
    ppermute x0 -> x6, waiting for transfers between devices: none -> 47.7 us  [to_partner(): lax.ppermute(piece, 'expert', [(source, source ^ number) for source in ra...]
    all_to_all x4, waiting for transfers between devices: 134 us -> 94.5 us  [exchange(): lax.all_to_all(message, 'expert', split_axis=0, concat_axis=0, tiled=True)]
    unnamed x58 -> x92, local copies, waits for them, and re-layouts: 34.3 us -> 50.2 us
    ppermute x0 -> x6, starting transfers between devices: none -> 9.41 us  [to_partner(): lax.ppermute(piece, 'expert', [(source, source ^ number) for source in ra...]
    pallas_call x12 -> x14, Pallas kernels: 60.6 us -> 68.3 us  [call(): pl.pallas_call(kernel, name=name, in_specs=specs or [VMEM] * len(operands...]
    ppermute x1, waiting for transfers between devices: 0.01 us -> 5.24 us  [shards(): down_other = lax.ppermute(down, 'pipe', swap)]
  transfers between devices with their start and end apart: 13 -> 19, of which waited for: 7 -> 14; matrix products, arithmetic and copies ran while one was open for 0% -> 0% of each run, Pallas kernels for 7% -> 10%
where the time goes in v3:
time: 431 us; the launch traced here: 430 us
  waiting for transfers between devices  152 us (35%)
  blocking collectives  109 us (25%)
  Pallas kernels  68.3 us (16%)
  local copies, waits for them, and re-layouts  50.4 us (12%)
  starting transfers between devices  46.9 us (11%)
    all_to_all x2, blocking collectives, exchange(): lax.all_to_all(message, 'expert', split_axis=0, concat_axis=0, tiled=True)  109 us
    all_to_all x4, waiting for transfers between devices, exchange(): lax.all_to_all(message, 'expert', split_axis=0, concat_axis=0, tiled=True)  94.5 us
    pallas_call x14, Pallas kernels, call(): pl.pallas_call(kernel, name=name, in_specs=specs or [VMEM] * len(operands...  68.3 us
    unnamed x92, local copies, waits for them, and re-layouts  50.2 us
    ppermute x6, waiting for transfers between devices, to_partner(): lax.ppermute(piece, 'expert', [(source, source ^ number) for source in ra...  47.7 us
    all_to_all x4, starting transfers between devices, exchange(): lax.all_to_all(message, 'expert', split_axis=0, concat_axis=0, tiled=True)  23.4 us
    ppermute x6, starting transfers between devices, to_partner(): lax.ppermute(piece, 'expert', [(source, source ^ number) for source in ra...  9.41 us
  transfers between devices with their start and end apart: 19, of which 14 were waited for; matrix products, arithmetic and copies ran while one was open for 0% of the time, Pallas kernels for 10%

profile of v3, /device:TPU:13, one launch (start us, length us, event | category | flops | bytes accessed | tf_op | source)
XLA Modules:
  0.0 429.5 jit_solution(17528555823820079996)
XLA Ops:
  11.4 6.6 %all-to-all-start = ((bf16[16,136,512]{2,1,0:T(8,128)(2,1)}), bf16[16,136,512]{2,1,0:T(8,128)(2,1)S(1)}, u32[]{:S(2)}, u32[]{:S(2)}) async-start(bf16[16,136,512]{2,1,0:T(8,128)(2,1)} %copy-done), calls=%async_computation | async-start | bytes 4456448 | tf_op jit(solution)/shard_map/all_to_all | solution.py:486
  18.0 5.2 %collective-permute-done.2.down_other = bf16[768,4096]{1,0:T(8,128)(2,1)} collective-permute-done((bf16[768,4096]{1,0:T(8,128)(2,1)}, bf16[768,4096]{1,0:T(8,128)(2,1)}, u32[]{:S(2)}, u32[]{:S(2)}) %collective-permute-start.2) | collective-permute-done | bytes 6291488 | tf_op jit(solution)/shard_map/ppermute | solution.py:513
  26.0 7.1 %weights.1 = (bf16[4096,768]{1,0:T(8,128)(2,1)S(1)}, bf16[768,4096]{1,0:T(8,128)(2,1)S(1)}, bf16[4096,768]{1,0:T(8,128)(2,1)S(1)}, bf16[768,4096]{1,0:T(8,128)(2,1)S(1)}) custom-call(s32[2]{0:T(128)S(1)} %pad_add_fusion.pick, bf16[4096,768]{1,0:T(8,128)(2,1)S(1)} %bitcast.23, bf16[768,4096]{1,0:T(8,128)(2,1)} %bitcast.32, ...), custom_call_target="tpu_custom_call" | custom-call | flops 8049999872 | tf_op jit(solution)/shard_map/weights/pallas_call | solution.py:468
  45.4 4.6 %send_cotangent.1 = (bf16[4,136,512]{2,1,0:T(8,128)(2,1)S(1)}, bf16[4,136,512]{2,1,0:T(8,128)(2,1)}, bf16[4,136,512]{2,1,0:T(8,128)(2,1)}, bf16[4,136,512]{2,1,0:T(8,128)(2,1)S(1)}, bf16[112,4096]{1,0:T(8,128)(2,1)S(1)}) custom-call(s32[2]{0:T(128)S(1)} %pad_add_fusion.pick, bf16[2,112,4096]{2,1,0:T(8,128)(2,1)S(1)} %copy-done.9, f32[4,112]{1,0:T(4,128)S(1)} %copy.18.across), custom_call_target="tpu_custom_call" | custom-call | flops 4600000000 | tf_op jit(solution)/shard_map/send_cotangent/pallas_call | solution.py:468
  55.0 13.4 %all-to-all-done.received = bf16[16,136,512]{2,1,0:T(8,128)(2,1)S(1)} async-done(((bf16[16,136,512]{2,1,0:T(8,128)(2,1)}), bf16[16,136,512]{2,1,0:T(8,128)(2,1)S(1)}, u32[]{:S(2)}, u32[]{:S(2)}) %all-to-all-start) | async-done | bytes 2228256 | tf_op jit(solution)/shard_map/all_to_all | solution.py:486
  74.1 7.1 %expert_forward.1 = (f32[272,768]{1,0:T(8,128)S(1)}, bf16[272,768]{1,0:T(8,128)(2,1)S(1)}, bf16[16,136,512]{2,1,0:T(8,128)(2,1)}) custom-call(bf16[16,136,512]{2,1,0:T(8,128)(2,1)S(1)} %all-to-all-done.received, bf16[4096,768]{1,0:T(8,128)(2,1)S(1)} %copy-done.18, bf16[768,4096]{1,0:T(8,128)(2,1)S(1)} %copy-done.20), custom_call_target="tpu_custom_call" | custom-call | flops 6899999744 | tf_op jit(solution)/shard_map/expert_forward/pallas_call | solution.py:468
  82.9 7.8 %collective-permute-done.4.refs_2_ = bf16[4,136,512]{2,1,0:T(8,128)(2,1)S(1)} collective-permute-done((bf16[4,136,512]{2,1,0:T(8,128)(2,1)}, bf16[4,136,512]{2,1,0:T(8,128)(2,1)S(1)}, u32[]{:S(2)}, u32[]{:S(2)}) %collective-permute-start.4) | collective-permute-done | bytes 557088 | tf_op jit(solution)/shard_map/ppermute | solution.py:493
  90.7 7.1 %all-to-all-start.1 = ((bf16[16,136,512]{2,1,0:T(8,128)(2,1)}), bf16[16,136,512]{2,1,0:T(8,128)(2,1)S(1)}, u32[]{:S(2)}, u32[]{:S(2)}) async-start(bf16[16,136,512]{2,1,0:T(8,128)(2,1)} %get-tuple-element.63), calls=%async_computation.1 | async-start | bytes 4456448 | tf_op jit(solution)/shard_map/all_to_all | solution.py:486
  102.7 12.4 %collective-permute-done.5.refs_1_ = bf16[4,136,512]{2,1,0:T(8,128)(2,1)S(1)} collective-permute-done((bf16[4,136,512]{2,1,0:T(8,128)(2,1)S(1)}, bf16[4,136,512]{2,1,0:T(8,128)(2,1)S(1)}, u32[]{:S(2)}, u32[]{:S(2)}) %collective-permute-start.5) | collective-permute-done | bytes 557088 | tf_op jit(solution)/shard_map/ppermute | solution.py:493
  115.1 12.4 %collective-permute-done.6.refs_2_ = bf16[4,136,512]{2,1,0:T(8,128)(2,1)S(1)} collective-permute-done((bf16[4,136,512]{2,1,0:T(8,128)(2,1)S(1)}, bf16[4,136,512]{2,1,0:T(8,128)(2,1)S(1)}, u32[]{:S(2)}, u32[]{:S(2)}) %collective-permute-start.6) | collective-permute-done | bytes 557088 | tf_op jit(solution)/shard_map/ppermute | solution.py:493
  127.5 11.3 %collective-permute-done.7.refs_3_ = bf16[4,136,512]{2,1,0:T(8,128)(2,1)S(1)} collective-permute-done((bf16[4,136,512]{2,1,0:T(8,128)(2,1)S(1)}, bf16[4,136,512]{2,1,0:T(8,128)(2,1)S(1)}, u32[]{:S(2)}, u32[]{:S(2)}) %collective-permute-start.7) | collective-permute-done | bytes 557088 | tf_op jit(solution)/shard_map/ppermute | solution.py:493
  144.1 17.7 %all-to-all-done.1.answer = bf16[16,136,512]{2,1,0:T(8,128)(2,1)S(1)} async-done(((bf16[16,136,512]{2,1,0:T(8,128)(2,1)}), bf16[16,136,512]{2,1,0:T(8,128)(2,1)S(1)}, u32[]{:S(2)}, u32[]{:S(2)}) %all-to-all-start.1) | async-done | bytes 2228256 | tf_op jit(solution)/shard_map/all_to_all | solution.py:486
  182.3 5.1 %hidden_back.1 = (f32[272,768]{1,0:T(8,128)S(1)}, bf16[16,136,512]{2,1,0:T(8,128)(2,1)S(1)}) custom-call(s32[2]{0:T(128)S(1)} %pad_add_fusion.pick, bf16[768,4096]{1,0:T(8,128)(2,1)S(1)} %copy-done.24, bf16[4,136,512]{2,1,0:T(8,128)(2,1)S(1)} %copy-done.26, bf16[4,136,512]{2,1,0:T(8,128)(2,1)S(1)} %collective-permute-done.5.refs_1_, ...), custom_call_target="tpu_custom_call" | custom-call | flops 5750000128 | tf_op jit(solution)/shard_map/hidden_back/pallas_call | solution.py:468
  189.8 38.6 %all-to-all-done.2.received = bf16[16,136,512]{2,1,0:T(8,128)(2,1)S(1)} async-done(((bf16[16,136,512]{2,1,0:T(8,128)(2,1)}), bf16[16,136,512]{2,1,0:T(8,128)(2,1)S(1)}, u32[]{:S(2)}, u32[]{:S(2)}) %all-to-all-start.2) | async-done | bytes 2228256 | tf_op jit(solution)/shard_map/all_to_all | solution.py:486
  232.3 6.0 %expert_turn.1 = (bf16[272,768]{1,0:T(8,128)(2,1)S(1)}, bf16[16,136,512]{2,1,0:T(8,128)(2,1)S(1)}) custom-call(bf16[16,136,512]{2,1,0:T(8,128)(2,1)S(1)} %all-to-all-done.2.received, f32[272,768]{1,0:T(8,128)S(1)} %copy-done.36, bf16[4096,768]{1,0:T(8,128)(2,1)S(1)} %copy-done.22), custom_call_target="tpu_custom_call" | custom-call | flops 6899999744 | tf_op jit(solution)/shard_map/expert_turn/pallas_call | solution.py:468
  239.1 54.3 %all_to_all.30.answer = bf16[16,136,512]{2,1,0:T(8,128)(2,1)S(1)} all-to-all(bf16[16,136,512]{2,1,0:T(8,128)(2,1)S(1)} %get-tuple-element.72), channel_id=1, replica_groups=mesh['pipe'=2,'expert'=16] {'expert'}, dimensions={0} | all-to-all | bytes 4456448 | tf_op jit(solution)/shard_map/all_to_all | solution.py:486
  293.4 4.6 %norm_back_send.1 = (bf16[112,4096]{1,0:T(8,128)(2,1)S(1)}, bf16[16,136,512]{2,1,0:T(8,128)(2,1)S(1)}) custom-call(bf16[112,4096]{1,0:T(8,128)(2,1)S(1)} %copy-done.38, bf16[112,4096]{1,0:T(8,128)(2,1)S(1)} %copy-done.40, bf16[16,136,512]{2,1,0:T(8,128)(2,1)S(1)} %all_to_all.30.answer, f32[112,4]{1,0:T(8,128)S(1)} %bitcast.19, f32[4,112]{1,0:T(4,128)S(1)} %copy.17.across), custom_call_target="tpu_custom_call" | custom-call | flops 5750000128 | tf_op jit(solution)/shard_map/norm_back_send/pallas_call | solution.py:468
  298.1 55.1 %all_to_all.31.refs_1_.received = bf16[16,136,512]{2,1,0:T(8,128)(2,1)S(1)} all-to-all(bf16[16,136,512]{2,1,0:T(8,128)(2,1)S(1)} %get-tuple-element.75), channel_id=1, replica_groups=mesh['pipe'=2,'expert'=16] {'expert'}, dimensions={0} | all-to-all | bytes 4456448 | tf_op jit(solution)/shard_map/all_to_all | solution.py:486
  353.2 6.9 %expert_backward.1 = bf16[16,136,512]{2,1,0:T(8,128)(2,1)} custom-call(bf16[16,136,512]{2,1,0:T(8,128)(2,1)S(1)} %all_to_all.31.refs_1_.received, f32[272,768]{1,0:T(8,128)S(1)} %copy-done.28, bf16[4096,768]{1,0:T(8,128)(2,1)S(1)} %bitcast.25, bf16[768,4096]{1,0:T(8,128)(2,1)S(1)} %bitcast.27), custom_call_target="tpu_custom_call" | custom-call | flops 6899999744 | tf_op jit(solution)/shard_map/expert_backward/pallas_call | solution.py:468
  360.2 5.5 %all-to-all-start.5 = ((bf16[16,136,512]{2,1,0:T(8,128)(2,1)}), bf16[16,136,512]{2,1,0:T(8,128)(2,1)}, u32[]{:S(2)}, u32[]{:S(2)}) async-start(bf16[16,136,512]{2,1,0:T(8,128)(2,1)} %expert_backward.1), calls=%async_computation.5 | async-start | bytes 4456448 | tf_op jit(solution)/shard_map/all_to_all | solution.py:486
  366.9 4.5 %collective-permute-start.10 = (bf16[16,136,512]{2,1,0:T(8,128)(2,1)S(1)}, bf16[16,136,512]{2,1,0:T(8,128)(2,1)S(1)}, u32[]{:S(2)}, u32[]{:S(2)}) collective-permute-start(bf16[16,136,512]{2,1,0:T(8,128)(2,1)S(1)} %all_to_all.31.refs_1_.received), channel_id=1, source_target_pairs={{16,0},{17,1},{18,2},{19,3},{20,4},{21,5},{22,6},{23,7},{24,8},{25... | collective-permute-start | bytes 6684680 | tf_op jit(solution)/shard_map/ppermute | solution.py:591
  380.3 11.6 %down_grad.1 = bf16[768,4096]{1,0:T(8,128)(2,1)} custom-call(s32[2]{0:T(128)S(1)} %pad_add_fusion.pick, bf16[272,768]{1,0:T(8,128)(2,1)S(1)} %copy-done.14, bf16[16,136,512]{2,1,0:T(8,128)(2,1)S(1)} %all_to_all.31.refs_1_.received, bf16[272,768]{1,0:T(8,128)(2,1)S(1)} %collective-permute-done.9.refs_2_, ...), custom_call_target="tpu_custom_call" | custom-call | flops 12650000384 | tf_op jit(solution)/shard_map/down_grad/pallas_call | solution.py:468
  392.0 24.8 %all-to-all-done.5.answer = bf16[16,136,512]{2,1,0:T(8,128)(2,1)} async-done(((bf16[16,136,512]{2,1,0:T(8,128)(2,1)}), bf16[16,136,512]{2,1,0:T(8,128)(2,1)}, u32[]{:S(2)}, u32[]{:S(2)}) %all-to-all-start.5) | async-done | bytes 2228256 | tf_op jit(solution)/shard_map/all_to_all | solution.py:486
  416.7 6.6 %norm_back_last.1 = (bf16[112,4096]{1,0:T(8,128)(2,1)}, bf16[2,112,4096]{2,1,0:T(8,128)(2,1)}) custom-call(s32[2]{0:T(128)} %copy-done.3, bf16[112,4096]{1,0:T(8,128)(2,1)} %copy-done.33, bf16[112,4096]{1,0:T(8,128)(2,1)} %copy-done.10, bf16[16,136,512]{2,1,0:T(8,128)(2,1)} %all-to-all-done.5.answer, f32[112,4]{1,0:T(8,128)} %bitcast.21, ...), custom_call_target="tpu_custom_call" | custom-call | flops 6899999744 | tf_op jit(solution)/shard_map/norm_back_last/pallas_call | solution.py:468
  (131 shorter events, 91.9 us)
Async XLA Ops:
  2.1 1.6 collective-permute-start
  3.8 14.3 %collective-permute-start.1 = (bf16[4096,768]{1,0:T(8,128)(2,1)}, bf16[4096,768]{1,0:T(8,128)(2,1)}, u32[]{:S(2)}, u32[]{:S(2)}) collective-permute-start(bf16[4096,768]{1,0:T(8,128)(2,1)} %bitcast.22), channel_id=1, source_target_pairs={{0,16},{16,0},{1,17},{17,1},{2,18},{18,2},{3,19},{19,3},{4,20},{20... | collective-permute-start | bytes 18874376 | tf_op jit(solution)/shard_map/ppermute | solution.py:512
  4.1 19.1 %collective-permute-start.2 = (bf16[768,4096]{1,0:T(8,128)(2,1)}, bf16[768,4096]{1,0:T(8,128)(2,1)}, u32[]{:S(2)}, u32[]{:S(2)}) collective-permute-start(bf16[768,4096]{1,0:T(8,128)(2,1)} %bitcast.31), channel_id=1, source_target_pairs={{0,16},{16,0},{1,17},{17,1},{2,18},{18,2},{3,19},{19,3},{4,20},{20... | collective-permute-start | bytes 18874376 | tf_op jit(solution)/shard_map/ppermute | solution.py:513
  4.5 372.2 %copy-start.3 = (s32[2]{0:T(128)}, s32[2]{0:T(128)S(1)}, u32[]{:S(2)}) copy-start(s32[2]{0:T(128)S(1)} %pad_add_fusion.pick) | copy-start | bytes 28
  4.5 157.3 %copy-start.2 = (f32[4,112]{0,1:T(8,128)}, f32[4,112]{0,1:T(8,128)S(1)}, u32[]{:S(2)}) copy-start(f32[4,112]{0,1:T(8,128)S(1)} %get-tuple-element.85) | copy-start | bytes 5380
  11.4 57.1 %all-to-all-start = ((bf16[16,136,512]{2,1,0:T(8,128)(2,1)}), bf16[16,136,512]{2,1,0:T(8,128)(2,1)S(1)}, u32[]{:S(2)}, u32[]{:S(2)}) async-start(bf16[16,136,512]{2,1,0:T(8,128)(2,1)} %copy-done), calls=%async_computation | async-start | bytes 4456448 | tf_op jit(solution)/shard_map/all_to_all | solution.py:486
  52.6 30.4 %collective-permute-start.3 = (bf16[4,136,512]{2,1,0:T(8,128)(2,1)}, bf16[4,136,512]{2,1,0:T(8,128)(2,1)S(1)}, u32[]{:S(2)}, u32[]{:S(2)}) collective-permute-start(bf16[4,136,512]{2,1,0:T(8,128)(2,1)} %get-tuple-element.50), channel_id=1, source_target_pairs={{0,4},{1,5},{2,6},{3,7},{4,0},{5,1},{6,2},{7,3},{8,12},{9,13},{10,... | collective-permute-start | bytes 1671176 | tf_op jit(solution)/shard_map/ppermute | solution.py:493
  52.7 38.0 %collective-permute-start.4 = (bf16[4,136,512]{2,1,0:T(8,128)(2,1)}, bf16[4,136,512]{2,1,0:T(8,128)(2,1)S(1)}, u32[]{:S(2)}, u32[]{:S(2)}) collective-permute-start(bf16[4,136,512]{2,1,0:T(8,128)(2,1)} %get-tuple-element.51), channel_id=1, source_target_pairs={{0,8},{1,9},{2,10},{3,11},{4,12},{5,13},{6,14},{7,15},{8,0},{9,1},... | collective-permute-start | bytes 1671176 | tf_op jit(solution)/shard_map/ppermute | solution.py:493
  90.7 71.1 %all-to-all-start.1 = ((bf16[16,136,512]{2,1,0:T(8,128)(2,1)}), bf16[16,136,512]{2,1,0:T(8,128)(2,1)S(1)}, u32[]{:S(2)}, u32[]{:S(2)}) async-start(bf16[16,136,512]{2,1,0:T(8,128)(2,1)} %get-tuple-element.63), calls=%async_computation.1 | async-start | bytes 4456448 | tf_op jit(solution)/shard_map/all_to_all | solution.py:486
  100.0 15.1 %collective-permute-start.5 = (bf16[4,136,512]{2,1,0:T(8,128)(2,1)S(1)}, bf16[4,136,512]{2,1,0:T(8,128)(2,1)S(1)}, u32[]{:S(2)}, u32[]{:S(2)}) collective-permute-start(bf16[4,136,512]{2,1,0:T(8,128)(2,1)S(1)} %get-tuple-element.60), channel_id=1, source_target_pairs={{0,1},{1,0},{2,3},{3,2},{4,5},{5,4},{6,7},{7,6},{8,9},{9,8},{10,11... | collective-permute-start | bytes 1671176 | tf_op jit(solution)/shard_map/ppermute | solution.py:493
  101.3 26.2 %collective-permute-start.6 = (bf16[4,136,512]{2,1,0:T(8,128)(2,1)S(1)}, bf16[4,136,512]{2,1,0:T(8,128)(2,1)S(1)}, u32[]{:S(2)}, u32[]{:S(2)}) collective-permute-start(bf16[4,136,512]{2,1,0:T(8,128)(2,1)S(1)} %get-tuple-element.61), channel_id=1, source_target_pairs={{0,2},{1,3},{2,0},{3,1},{4,6},{5,7},{6,4},{7,5},{8,10},{9,11},{10,... | collective-permute-start | bytes 1671176 | tf_op jit(solution)/shard_map/ppermute | solution.py:493
  101.6 37.3 %collective-permute-start.7 = (bf16[4,136,512]{2,1,0:T(8,128)(2,1)S(1)}, bf16[4,136,512]{2,1,0:T(8,128)(2,1)S(1)}, u32[]{:S(2)}, u32[]{:S(2)}) collective-permute-start(bf16[4,136,512]{2,1,0:T(8,128)(2,1)S(1)} %get-tuple-element.62), channel_id=1, source_target_pairs={{0,3},{1,2},{2,1},{3,0},{4,7},{5,6},{6,5},{7,4},{8,11},{9,10},{10,... | collective-permute-start | bytes 1671176 | tf_op jit(solution)/shard_map/ppermute | solution.py:493
  139.8 33.4 %collective-permute-start.8 = (bf16[4,136,512]{2,1,0:T(8,128)(2,1)}, bf16[4,136,512]{2,1,0:T(8,128)(2,1)}, u32[]{:S(2)}, u32[]{:S(2)}) collective-permute-start(bf16[4,136,512]{2,1,0:T(8,128)(2,1)} %far_plane.1), channel_id=1, source_target_pairs={{0,12},{1,13},{2,14},{3,15},{4,8},{5,9},{6,10},{7,11},{8,4},{9,5},... | collective-permute-start | bytes 1671176 | tf_op jit(solution)/shard_map/ppermute | solution.py:493
  173.2 55.2 %all-to-all-start.2 = ((bf16[16,136,512]{2,1,0:T(8,128)(2,1)}), bf16[16,136,512]{2,1,0:T(8,128)(2,1)S(1)}, u32[]{:S(2)}, u32[]{:S(2)}) async-start(bf16[16,136,512]{2,1,0:T(8,128)(2,1)} %copy-done.1), calls=%async_computation.2 | async-start | bytes 4456448 | tf_op jit(solution)/shard_map/all_to_all | solution.py:486
  239.1 114.1 %slice-start = ((s8[6291456]{0:T(1024)(128)(4,1)}), s8[4194304]{0:T(1024)(128)(4,1)S(1)}, s32[]{:S(2)}) async-start(s8[6291456]{0:T(1024)(128)(4,1)} %bitcast.24), calls=%async_computation.6 | async-start | bytes 8388608
  239.1 114.1 %slice-start.2 = ((s8[6291456]{0:T(1024)(128)(4,1)}), s8[4194304]{0:T(1024)(128)(4,1)S(1)}, s32[]{:S(2)}) async-start(s8[6291456]{0:T(1024)(128)(4,1)} %bitcast.26), calls=%async_computation.8 | async-start | bytes 8388608
  298.1 76.0 %copy-start.10 = (bf16[112,4096]{1,0:T(8,128)(2,1)}, bf16[112,4096]{1,0:T(8,128)(2,1)S(1)}, u32[]{:S(2)}) copy-start(bf16[112,4096]{1,0:T(8,128)(2,1)S(1)} %get-tuple-element.73.incoming) | copy-start | bytes 2752516
  360.2 56.6 %all-to-all-start.5 = ((bf16[16,136,512]{2,1,0:T(8,128)(2,1)}), bf16[16,136,512]{2,1,0:T(8,128)(2,1)}, u32[]{:S(2)}, u32[]{:S(2)}) async-start(bf16[16,136,512]{2,1,0:T(8,128)(2,1)} %expert_backward.1), calls=%async_computation.5 | async-start | bytes 4456448 | tf_op jit(solution)/shard_map/all_to_all | solution.py:486
  365.7 10.4 %collective-permute-start.12 = (bf16[16,136,512]{2,1,0:T(8,128)(2,1)}, bf16[16,136,512]{2,1,0:T(8,128)(2,1)S(1)}, u32[]{:S(2)}, u32[]{:S(2)}) collective-permute-start(bf16[16,136,512]{2,1,0:T(8,128)(2,1)} %copy-done.6), channel_id=1, source_target_pairs={{0,16},{1,17},{2,18},{3,19},{4,20},{5,21},{6,22},{7,23},{8,24},{9,... | collective-permute-start | bytes 6684680 | tf_op jit(solution)/shard_map/ppermute | solution.py:591
  366.9 9.7 %collective-permute-start.10 = (bf16[16,136,512]{2,1,0:T(8,128)(2,1)S(1)}, bf16[16,136,512]{2,1,0:T(8,128)(2,1)S(1)}, u32[]{:S(2)}, u32[]{:S(2)}) collective-permute-start(bf16[16,136,512]{2,1,0:T(8,128)(2,1)S(1)} %all_to_all.31.refs_1_.received), channel_id=1, source_target_pairs={{16,0},{17,1},{18,2},{19,3},{20,4},{21,5},{22,6},{23,7},{24,8},{25... | collective-permute-start | bytes 6684680 | tf_op jit(solution)/shard_map/ppermute | solution.py:591
  371.5 4.6 %collective-permute-start.9 = (bf16[272,768]{1,0:T(8,128)(2,1)}, bf16[272,768]{1,0:T(8,128)(2,1)S(1)}, u32[]{:S(2)}, u32[]{:S(2)}) collective-permute-start(bf16[272,768]{1,0:T(8,128)(2,1)} %copy-done.13), channel_id=1, source_target_pairs={{16,0},{17,1},{18,2},{19,3},{20,4},{21,5},{22,6},{23,7},{24,8},{25... | collective-permute-start | bytes 1253384 | tf_op jit(solution)/shard_map/ppermute | solution.py:591
  372.8 3.9 collective-permute-start.11
  374.1 17.9 %collective-permute-start.13 = (bf16[112,4096]{1,0:T(8,128)(2,1)S(1)}, bf16[112,4096]{1,0:T(8,128)(2,1)}, u32[]{:S(2)}, u32[]{:S(2)}) collective-permute-start(bf16[112,4096]{1,0:T(8,128)(2,1)S(1)} %get-tuple-element.73.incoming), channel_id=1, source_target_pairs={{0,16},{1,17},{2,18},{3,19},{4,20},{5,21},{6,22},{7,23},{8,24},{9,... | collective-permute-start | bytes 2752520 | tf_op jit(solution)/shard_map/ppermute | solution.py:597
  423.4 5.4 %collective-permute-start.14 = (bf16[112,4096]{1,0:T(8,128)(2,1)}, bf16[112,4096]{1,0:T(8,128)(2,1)S(1)}, u32[]{:S(2)}, u32[]{:S(2)}) collective-permute-start(bf16[112,4096]{1,0:T(8,128)(2,1)} %get-tuple-element.81), channel_id=1, source_target_pairs={{16,0},{17,1},{18,2},{19,3},{20,4},{21,5},{22,6},{23,7},{24,8},{25... | collective-permute-start | bytes 2752520 | tf_op jit(solution)/shard_map/ppermute | solution.py:605
  (40 other events, 424.4 us)

commit v4 on v3

--- a/solution.py
+++ b/solution.py
@@ -31,6 +31,12 @@
         self.slots = experts * self.capacity
         self.message = (experts, FEATURE_BLOCKS * self.capacity, self.lanes)
         self.in_plane = experts // PLANES
+
+
+def bring(source, place, done):
+    copy = pltpu.make_async_copy(source, place, done)
+    copy.start()
+    return copy
 
 
 def iota(shape, axis):
@@ -214,20 +220,7 @@
     return lax.rsqrt(total / sizes.features + EPSILON)
 
 
-def clip_copy(pick, clips, place, done):
-    copy = pltpu.make_async_copy(clips.at[pick[0]], place, done)
-    copy.start()
-    return copy
-
-
-def first_kernel(sizes, pick, clips, across, message, clip, done):
-    clip_copy(pick, clips, clip, done.at[0]).wait()
-    send_normed(sizes, clip, across, message)
-
-
-def cotangent_kernel(sizes, pick, clips, across, *refs):
-    planes, (clip, done) = refs[:PLANES], refs[PLANES:]
-    clip_copy(pick, clips, clip, done.at[0]).wait()
+def cotangent_kernel(sizes, pick, clip, across, *planes):
     send_weighted(sizes, clip, across, planes, pick[1])
 
 
@@ -277,9 +270,9 @@
 
 def norm_back(sizes, carried, incoming, answer, table, result, upstream, copies=()):
     select = tokens_by_slot(sizes, table[...], False)
+    for copy in copies[:2]:
+        copy.wait()
     rest = read_rest(sizes, answer)
-    for copy in copies[:1]:
-        copy.wait()
     inner = jnp.zeros((sizes.rows, 1), F32)
     squares = jnp.zeros((sizes.rows, 1), F32)
     for block in range(FEATURE_BLOCKS):
@@ -291,7 +284,7 @@
         squares = squares + jnp.sum(wide * wide, axis=1, keepdims=True)
     scale = lax.rsqrt(squares / sizes.features + EPSILON)
     pull = scale * scale * scale * (inner / sizes.features)
-    for copy in copies[1:]:
+    for copy in copies[2:]:
         copy.wait()
     for block in range(FEATURE_BLOCKS):
         here = span(sizes, block)
@@ -301,35 +294,34 @@
         ).astype(BF16)
 
 
+def hold_kernel(pick, grad, far, whole, done):
+    @pl.when(pick[0] != 0)
+    def _():
+        copies = [bring(far, whole.at[0], done.at[0]), bring(grad, whole.at[1], done.at[1])]
+        for copy in copies:
+            copy.wait()
+
+
+def assemble_kernel(pick, far, held, whole, done):
+    @pl.when(pick[0] == 0)
+    def _():
+        bring(far, whole.at[1], done.at[0]).wait()
+
+
 def last_kernel(
-    sizes, pick, before, incoming, answer, table, far,
-    result, whole, upstream, clip, grad, apart, done,
+    sizes, pick, before, incoming, answer_far, table, held, result, whole,
+    upstream, clip, grad, answer, done,
 ):
     copies = [
-        pltpu.make_async_copy(before, clip, done.at[0]),
-        pltpu.make_async_copy(incoming, grad, done.at[1]),
+        bring(answer_far, answer, done.at[0]),
+        bring(before, clip, done.at[1]),
+        bring(incoming, grad, done.at[2]),
     ]
-    for copy in copies:
-        copy.start()
-    far_copy = pltpu.make_async_copy(far, apart, done.at[2])
-    far_copy.start()
     norm_back(sizes, clip, grad, answer, table, result, upstream, copies)
-    far_copy.wait()
 
     @pl.when(pick[0] == 0)
     def _():
-        near_first = pltpu.make_async_copy(result, whole.at[0], done.at[2])
-        near_first.start()
-        near_first.wait()
-
-    @pl.when(pick[0] != 0)
-    def _():
-        far_first = pltpu.make_async_copy(apart, whole.at[0], done.at[2])
-        near_last = pltpu.make_async_copy(grad, whole.at[1], done.at[3])
-        far_first.start()
-        near_last.start()
-        far_first.wait()
-        near_last.wait()
+        bring(result, whole.at[0], done.at[3]).wait()
 
 
 def turn_kernel(sizes, carried, incoming, answer, table, across, result, message, upstream):
@@ -426,14 +418,6 @@
     choose(pick, 0, mine + others + others + mine, (up_0, down_0, up_1, down_1), done)
 
 
-def assemble_kernel(pick, far, mine, whole, done):
-    @pl.when(pick[0] == 0)
-    def _():
-        copy = pltpu.make_async_copy(far, whole.at[1], done.at[0])
-        copy.start()
-        copy.wait()
-
-
 def down_grad_kernel(sizes, pick, *refs):
     sources, result, here, done = refs[:8], refs[8], refs[9:13], refs[13]
     choose(pick, 0, sources, here, done)
@@ -451,7 +435,7 @@
 TOOK = {
     "weights": 7, "send_tokens": 3, "send_cotangent": 4, "expert_forward": 6, "hidden_back": 5,
     "combine_send": 4, "expert_turn": 6, "norm_back_send": 5, "expert_backward": 6,
-    "down_grad": 11, "norm_back_last": 6, "assemble": 1, "regroup": 2, "far_plane": 1,
+    "down_grad": 11, "norm_back_last": 6, "hold": 1, "assemble": 1, "regroup": 2, "far_plane": 1,
 }
 FLOPS_PER_MICROSECOND = 1_150_000_000
 
@@ -505,6 +489,8 @@
     mine = lax.dynamic_index_in_dim(tables, core, 0, keepdims=False)
     theirs = lax.dynamic_index_in_dim(tables, 1 - core, 0, keepdims=False)
     theirs = lax.ppermute(theirs, "pipe", swap)
+    clip = lax.dynamic_index_in_dim(tokens, core, 0, keepdims=False)
+    clip_grad = lax.dynamic_index_in_dim(cotangent, core, 0, keepdims=False)
     across_0 = jnp.where(core == 0, mine, theirs)
     across_1 = jnp.where(core == 0, theirs, mine)
     table_0, table_1 = across_0.T, across_1.T
@@ -530,17 +516,14 @@
         weights_kernel, "weights", [pick, up, down, up_other, down_other],
         [up_shape, down_shape] * 2, [done(4)], [SMEM] + [HBM] * 4, [HBM] * 4,
     )
-    out_0, clip = call(
-        kernel(first_kernel), "send_tokens", [pick, tokens, across_0], [message, home_rows],
-        [done(1)], [SMEM, HBM, VMEM],
-    )
+    (out_0,) = call(kernel(send_normed), "send_tokens", [clip, across_0], [message])
     across_1_late, _, _ = lax.optimization_barrier((across_1, out_0, up_1))
     in_0 = exchange(out_0)
     plane = ((sizes.in_plane,) + sizes.message[1:], BF16)
     place = ((PLANES,) + sizes.message[1:], BF16)
-    *planes, clip_grad = call(
-        kernel(cotangent_kernel), "send_cotangent", [pick, cotangent, across_1_late],
-        [plane] * PLANES + [home_rows], [done(1)], [SMEM, HBM, VMEM],
+    planes = call(
+        kernel(cotangent_kernel), "send_cotangent", [pick, clip_grad, across_1_late],
+        [plane] * PLANES, (), [SMEM, VMEM, VMEM],
     )
     last = PLANES - 1
     near = [to_partner(planes[number], number * sizes.in_plane) for number in range(last)]
@@ -595,16 +578,22 @@
         [SMEM] + [HBM] * 8,
     )
     far_1 = lax.ppermute(grad_1, "pipe", to_second)
-    down_grad, far_1, back_home_0 = lax.optimization_barrier((down_grad, far_1, back_home_0))
     held = (tokens.shape, BF16)
+    (input_grad,) = call(
+        hold_kernel, "hold", [pick, grad_1, far_1], [held], [done(2)], [SMEM, HBM, HBM], [HBM]
+    )
+    down_grad, input_grad, back_home_0 = lax.optimization_barrier(
+        (down_grad, input_grad, back_home_0)
+    )
     grad_0, input_grad = call(
-        kernel(last_kernel), "norm_back_last", [pick, clip, grad_1, back_home_0, table_0, far_1],
-        [home_rows, held], [upstream_scratch] + [rows_scratch] * 3 + [done(4)],
-        [SMEM, HBM, HBM, VMEM, VMEM, HBM], [VMEM, HBM], vmem=WHOLE_VMEM_BYTES,
+        kernel(last_kernel), "norm_back_last",
+        [pick, clip, grad_1, back_home_0, table_0, input_grad], [home_rows, held],
+        [upstream_scratch, rows_scratch, rows_scratch, pltpu.VMEM(*message), done(4)],
+        [SMEM, HBM, HBM, HBM, VMEM, HBM], [VMEM, HBM], {5: 1}, WHOLE_VMEM_BYTES,
     )
     far_0 = lax.ppermute(grad_0, "pipe", to_first)
     (input_grad,) = call(
-        assemble_kernel, "assemble", [pick, far_0, input_grad], [held], [pltpu.SemaphoreType.DMA((1,))],
+        assemble_kernel, "assemble", [pick, far_0, input_grad], [held], [done(1)],
         [SMEM, HBM, HBM], [HBM], {2: 0},
     )
     return input_grad[None], down_grad[None, None]

time: 431 us -> 430 us (level)
  starting transfers between devices: 46.9 us -> 53.8 us
  local copies, waits for them, and re-layouts: 50.4 us -> 44 us
    all_to_all x4, waiting for transfers between devices: 94.5 us -> 76.5 us  [exchange(): lax.all_to_all(message, 'expert', split_axis=0, concat_axis=0, tiled=True)]
    ppermute x6, waiting for transfers between devices: 47.7 us -> 62.7 us  [to_partner(): lax.ppermute(piece, 'expert', [(source, source ^ number) for source in ra...]
    unnamed x92 -> x98, local copies, waits for them, and re-layouts: 50.2 us -> 41.5 us
    pallas_call x14 -> x15, Pallas kernels: 68.3 us -> 69 us  [call(): pl.pallas_call(kernel, name=name, in_specs=specs or [VMEM] * len(operands...]
  transfers between devices with their start and end apart: 19 -> 19, of which waited for: 14 -> 13; matrix products, arithmetic and copies ran while one was open for 0% -> 1% of each run, Pallas kernels for 10% -> 11%
where the time goes in v4:
time: 430 us; the launch traced here: 429 us
  waiting for transfers between devices  149 us (35%)
  blocking collectives  110 us (26%)
  Pallas kernels  69 us (16%)
  starting transfers between devices  53.8 us (13%)
  local copies, waits for them, and re-layouts  44 us (10%)
    all_to_all x2, blocking collectives, exchange(): lax.all_to_all(message, 'expert', split_axis=0, concat_axis=0, tiled=True)  110 us
    all_to_all x4, waiting for transfers between devices, exchange(): lax.all_to_all(message, 'expert', split_axis=0, concat_axis=0, tiled=True)  76.5 us
    pallas_call x15, Pallas kernels, call(): pl.pallas_call(kernel, name=name, in_specs=specs or [VMEM] * len(operands...  69 us
    ppermute x6, waiting for transfers between devices, to_partner(): lax.ppermute(piece, 'expert', [(source, source ^ number) for source in ra...  62.7 us
    unnamed x98, local copies, waits for them, and re-layouts  41.5 us
    all_to_all x4, starting transfers between devices, exchange(): lax.all_to_all(message, 'expert', split_axis=0, concat_axis=0, tiled=True)  25.3 us
    ppermute x6, starting transfers between devices, to_partner(): lax.ppermute(piece, 'expert', [(source, source ^ number) for source in ra...  11.1 us
    ppermute x4, starting transfers between devices, shards(): operands += near + [lax.ppermute(array, 'pipe', way) for array in near]  10.5 us
  transfers between devices with their start and end apart: 19, of which 13 were waited for; matrix products, arithmetic and copies ran while one was open for 1% of the time, Pallas kernels for 11%

profile of v4, /device:TPU:13, one launch (start us, length us, event | category | flops | bytes accessed | tf_op | source)
XLA Modules:
  0.0 428.5 jit_solution(6672980466626712824)
XLA Ops:
  8.4 6.6 %all-to-all-start = ((bf16[16,136,512]{2,1,0:T(8,128)(2,1)}), bf16[16,136,512]{2,1,0:T(8,128)(2,1)S(1)}, u32[]{:S(2)}, u32[]{:S(2)}) async-start(bf16[16,136,512]{2,1,0:T(8,128)(2,1)} %copy-done.2), calls=%async_computation | async-start | bytes 4456448 | tf_op jit(solution)/shard_map/all_to_all | solution.py:470
  17.3 6.2 %collective-permute-done.2.down_other = bf16[768,4096]{1,0:T(8,128)(2,1)} collective-permute-done((bf16[768,4096]{1,0:T(8,128)(2,1)}, bf16[768,4096]{1,0:T(8,128)(2,1)}, u32[]{:S(2)}, u32[]{:S(2)}) %collective-permute-start.2) | collective-permute-done | bytes 6291488 | tf_op jit(solution)/shard_map/ppermute | solution.py:499
  26.2 7.1 %weights.1 = (bf16[4096,768]{1,0:T(8,128)(2,1)S(1)}, bf16[768,4096]{1,0:T(8,128)(2,1)S(1)}, bf16[4096,768]{1,0:T(8,128)(2,1)S(1)}, bf16[768,4096]{1,0:T(8,128)(2,1)S(1)}) custom-call(s32[2]{0:T(128)S(1)} %pad_add_fusion.pick, bf16[4096,768]{1,0:T(8,128)(2,1)S(1)} %bitcast.27, bf16[768,4096]{1,0:T(8,128)(2,1)} %bitcast.36, ...), custom_call_target="tpu_custom_call" | custom-call | flops 8049999872 | tf_op jit(solution)/shard_map/weights/pallas_call | solution.py:452
  53.7 11.9 %all-to-all-done.received = bf16[16,136,512]{2,1,0:T(8,128)(2,1)S(1)} async-done(((bf16[16,136,512]{2,1,0:T(8,128)(2,1)}), bf16[16,136,512]{2,1,0:T(8,128)(2,1)S(1)}, u32[]{:S(2)}, u32[]{:S(2)}) %all-to-all-start) | async-done | bytes 2228256 | tf_op jit(solution)/shard_map/all_to_all | solution.py:470
  71.2 7.1 %expert_forward.1 = (f32[272,768]{1,0:T(8,128)S(1)}, bf16[272,768]{1,0:T(8,128)(2,1)S(1)}, bf16[16,136,512]{2,1,0:T(8,128)(2,1)}) custom-call(bf16[16,136,512]{2,1,0:T(8,128)(2,1)S(1)} %all-to-all-done.received, bf16[4096,768]{1,0:T(8,128)(2,1)S(1)} %copy-done.25, bf16[768,4096]{1,0:T(8,128)(2,1)S(1)} %copy-done.27), custom_call_target="tpu_custom_call" | custom-call | flops 6899999744 | tf_op jit(solution)/shard_map/expert_forward/pallas_call | solution.py:452
  80.0 7.7 %collective-permute-done.4.refs_2_ = bf16[4,136,512]{2,1,0:T(8,128)(2,1)} collective-permute-done((bf16[4,136,512]{2,1,0:T(8,128)(2,1)}, bf16[4,136,512]{2,1,0:T(8,128)(2,1)}, u32[]{:S(2)}, u32[]{:S(2)}) %collective-permute-start.4) | collective-permute-done | bytes 557088 | tf_op jit(solution)/shard_map/ppermute | solution.py:477
  87.7 7.2 %all-to-all-start.1 = ((bf16[16,136,512]{2,1,0:T(8,128)(2,1)}), bf16[16,136,512]{2,1,0:T(8,128)(2,1)S(1)}, u32[]{:S(2)}, u32[]{:S(2)}) async-start(bf16[16,136,512]{2,1,0:T(8,128)(2,1)} %get-tuple-element.58), calls=%async_computation.1 | async-start | bytes 4456448 | tf_op jit(solution)/shard_map/all_to_all | solution.py:470
  101.0 13.8 %collective-permute-done.5.refs_1_ = bf16[4,136,512]{2,1,0:T(8,128)(2,1)S(1)} collective-permute-done((bf16[4,136,512]{2,1,0:T(8,128)(2,1)S(1)}, bf16[4,136,512]{2,1,0:T(8,128)(2,1)S(1)}, u32[]{:S(2)}, u32[]{:S(2)}) %collective-permute-start.5) | collective-permute-done | bytes 557088 | tf_op jit(solution)/shard_map/ppermute | solution.py:477
  114.8 15.3 %collective-permute-done.6.refs_2_ = bf16[4,136,512]{2,1,0:T(8,128)(2,1)S(1)} collective-permute-done((bf16[4,136,512]{2,1,0:T(8,128)(2,1)S(1)}, bf16[4,136,512]{2,1,0:T(8,128)(2,1)S(1)}, u32[]{:S(2)}, u32[]{:S(2)}) %collective-permute-start.6) | collective-permute-done | bytes 557088 | tf_op jit(solution)/shard_map/ppermute | solution.py:477
  130.1 7.5 %collective-permute-done.7.refs_3_ = bf16[4,136,512]{2,1,0:T(8,128)(2,1)S(1)} collective-permute-done((bf16[4,136,512]{2,1,0:T(8,128)(2,1)S(1)}, bf16[4,136,512]{2,1,0:T(8,128)(2,1)S(1)}, u32[]{:S(2)}, u32[]{:S(2)}) %collective-permute-start.7) | collective-permute-done | bytes 557088 | tf_op jit(solution)/shard_map/ppermute | solution.py:477
  138.7 5.9 %collective-permute-start.8 = (bf16[4,136,512]{2,1,0:T(8,128)(2,1)}, bf16[4,136,512]{2,1,0:T(8,128)(2,1)}, u32[]{:S(2)}, u32[]{:S(2)}) collective-permute-start(bf16[4,136,512]{2,1,0:T(8,128)(2,1)} %far_plane.1), channel_id=1, source_target_pairs={{0,12},{1,13},{2,14},{3,15},{4,8},{5,9},{6,10},{7,11},{8,4},{9,5},... | collective-permute-start | bytes 1671176 | tf_op jit(solution)/shard_map/ppermute | solution.py:477
  151.9 18.4 %collective-permute-done.8.refs_4_ = bf16[4,136,512]{2,1,0:T(8,128)(2,1)} collective-permute-done((bf16[4,136,512]{2,1,0:T(8,128)(2,1)}, bf16[4,136,512]{2,1,0:T(8,128)(2,1)}, u32[]{:S(2)}, u32[]{:S(2)}) %collective-permute-start.8) | collective-permute-done | bytes 557088 | tf_op jit(solution)/shard_map/ppermute | solution.py:477
  170.4 6.1 %all-to-all-start.2 = ((bf16[16,136,512]{2,1,0:T(8,128)(2,1)}), bf16[16,136,512]{2,1,0:T(8,128)(2,1)S(1)}, u32[]{:S(2)}, u32[]{:S(2)}) async-start(bf16[16,136,512]{2,1,0:T(8,128)(2,1)} %copy-done.3), calls=%async_computation.2 | async-start | bytes 4456448 | tf_op jit(solution)/shard_map/all_to_all | solution.py:470
  182.4 5.1 %hidden_back.1 = (f32[272,768]{1,0:T(8,128)S(1)}, bf16[16,136,512]{2,1,0:T(8,128)(2,1)S(1)}) custom-call(s32[2]{0:T(128)S(1)} %pad_add_fusion.pick, bf16[768,4096]{1,0:T(8,128)(2,1)S(1)} %copy-done.31, bf16[4,136,512]{2,1,0:T(8,128)(2,1)S(1)} %copy-done.33, bf16[4,136,512]{2,1,0:T(8,128)(2,1)S(1)} %copy-done.15, bf16[4,136,512]{2,1,0:T(8,128)(2,1)S(1)} %copy-done.17, ...), custom_call_target="tpu_custom_call" | custom-call | flops 5750000128 | tf_op jit(solution)/shard_map/hidden_back/pallas_call | solution.py:452
  189.8 37.3 %all-to-all-done.2.received = bf16[16,136,512]{2,1,0:T(8,128)(2,1)S(1)} async-done(((bf16[16,136,512]{2,1,0:T(8,128)(2,1)}), bf16[16,136,512]{2,1,0:T(8,128)(2,1)S(1)}, u32[]{:S(2)}, u32[]{:S(2)}) %all-to-all-start.2) | async-done | bytes 2228256 | tf_op jit(solution)/shard_map/all_to_all | solution.py:470
  231.0 6.0 %expert_turn.1 = (bf16[272,768]{1,0:T(8,128)(2,1)S(1)}, bf16[16,136,512]{2,1,0:T(8,128)(2,1)S(1)}) custom-call(bf16[16,136,512]{2,1,0:T(8,128)(2,1)S(1)} %all-to-all-done.2.received, f32[272,768]{1,0:T(8,128)S(1)} %copy-done.41, bf16[4096,768]{1,0:T(8,128)(2,1)S(1)} %copy-done.29), custom_call_target="tpu_custom_call" | custom-call | flops 6899999744 | tf_op jit(solution)/shard_map/expert_turn/pallas_call | solution.py:452
  237.1 54.8 %all_to_all.30.answer = bf16[16,136,512]{2,1,0:T(8,128)(2,1)S(1)} all-to-all(bf16[16,136,512]{2,1,0:T(8,128)(2,1)S(1)} %get-tuple-element.66), channel_id=1, replica_groups=mesh['pipe'=2,'expert'=16] {'expert'}, dimensions={0} | all-to-all | bytes 4456448 | tf_op jit(solution)/shard_map/all_to_all | solution.py:470
  291.9 4.7 %norm_back_send.1 = (bf16[112,4096]{1,0:T(8,128)(2,1)S(1)}, bf16[16,136,512]{2,1,0:T(8,128)(2,1)S(1)}) custom-call(bf16[112,4096]{1,0:T(8,128)(2,1)S(1)} %copy-done.43, bf16[112,4096]{1,0:T(8,128)(2,1)S(1)} %copy-done.6, bf16[16,136,512]{2,1,0:T(8,128)(2,1)S(1)} %all_to_all.30.answer, f32[112,4]{1,0:T(8,128)S(1)} %bitcast.23, f32[4,112]{1,0:T(4,128)S(1)} %copy.18.across), custom_call_target="tpu_custom_call" | custom-call | flops 5750000128 | tf_op jit(solution)/shard_map/norm_back_send/pallas_call | solution.py:452
  296.6 55.1 %all_to_all.31.refs_1_.received = bf16[16,136,512]{2,1,0:T(8,128)(2,1)S(1)} all-to-all(bf16[16,136,512]{2,1,0:T(8,128)(2,1)S(1)} %get-tuple-element.69), channel_id=1, replica_groups=mesh['pipe'=2,'expert'=16] {'expert'}, dimensions={0} | all-to-all | bytes 4456448 | tf_op jit(solution)/shard_map/all_to_all | solution.py:470
  351.7 6.9 %expert_backward.1 = bf16[16,136,512]{2,1,0:T(8,128)(2,1)} custom-call(bf16[16,136,512]{2,1,0:T(8,128)(2,1)S(1)} %all_to_all.31.refs_1_.received, f32[272,768]{1,0:T(8,128)S(1)} %copy-done.35, bf16[4096,768]{1,0:T(8,128)(2,1)S(1)} %bitcast.29, bf16[768,4096]{1,0:T(8,128)(2,1)S(1)} %bitcast.31), custom_call_target="tpu_custom_call" | custom-call | flops 6899999744 | tf_op jit(solution)/shard_map/expert_backward/pallas_call | solution.py:452
  358.6 5.5 %all-to-all-start.5 = ((bf16[16,136,512]{2,1,0:T(8,128)(2,1)}), bf16[16,136,512]{2,1,0:T(8,128)(2,1)}, u32[]{:S(2)}, u32[]{:S(2)}) async-start(bf16[16,136,512]{2,1,0:T(8,128)(2,1)} %expert_backward.1), calls=%async_computation.5 | async-start | bytes 4456448 | tf_op jit(solution)/shard_map/all_to_all | solution.py:470
  378.4 11.7 %down_grad.1 = bf16[768,4096]{1,0:T(8,128)(2,1)} custom-call(s32[2]{0:T(128)S(1)} %pad_add_fusion.pick, bf16[272,768]{1,0:T(8,128)(2,1)S(1)} %copy-done.21, bf16[16,136,512]{2,1,0:T(8,128)(2,1)S(1)} %all_to_all.31.refs_1_.received, bf16[272,768]{1,0:T(8,128)(2,1)S(1)} %collective-permute-done.9.refs_2_, ...), custom_call_target="tpu_custom_call" | custom-call | flops 12650000384 | tf_op jit(solution)/shard_map/down_grad/pallas_call | solution.py:452
  390.1 25.0 %all-to-all-done.5.answer_far = bf16[16,136,512]{2,1,0:T(8,128)(2,1)} async-done(((bf16[16,136,512]{2,1,0:T(8,128)(2,1)}), bf16[16,136,512]{2,1,0:T(8,128)(2,1)}, u32[]{:S(2)}, u32[]{:S(2)}) %all-to-all-start.5) | async-done | bytes 2228256 | tf_op jit(solution)/shard_map/all_to_all | solution.py:470
  415.1 5.3 %norm_back_last.1 = (bf16[112,4096]{1,0:T(8,128)(2,1)}, bf16[2,112,4096]{2,1,0:T(8,128)(2,1)}) custom-call(s32[2]{0:T(128)} %copy-done.8, bf16[112,4096]{1,0:T(8,128)(2,1)} %copy-done.4, bf16[112,4096]{1,0:T(8,128)(2,1)} %copy-done.13, bf16[16,136,512]{2,1,0:T(8,128)(2,1)} %all-to-all-done.5.answer_far, ...), custom_call_target="tpu_custom_call", output_to_operand_aliasing={{1}: (5, {})} | custom-call | flops 6899999744 | tf_op jit(solution)/shard_map/norm_back_last/pallas_call | solution.py:452
  (140 shorter events, 89.5 us)
Async XLA Ops:
  2.3 1.6 collective-permute-start
  3.9 13.3 %collective-permute-start.1 = (bf16[4096,768]{1,0:T(8,128)(2,1)}, bf16[4096,768]{1,0:T(8,128)(2,1)}, u32[]{:S(2)}, u32[]{:S(2)}) collective-permute-start(bf16[4096,768]{1,0:T(8,128)(2,1)} %bitcast.26), channel_id=1, source_target_pairs={{0,16},{16,0},{1,17},{17,1},{2,18},{18,2},{3,19},{19,3},{4,20},{20... | collective-permute-start | bytes 18874376 | tf_op jit(solution)/shard_map/ppermute | solution.py:498
  4.3 19.1 %collective-permute-start.2 = (bf16[768,4096]{1,0:T(8,128)(2,1)}, bf16[768,4096]{1,0:T(8,128)(2,1)}, u32[]{:S(2)}, u32[]{:S(2)}) collective-permute-start(bf16[768,4096]{1,0:T(8,128)(2,1)} %bitcast.35), channel_id=1, source_target_pairs={{0,16},{16,0},{1,17},{17,1},{2,18},{18,2},{3,19},{19,3},{4,20},{20... | collective-permute-start | bytes 18874376 | tf_op jit(solution)/shard_map/ppermute | solution.py:499
  4.6 142.3 %copy-start.4 = (bf16[112,4096]{1,0:T(8,128)(2,1)}, bf16[112,4096]{1,0:T(8,128)(2,1)S(1)}, u32[]{:S(2)}) copy-start(bf16[112,4096]{1,0:T(8,128)(2,1)S(1)} %dynamic-slice_bitcast_fusion.1.carried.before) | copy-start | bytes 2752516
  4.6 142.3 %copy-start.7 = (f32[4,112]{0,1:T(8,128)}, f32[4,112]{0,1:T(8,128)S(1)}, u32[]{:S(2)}) copy-start(f32[4,112]{0,1:T(8,128)S(1)} %get-tuple-element.78) | copy-start | bytes 5380
  8.4 57.2 %all-to-all-start = ((bf16[16,136,512]{2,1,0:T(8,128)(2,1)}), bf16[16,136,512]{2,1,0:T(8,128)(2,1)S(1)}, u32[]{:S(2)}, u32[]{:S(2)}) async-start(bf16[16,136,512]{2,1,0:T(8,128)(2,1)} %copy-done.2), calls=%async_computation | async-start | bytes 4456448 | tf_op jit(solution)/shard_map/all_to_all | solution.py:470
  15.1 363.4 %copy-start.8 = (s32[2]{0:T(128)}, s32[2]{0:T(128)S(1)}, u32[]{:S(2)}) copy-start(s32[2]{0:T(128)S(1)} %pad_add_fusion.pick) | copy-start | bytes 28
  51.2 28.8 %collective-permute-start.3 = (bf16[4,136,512]{2,1,0:T(8,128)(2,1)}, bf16[4,136,512]{2,1,0:T(8,128)(2,1)}, u32[]{:S(2)}, u32[]{:S(2)}) collective-permute-start(bf16[4,136,512]{2,1,0:T(8,128)(2,1)} %get-tuple-element.45), channel_id=1, source_target_pairs={{0,4},{1,5},{2,6},{3,7},{4,0},{5,1},{6,2},{7,3},{8,12},{9,13},{10,... | collective-permute-start | bytes 1671176 | tf_op jit(solution)/shard_map/ppermute | solution.py:477
  51.4 36.3 %collective-permute-start.4 = (bf16[4,136,512]{2,1,0:T(8,128)(2,1)}, bf16[4,136,512]{2,1,0:T(8,128)(2,1)}, u32[]{:S(2)}, u32[]{:S(2)}) collective-permute-start(bf16[4,136,512]{2,1,0:T(8,128)(2,1)} %get-tuple-element.46), channel_id=1, source_target_pairs={{0,8},{1,9},{2,10},{3,11},{4,12},{5,13},{6,14},{7,15},{8,0},{9,1},... | collective-permute-start | bytes 1671176 | tf_op jit(solution)/shard_map/ppermute | solution.py:477
  87.7 59.3 %all-to-all-start.1 = ((bf16[16,136,512]{2,1,0:T(8,128)(2,1)}), bf16[16,136,512]{2,1,0:T(8,128)(2,1)S(1)}, u32[]{:S(2)}, u32[]{:S(2)}) async-start(bf16[16,136,512]{2,1,0:T(8,128)(2,1)} %get-tuple-element.58), calls=%async_computation.1 | async-start | bytes 4456448 | tf_op jit(solution)/shard_map/all_to_all | solution.py:470
  98.3 16.5 %collective-permute-start.5 = (bf16[4,136,512]{2,1,0:T(8,128)(2,1)S(1)}, bf16[4,136,512]{2,1,0:T(8,128)(2,1)S(1)}, u32[]{:S(2)}, u32[]{:S(2)}) collective-permute-start(bf16[4,136,512]{2,1,0:T(8,128)(2,1)S(1)} %get-tuple-element.55), channel_id=1, source_target_pairs={{0,1},{1,0},{2,3},{3,2},{4,5},{5,4},{6,7},{7,6},{8,9},{9,8},{10,11... | collective-permute-start | bytes 1671176 | tf_op jit(solution)/shard_map/ppermute | solution.py:477
  99.6 30.6 %collective-permute-start.6 = (bf16[4,136,512]{2,1,0:T(8,128)(2,1)S(1)}, bf16[4,136,512]{2,1,0:T(8,128)(2,1)S(1)}, u32[]{:S(2)}, u32[]{:S(2)}) collective-permute-start(bf16[4,136,512]{2,1,0:T(8,128)(2,1)S(1)} %get-tuple-element.56), channel_id=1, source_target_pairs={{0,2},{1,3},{2,0},{3,1},{4,6},{5,7},{6,4},{7,5},{8,10},{9,11},{10,... | collective-permute-start | bytes 1671176 | tf_op jit(solution)/shard_map/ppermute | solution.py:477
  99.9 37.8 %collective-permute-start.7 = (bf16[4,136,512]{2,1,0:T(8,128)(2,1)S(1)}, bf16[4,136,512]{2,1,0:T(8,128)(2,1)S(1)}, u32[]{:S(2)}, u32[]{:S(2)}) collective-permute-start(bf16[4,136,512]{2,1,0:T(8,128)(2,1)S(1)} %get-tuple-element.57), channel_id=1, source_target_pairs={{0,3},{1,2},{2,1},{3,0},{4,7},{5,6},{6,5},{7,4},{8,11},{9,10},{10,... | collective-permute-start | bytes 1671176 | tf_op jit(solution)/shard_map/ppermute | solution.py:477
  138.7 31.7 %collective-permute-start.8 = (bf16[4,136,512]{2,1,0:T(8,128)(2,1)}, bf16[4,136,512]{2,1,0:T(8,128)(2,1)}, u32[]{:S(2)}, u32[]{:S(2)}) collective-permute-start(bf16[4,136,512]{2,1,0:T(8,128)(2,1)} %far_plane.1), channel_id=1, source_target_pairs={{0,12},{1,13},{2,14},{3,15},{4,8},{5,9},{6,10},{7,11},{8,4},{9,5},... | collective-permute-start | bytes 1671176 | tf_op jit(solution)/shard_map/ppermute | solution.py:477
  170.4 56.7 %all-to-all-start.2 = ((bf16[16,136,512]{2,1,0:T(8,128)(2,1)}), bf16[16,136,512]{2,1,0:T(8,128)(2,1)S(1)}, u32[]{:S(2)}, u32[]{:S(2)}) async-start(bf16[16,136,512]{2,1,0:T(8,128)(2,1)} %copy-done.3), calls=%async_computation.2 | async-start | bytes 4456448 | tf_op jit(solution)/shard_map/all_to_all | solution.py:470
  237.1 114.6 %slice-start = ((s8[6291456]{0:T(1024)(128)(4,1)}), s8[4194304]{0:T(1024)(128)(4,1)S(1)}, s32[]{:S(2)}) async-start(s8[6291456]{0:T(1024)(128)(4,1)} %bitcast.28), calls=%async_computation.6 | async-start | bytes 8388608
  237.1 114.6 %slice-start.2 = ((s8[6291456]{0:T(1024)(128)(4,1)}), s8[4194304]{0:T(1024)(128)(4,1)S(1)}, s32[]{:S(2)}) async-start(s8[6291456]{0:T(1024)(128)(4,1)} %bitcast.30), calls=%async_computation.8 | async-start | bytes 8388608
  358.6 56.6 %all-to-all-start.5 = ((bf16[16,136,512]{2,1,0:T(8,128)(2,1)}), bf16[16,136,512]{2,1,0:T(8,128)(2,1)}, u32[]{:S(2)}, u32[]{:S(2)}) async-start(bf16[16,136,512]{2,1,0:T(8,128)(2,1)} %expert_backward.1), calls=%async_computation.5 | async-start | bytes 4456448 | tf_op jit(solution)/shard_map/all_to_all | solution.py:470
  364.1 13.6 %collective-permute-start.12 = (bf16[16,136,512]{2,1,0:T(8,128)(2,1)}, bf16[16,136,512]{2,1,0:T(8,128)(2,1)S(1)}, u32[]{:S(2)}, u32[]{:S(2)}) collective-permute-start(bf16[16,136,512]{2,1,0:T(8,128)(2,1)} %copy-done.11), channel_id=1, source_target_pairs={{0,16},{1,17},{2,18},{3,19},{4,20},{5,21},{6,22},{7,23},{8,24},{9,... | collective-permute-start | bytes 6684680 | tf_op jit(solution)/shard_map/ppermute | solution.py:574
  365.6 12.8 %collective-permute-start.10 = (bf16[16,136,512]{2,1,0:T(8,128)(2,1)S(1)}, bf16[16,136,512]{2,1,0:T(8,128)(2,1)S(1)}, u32[]{:S(2)}, u32[]{:S(2)}) collective-permute-start(bf16[16,136,512]{2,1,0:T(8,128)(2,1)S(1)} %all_to_all.31.refs_1_.received), channel_id=1, source_target_pairs={{16,0},{17,1},{18,2},{19,3},{20,4},{21,5},{22,6},{23,7},{24,8},{25... | collective-permute-start | bytes 6684680 | tf_op jit(solution)/shard_map/ppermute | solution.py:574
  370.1 5.7 %collective-permute-start.13 = (bf16[112,4096]{1,0:T(8,128)(2,1)S(1)}, bf16[112,4096]{1,0:T(8,128)(2,1)S(1)}, u32[]{:S(2)}, u32[]{:S(2)}) collective-permute-start(bf16[112,4096]{1,0:T(8,128)(2,1)S(1)} %get-tuple-element.67.grad.incoming), channel_id=1, source_target_pairs={{0,16},{1,17},{2,18},{3,19},{4,20},{5,21},{6,22},{7,23},{8,24},{9,... | collective-permute-start | bytes 2752520 | tf_op jit(solution)/shard_map/ppermute | solution.py:580
  371.4 6.2 %collective-permute-start.9 = (bf16[272,768]{1,0:T(8,128)(2,1)}, bf16[272,768]{1,0:T(8,128)(2,1)S(1)}, u32[]{:S(2)}, u32[]{:S(2)}) collective-permute-start(bf16[272,768]{1,0:T(8,128)(2,1)} %copy-done.20), channel_id=1, source_target_pairs={{16,0},{17,1},{18,2},{19,3},{20,4},{21,5},{22,6},{23,7},{24,8},{25... | collective-permute-start | bytes 1253384 | tf_op jit(solution)/shard_map/ppermute | solution.py:574
  374.5 3.9 collective-permute-start.11
  420.4 6.6 %collective-permute-start.14 = (bf16[112,4096]{1,0:T(8,128)(2,1)}, bf16[112,4096]{1,0:T(8,128)(2,1)S(1)}, u32[]{:S(2)}, u32[]{:S(2)}) collective-permute-start(bf16[112,4096]{1,0:T(8,128)(2,1)} %get-tuple-element.75), channel_id=1, source_target_pairs={{16,0},{17,1},{18,2},{19,3},{20,4},{21,5},{22,6},{23,7},{24,8},{25... | collective-permute-start | bytes 2752520 | tf_op jit(solution)/shard_map/ppermute | solution.py:594
  (43 other events, 648.1 us)

commit v5 on v4

--- a/solution.py
+++ b/solution.py
@@ -15,6 +15,7 @@
 FEATURE_BLOCKS = 8
 PLANES = 4
 SLOT_TILE = 16
+FEW_REST_ROWS = 32
 VMEM_BYTES = 20 * 1024 * 1024
 WHOLE_VMEM_BYTES = 60 * 1024 * 1024
 
@@ -158,9 +159,20 @@
     return (iota(shape, 1) == iota(shape, 0) * FEATURE_BLOCKS + block).astype(BF16)
 
 
+def all_rest_places(sizes, across):
+    rows = sizes.rest_rows
+    shape = (rows * FEATURE_BLOCKS, rows * FEATURE_BLOCKS)
+    to, source = iota(shape, across), iota(shape, 1 - across)
+    return ((to % FEATURE_BLOCKS) * rows + to // FEATURE_BLOCKS == source).astype(BF16)
+
+
+def few_rest_rows(sizes):
+    return sizes.rest_rows <= FEW_REST_ROWS and sizes.rest_rows % SLOT_TILE == 0
+
+
 def write_pieces(sizes, pieces, block_values):
     tile, each = sizes.tiled, sizes.experts // len(pieces)
-    rest = None
+    rest, others = None, []
     for block in range(FEATURE_BLOCKS):
         values = block_values(block)
         if tile:
@@ -170,8 +182,14 @@
                     each, tile, sizes.lanes
                 )
         if sizes.rest:
-            part = dot(rest_places(sizes, block), values[sizes.tiled_rows :].astype(BF16))
-            rest = part if rest is None else rest + part
+            other = values[sizes.tiled_rows :].astype(BF16)
+            if few_rest_rows(sizes):
+                others.append(other)
+            else:
+                part = dot(rest_places(sizes, block), other)
+                rest = part if rest is None else rest + part
+    if others:
+        rest = dot(all_rest_places(sizes, 0), jnp.concatenate(others, axis=0))
     if sizes.rest:
         first, each_rest = FEATURE_BLOCKS * tile, FEATURE_BLOCKS * sizes.rest
         for number, piece in enumerate(pieces):
@@ -187,12 +205,11 @@
     if not sizes.rest:
         return None
     first = FEATURE_BLOCKS * sizes.tiled
-    return (
-        message[:, first:, :]
-        .astype(F32)
-        .reshape(sizes.rest_rows * FEATURE_BLOCKS, sizes.lanes)
-        .astype(BF16)
-    )
+    rows = message[:, first:, :].astype(F32).reshape(sizes.rest_rows * FEATURE_BLOCKS, sizes.lanes)
+    rows = rows.astype(BF16)
+    if few_rest_rows(sizes):
+        rows = dot(all_rest_places(sizes, 1), rows).astype(BF16)
+    return rows
 
 
 def read_block(sizes, message, rest, block):
@@ -203,7 +220,9 @@
                 sizes.tiled_rows, sizes.lanes
             )
         )
-    if sizes.rest:
+    if sizes.rest and few_rest_rows(sizes):
+        parts.append(rest[block * sizes.rest_rows : (block + 1) * sizes.rest_rows])
+    elif sizes.rest:
         parts.append(dot(rest_places_across(sizes, block), rest).astype(BF16))
     return jnp.concatenate(parts, axis=0)
 
@@ -309,8 +328,8 @@
 
 
 def last_kernel(
-    sizes, pick, before, incoming, answer_far, table, held, result, whole,
-    upstream, clip, grad, answer, done,
+    sizes, pick, before, incoming, answer_far, table, held, result_out, whole,
+    upstream, clip, grad, answer, result, done,
 ):
     copies = [
         bring(answer_far, answer, done.at[0]),
@@ -319,9 +338,13 @@
     ]
     norm_back(sizes, clip, grad, answer, table, result, upstream, copies)
 
+    leaving = bring(result, result_out, done.at[4])
+
     @pl.when(pick[0] == 0)
     def _():
         bring(result, whole.at[0], done.at[3]).wait()
+
+    leaving.wait()
 
 
 def turn_kernel(sizes, carried, incoming, answer, table, across, result, message, upstream):
@@ -588,8 +611,8 @@
     grad_0, input_grad = call(
         kernel(last_kernel), "norm_back_last",
         [pick, clip, grad_1, back_home_0, table_0, input_grad], [home_rows, held],
-        [upstream_scratch, rows_scratch, rows_scratch, pltpu.VMEM(*message), done(4)],
-        [SMEM, HBM, HBM, HBM, VMEM, HBM], [VMEM, HBM], {5: 1}, WHOLE_VMEM_BYTES,
+        [upstream_scratch, rows_scratch, rows_scratch, pltpu.VMEM(*message), rows_scratch, done(5)],
+        [SMEM, HBM, HBM, HBM, VMEM, HBM], [HBM, HBM], {5: 1}, WHOLE_VMEM_BYTES,
     )
     far_0 = lax.ppermute(grad_0, "pipe", to_first)
     (input_grad,) = call(

time: 430 us -> 426 us (level)
  Pallas kernels: 69 us -> 60.2 us
    pallas_call x15, Pallas kernels: 69 us -> 60.2 us  [call(): pl.pallas_call(kernel, name=name, in_specs=specs or [VMEM] * len(operands...]
  transfers between devices with their start and end apart: 19 -> 19, of which waited for: 13 -> 13; matrix products, arithmetic and copies ran while one was open for 1% -> 1% of each run, Pallas kernels for 11% -> 9%
where the time goes in v5:
time: 426 us; the launch traced here: 424 us
  waiting for transfers between devices  153 us (36%)
  blocking collectives  110 us (26%)
  Pallas kernels  60.2 us (14%)
  starting transfers between devices  54.8 us (13%)
  local copies, waits for them, and re-layouts  44 us (10%)
    all_to_all x2, blocking collectives, exchange(): lax.all_to_all(message, 'expert', split_axis=0, concat_axis=0, tiled=True)  110 us
    all_to_all x4, waiting for transfers between devices, exchange(): lax.all_to_all(message, 'expert', split_axis=0, concat_axis=0, tiled=True)  77.4 us
    ppermute x6, waiting for transfers between devices, to_partner(): lax.ppermute(piece, 'expert', [(source, source ^ number) for source in ra...  64.6 us
    pallas_call x15, Pallas kernels, call(): pl.pallas_call(kernel, name=name, in_specs=specs or [VMEM] * len(operands...  60.2 us
    unnamed x98, local copies, waits for them, and re-layouts  41.5 us
    all_to_all x4, starting transfers between devices, exchange(): lax.all_to_all(message, 'expert', split_axis=0, concat_axis=0, tiled=True)  27.5 us
    ppermute x6, starting transfers between devices, to_partner(): lax.ppermute(piece, 'expert', [(source, source ^ number) for source in ra...  10.5 us
    ppermute x4, starting transfers between devices, shards(): operands += near + [lax.ppermute(array, 'pipe', way) for array in near]  10.5 us
  transfers between devices with their start and end apart: 19, of which 13 were waited for; matrix products, arithmetic and copies ran while one was open for 1% of the time, Pallas kernels for 9%

profile of v5, /device:TPU:13, one launch (start us, length us, event | category | flops | bytes accessed | tf_op | source)
XLA Modules:
  0.0 424.4 jit_solution(9994619812665854764)
XLA Ops:
  7.3 6.6 %all-to-all-start = ((bf16[16,136,512]{2,1,0:T(8,128)(2,1)}), bf16[16,136,512]{2,1,0:T(8,128)(2,1)S(1)}, u32[]{:S(2)}, u32[]{:S(2)}) async-start(bf16[16,136,512]{2,1,0:T(8,128)(2,1)} %copy-done.2), calls=%async_computation | async-start | bytes 4456448 | tf_op jit(solution)/shard_map/all_to_all | solution.py:493
  16.2 7.2 %collective-permute-done.2.down_other = bf16[768,4096]{1,0:T(8,128)(2,1)} collective-permute-done((bf16[768,4096]{1,0:T(8,128)(2,1)}, bf16[768,4096]{1,0:T(8,128)(2,1)}, u32[]{:S(2)}, u32[]{:S(2)}) %collective-permute-start.2) | collective-permute-done | bytes 6291488 | tf_op jit(solution)/shard_map/ppermute | solution.py:522
  26.2 7.1 %weights.1 = (bf16[4096,768]{1,0:T(8,128)(2,1)S(1)}, bf16[768,4096]{1,0:T(8,128)(2,1)S(1)}, bf16[4096,768]{1,0:T(8,128)(2,1)S(1)}, bf16[768,4096]{1,0:T(8,128)(2,1)S(1)}) custom-call(s32[2]{0:T(128)S(1)} %pad_add_fusion.pick, bf16[4096,768]{1,0:T(8,128)(2,1)S(1)} %bitcast.27, bf16[768,4096]{1,0:T(8,128)(2,1)} %bitcast.36, ...), custom_call_target="tpu_custom_call" | custom-call | flops 8049999872 | tf_op jit(solution)/shard_map/weights/pallas_call | solution.py:475
  52.7 11.9 %all-to-all-done.received = bf16[16,136,512]{2,1,0:T(8,128)(2,1)S(1)} async-done(((bf16[16,136,512]{2,1,0:T(8,128)(2,1)}), bf16[16,136,512]{2,1,0:T(8,128)(2,1)S(1)}, u32[]{:S(2)}, u32[]{:S(2)}) %all-to-all-start) | async-done | bytes 2228256 | tf_op jit(solution)/shard_map/all_to_all | solution.py:493
  70.1 6.4 %expert_forward.1 = (f32[272,768]{1,0:T(8,128)S(1)}, bf16[272,768]{1,0:T(8,128)(2,1)S(1)}, bf16[16,136,512]{2,1,0:T(8,128)(2,1)}) custom-call(bf16[16,136,512]{2,1,0:T(8,128)(2,1)S(1)} %all-to-all-done.received, bf16[4096,768]{1,0:T(8,128)(2,1)S(1)} %copy-done.25, bf16[768,4096]{1,0:T(8,128)(2,1)S(1)} %copy-done.27), custom_call_target="tpu_custom_call" | custom-call | flops 6899999744 | tf_op jit(solution)/shard_map/expert_forward/pallas_call | solution.py:475
  78.2 8.4 %collective-permute-done.4.refs_2_ = bf16[4,136,512]{2,1,0:T(8,128)(2,1)} collective-permute-done((bf16[4,136,512]{2,1,0:T(8,128)(2,1)}, bf16[4,136,512]{2,1,0:T(8,128)(2,1)}, u32[]{:S(2)}, u32[]{:S(2)}) %collective-permute-start.4) | collective-permute-done | bytes 557088 | tf_op jit(solution)/shard_map/ppermute | solution.py:500
  86.6 7.2 %all-to-all-start.1 = ((bf16[16,136,512]{2,1,0:T(8,128)(2,1)}), bf16[16,136,512]{2,1,0:T(8,128)(2,1)S(1)}, u32[]{:S(2)}, u32[]{:S(2)}) async-start(bf16[16,136,512]{2,1,0:T(8,128)(2,1)} %get-tuple-element.58), calls=%async_computation.1 | async-start | bytes 4456448 | tf_op jit(solution)/shard_map/all_to_all | solution.py:493
  100.0 14.6 %collective-permute-done.5.refs_1_ = bf16[4,136,512]{2,1,0:T(8,128)(2,1)S(1)} collective-permute-done((bf16[4,136,512]{2,1,0:T(8,128)(2,1)S(1)}, bf16[4,136,512]{2,1,0:T(8,128)(2,1)S(1)}, u32[]{:S(2)}, u32[]{:S(2)}) %collective-permute-start.5) | collective-permute-done | bytes 557088 | tf_op jit(solution)/shard_map/ppermute | solution.py:500
  114.6 14.1 %collective-permute-done.6.refs_2_ = bf16[4,136,512]{2,1,0:T(8,128)(2,1)S(1)} collective-permute-done((bf16[4,136,512]{2,1,0:T(8,128)(2,1)S(1)}, bf16[4,136,512]{2,1,0:T(8,128)(2,1)S(1)}, u32[]{:S(2)}, u32[]{:S(2)}) %collective-permute-start.6) | collective-permute-done | bytes 557088 | tf_op jit(solution)/shard_map/ppermute | solution.py:500
  128.8 8.7 %collective-permute-done.7.refs_3_ = bf16[4,136,512]{2,1,0:T(8,128)(2,1)S(1)} collective-permute-done((bf16[4,136,512]{2,1,0:T(8,128)(2,1)S(1)}, bf16[4,136,512]{2,1,0:T(8,128)(2,1)S(1)}, u32[]{:S(2)}, u32[]{:S(2)}) %collective-permute-start.7) | collective-permute-done | bytes 557088 | tf_op jit(solution)/shard_map/ppermute | solution.py:500
  138.5 5.4 %collective-permute-start.8 = (bf16[4,136,512]{2,1,0:T(8,128)(2,1)}, bf16[4,136,512]{2,1,0:T(8,128)(2,1)}, u32[]{:S(2)}, u32[]{:S(2)}) collective-permute-start(bf16[4,136,512]{2,1,0:T(8,128)(2,1)} %far_plane.1), channel_id=1, source_target_pairs={{0,12},{1,13},{2,14},{3,15},{4,8},{5,9},{6,10},{7,11},{8,4},{9,5},... | collective-permute-start | bytes 1671176 | tf_op jit(solution)/shard_map/ppermute | solution.py:500
  149.5 18.7 %collective-permute-done.8.refs_4_ = bf16[4,136,512]{2,1,0:T(8,128)(2,1)} collective-permute-done((bf16[4,136,512]{2,1,0:T(8,128)(2,1)}, bf16[4,136,512]{2,1,0:T(8,128)(2,1)}, u32[]{:S(2)}, u32[]{:S(2)}) %collective-permute-start.8) | collective-permute-done | bytes 557088 | tf_op jit(solution)/shard_map/ppermute | solution.py:500
  168.1 8.1 %all-to-all-start.2 = ((bf16[16,136,512]{2,1,0:T(8,128)(2,1)}), bf16[16,136,512]{2,1,0:T(8,128)(2,1)S(1)}, u32[]{:S(2)}, u32[]{:S(2)}) async-start(bf16[16,136,512]{2,1,0:T(8,128)(2,1)} %copy-done.3), calls=%async_computation.2 | async-start | bytes 4456448 | tf_op jit(solution)/shard_map/all_to_all | solution.py:493
  182.2 4.5 %hidden_back.1 = (f32[272,768]{1,0:T(8,128)S(1)}, bf16[16,136,512]{2,1,0:T(8,128)(2,1)S(1)}) custom-call(s32[2]{0:T(128)S(1)} %pad_add_fusion.pick, bf16[768,4096]{1,0:T(8,128)(2,1)S(1)} %copy-done.31, bf16[4,136,512]{2,1,0:T(8,128)(2,1)S(1)} %copy-done.33, bf16[4,136,512]{2,1,0:T(8,128)(2,1)S(1)} %copy-done.15, bf16[4,136,512]{2,1,0:T(8,128)(2,1)S(1)} %copy-done.17, ...), custom_call_target="tpu_custom_call" | custom-call | flops 5750000128 | tf_op jit(solution)/shard_map/hidden_back/pallas_call | solution.py:475
  189.0 37.9 %all-to-all-done.2.received = bf16[16,136,512]{2,1,0:T(8,128)(2,1)S(1)} async-done(((bf16[16,136,512]{2,1,0:T(8,128)(2,1)}), bf16[16,136,512]{2,1,0:T(8,128)(2,1)S(1)}, u32[]{:S(2)}, u32[]{:S(2)}) %all-to-all-start.2) | async-done | bytes 2228256 | tf_op jit(solution)/shard_map/all_to_all | solution.py:493
  230.8 5.0 %expert_turn.1 = (bf16[272,768]{1,0:T(8,128)(2,1)S(1)}, bf16[16,136,512]{2,1,0:T(8,128)(2,1)S(1)}) custom-call(bf16[16,136,512]{2,1,0:T(8,128)(2,1)S(1)} %all-to-all-done.2.received, f32[272,768]{1,0:T(8,128)S(1)} %copy-done.41, bf16[4096,768]{1,0:T(8,128)(2,1)S(1)} %copy-done.29), custom_call_target="tpu_custom_call" | custom-call | flops 6899999744 | tf_op jit(solution)/shard_map/expert_turn/pallas_call | solution.py:475
  235.9 54.6 %all_to_all.30.answer = bf16[16,136,512]{2,1,0:T(8,128)(2,1)S(1)} all-to-all(bf16[16,136,512]{2,1,0:T(8,128)(2,1)S(1)} %get-tuple-element.66), channel_id=1, replica_groups=mesh['pipe'=2,'expert'=16] {'expert'}, dimensions={0} | all-to-all | bytes 4456448 | tf_op jit(solution)/shard_map/all_to_all | solution.py:493
  293.7 55.1 %all_to_all.31.refs_1_.received = bf16[16,136,512]{2,1,0:T(8,128)(2,1)S(1)} all-to-all(bf16[16,136,512]{2,1,0:T(8,128)(2,1)S(1)} %get-tuple-element.69), channel_id=1, replica_groups=mesh['pipe'=2,'expert'=16] {'expert'}, dimensions={0} | all-to-all | bytes 4456448 | tf_op jit(solution)/shard_map/all_to_all | solution.py:493
  348.9 6.3 %expert_backward.1 = bf16[16,136,512]{2,1,0:T(8,128)(2,1)} custom-call(bf16[16,136,512]{2,1,0:T(8,128)(2,1)S(1)} %all_to_all.31.refs_1_.received, f32[272,768]{1,0:T(8,128)S(1)} %copy-done.35, bf16[4096,768]{1,0:T(8,128)(2,1)S(1)} %bitcast.29, bf16[768,4096]{1,0:T(8,128)(2,1)S(1)} %bitcast.31), custom_call_target="tpu_custom_call" | custom-call | flops 6899999744 | tf_op jit(solution)/shard_map/expert_backward/pallas_call | solution.py:475
  355.2 5.7 %all-to-all-start.5 = ((bf16[16,136,512]{2,1,0:T(8,128)(2,1)}), bf16[16,136,512]{2,1,0:T(8,128)(2,1)}, u32[]{:S(2)}, u32[]{:S(2)}) async-start(bf16[16,136,512]{2,1,0:T(8,128)(2,1)} %expert_backward.1), calls=%async_computation.5 | async-start | bytes 4456448 | tf_op jit(solution)/shard_map/all_to_all | solution.py:493
  362.5 4.5 %collective-permute-start.10 = (bf16[16,136,512]{2,1,0:T(8,128)(2,1)S(1)}, bf16[16,136,512]{2,1,0:T(8,128)(2,1)S(1)}, u32[]{:S(2)}, u32[]{:S(2)}) collective-permute-start(bf16[16,136,512]{2,1,0:T(8,128)(2,1)S(1)} %all_to_all.31.refs_1_.received), channel_id=1, source_target_pairs={{16,0},{17,1},{18,2},{19,3},{20,4},{21,5},{22,6},{23,7},{24,8},{25... | collective-permute-start | bytes 6684680 | tf_op jit(solution)/shard_map/ppermute | solution.py:597
  375.3 11.1 %down_grad.1 = bf16[768,4096]{1,0:T(8,128)(2,1)} custom-call(s32[2]{0:T(128)S(1)} %pad_add_fusion.pick, bf16[272,768]{1,0:T(8,128)(2,1)S(1)} %copy-done.21, bf16[16,136,512]{2,1,0:T(8,128)(2,1)S(1)} %all_to_all.31.refs_1_.received, bf16[272,768]{1,0:T(8,128)(2,1)S(1)} %collective-permute-done.9.refs_2_, ...), custom_call_target="tpu_custom_call" | custom-call | flops 12650000384 | tf_op jit(solution)/shard_map/down_grad/pallas_call | solution.py:475
  386.4 25.6 %all-to-all-done.5.answer_far = bf16[16,136,512]{2,1,0:T(8,128)(2,1)} async-done(((bf16[16,136,512]{2,1,0:T(8,128)(2,1)}), bf16[16,136,512]{2,1,0:T(8,128)(2,1)}, u32[]{:S(2)}, u32[]{:S(2)}) %all-to-all-start.5) | async-done | bytes 2228256 | tf_op jit(solution)/shard_map/all_to_all | solution.py:493
  412.0 4.9 %norm_back_last.1 = (bf16[112,4096]{1,0:T(8,128)(2,1)}, bf16[2,112,4096]{2,1,0:T(8,128)(2,1)}) custom-call(s32[2]{0:T(128)} %copy-done.8, bf16[112,4096]{1,0:T(8,128)(2,1)} %copy-done.4, bf16[112,4096]{1,0:T(8,128)(2,1)} %copy-done.13, bf16[16,136,512]{2,1,0:T(8,128)(2,1)} %all-to-all-done.5.answer_far, ...), custom_call_target="tpu_custom_call", output_to_operand_aliasing={{1}: (5, {})} | custom-call | flops 6899999744 | tf_op jit(solution)/shard_map/norm_back_last/pallas_call | solution.py:475
  (140 shorter events, 83.7 us)
Async XLA Ops:
  2.3 1.6 collective-permute-start
  3.9 12.3 %collective-permute-start.1 = (bf16[4096,768]{1,0:T(8,128)(2,1)}, bf16[4096,768]{1,0:T(8,128)(2,1)}, u32[]{:S(2)}, u32[]{:S(2)}) collective-permute-start(bf16[4096,768]{1,0:T(8,128)(2,1)} %bitcast.26), channel_id=1, source_target_pairs={{0,16},{16,0},{1,17},{17,1},{2,18},{18,2},{3,19},{19,3},{4,20},{20... | collective-permute-start | bytes 18874376 | tf_op jit(solution)/shard_map/ppermute | solution.py:521
  4.3 19.1 %collective-permute-start.2 = (bf16[768,4096]{1,0:T(8,128)(2,1)}, bf16[768,4096]{1,0:T(8,128)(2,1)}, u32[]{:S(2)}, u32[]{:S(2)}) collective-permute-start(bf16[768,4096]{1,0:T(8,128)(2,1)} %bitcast.35), channel_id=1, source_target_pairs={{0,16},{16,0},{1,17},{17,1},{2,18},{18,2},{3,19},{19,3},{4,20},{20... | collective-permute-start | bytes 18874376 | tf_op jit(solution)/shard_map/ppermute | solution.py:522
  4.6 141.3 %copy-start.4 = (bf16[112,4096]{1,0:T(8,128)(2,1)}, bf16[112,4096]{1,0:T(8,128)(2,1)S(1)}, u32[]{:S(2)}) copy-start(bf16[112,4096]{1,0:T(8,128)(2,1)S(1)} %dynamic-slice_bitcast_fusion.1.carried.before) | copy-start | bytes 2752516
  4.6 141.3 %copy-start.7 = (f32[4,112]{0,1:T(8,128)}, f32[4,112]{0,1:T(8,128)S(1)}, u32[]{:S(2)}) copy-start(f32[4,112]{0,1:T(8,128)S(1)} %get-tuple-element.78) | copy-start | bytes 5380
  7.3 57.2 %all-to-all-start = ((bf16[16,136,512]{2,1,0:T(8,128)(2,1)}), bf16[16,136,512]{2,1,0:T(8,128)(2,1)S(1)}, u32[]{:S(2)}, u32[]{:S(2)}) async-start(bf16[16,136,512]{2,1,0:T(8,128)(2,1)} %copy-done.2), calls=%async_computation | async-start | bytes 4456448 | tf_op jit(solution)/shard_map/all_to_all | solution.py:493
  14.0 361.2 %copy-start.8 = (s32[2]{0:T(128)}, s32[2]{0:T(128)S(1)}, u32[]{:S(2)}) copy-start(s32[2]{0:T(128)S(1)} %pad_add_fusion.pick) | copy-start | bytes 28
  50.2 28.0 %collective-permute-start.3 = (bf16[4,136,512]{2,1,0:T(8,128)(2,1)}, bf16[4,136,512]{2,1,0:T(8,128)(2,1)}, u32[]{:S(2)}, u32[]{:S(2)}) collective-permute-start(bf16[4,136,512]{2,1,0:T(8,128)(2,1)} %get-tuple-element.45), channel_id=1, source_target_pairs={{0,4},{1,5},{2,6},{3,7},{4,0},{5,1},{6,2},{7,3},{8,12},{9,13},{10,... | collective-permute-start | bytes 1671176 | tf_op jit(solution)/shard_map/ppermute | solution.py:500
  50.4 36.3 %collective-permute-start.4 = (bf16[4,136,512]{2,1,0:T(8,128)(2,1)}, bf16[4,136,512]{2,1,0:T(8,128)(2,1)}, u32[]{:S(2)}, u32[]{:S(2)}) collective-permute-start(bf16[4,136,512]{2,1,0:T(8,128)(2,1)} %get-tuple-element.46), channel_id=1, source_target_pairs={{0,8},{1,9},{2,10},{3,11},{4,12},{5,13},{6,14},{7,15},{8,0},{9,1},... | collective-permute-start | bytes 1671176 | tf_op jit(solution)/shard_map/ppermute | solution.py:500
  86.6 59.3 %all-to-all-start.1 = ((bf16[16,136,512]{2,1,0:T(8,128)(2,1)}), bf16[16,136,512]{2,1,0:T(8,128)(2,1)S(1)}, u32[]{:S(2)}, u32[]{:S(2)}) async-start(bf16[16,136,512]{2,1,0:T(8,128)(2,1)} %get-tuple-element.58), calls=%async_computation.1 | async-start | bytes 4456448 | tf_op jit(solution)/shard_map/all_to_all | solution.py:493
  97.3 17.3 %collective-permute-start.5 = (bf16[4,136,512]{2,1,0:T(8,128)(2,1)S(1)}, bf16[4,136,512]{2,1,0:T(8,128)(2,1)S(1)}, u32[]{:S(2)}, u32[]{:S(2)}) collective-permute-start(bf16[4,136,512]{2,1,0:T(8,128)(2,1)S(1)} %get-tuple-element.55), channel_id=1, source_target_pairs={{0,1},{1,0},{2,3},{3,2},{4,5},{5,4},{6,7},{7,6},{8,9},{9,8},{10,11... | collective-permute-start | bytes 1671176 | tf_op jit(solution)/shard_map/ppermute | solution.py:500
  98.5 30.2 %collective-permute-start.6 = (bf16[4,136,512]{2,1,0:T(8,128)(2,1)S(1)}, bf16[4,136,512]{2,1,0:T(8,128)(2,1)S(1)}, u32[]{:S(2)}, u32[]{:S(2)}) collective-permute-start(bf16[4,136,512]{2,1,0:T(8,128)(2,1)S(1)} %get-tuple-element.56), channel_id=1, source_target_pairs={{0,2},{1,3},{2,0},{3,1},{4,6},{5,7},{6,4},{7,5},{8,10},{9,11},{10,... | collective-permute-start | bytes 1671176 | tf_op jit(solution)/shard_map/ppermute | solution.py:500
  98.8 38.7 %collective-permute-start.7 = (bf16[4,136,512]{2,1,0:T(8,128)(2,1)S(1)}, bf16[4,136,512]{2,1,0:T(8,128)(2,1)S(1)}, u32[]{:S(2)}, u32[]{:S(2)}) collective-permute-start(bf16[4,136,512]{2,1,0:T(8,128)(2,1)S(1)} %get-tuple-element.57), channel_id=1, source_target_pairs={{0,3},{1,2},{2,1},{3,0},{4,7},{5,6},{6,5},{7,4},{8,11},{9,10},{10,... | collective-permute-start | bytes 1671176 | tf_op jit(solution)/shard_map/ppermute | solution.py:500
  138.5 29.6 %collective-permute-start.8 = (bf16[4,136,512]{2,1,0:T(8,128)(2,1)}, bf16[4,136,512]{2,1,0:T(8,128)(2,1)}, u32[]{:S(2)}, u32[]{:S(2)}) collective-permute-start(bf16[4,136,512]{2,1,0:T(8,128)(2,1)} %far_plane.1), channel_id=1, source_target_pairs={{0,12},{1,13},{2,14},{3,15},{4,8},{5,9},{6,10},{7,11},{8,4},{9,5},... | collective-permute-start | bytes 1671176 | tf_op jit(solution)/shard_map/ppermute | solution.py:500
  168.1 58.8 %all-to-all-start.2 = ((bf16[16,136,512]{2,1,0:T(8,128)(2,1)}), bf16[16,136,512]{2,1,0:T(8,128)(2,1)S(1)}, u32[]{:S(2)}, u32[]{:S(2)}) async-start(bf16[16,136,512]{2,1,0:T(8,128)(2,1)} %copy-done.3), calls=%async_computation.2 | async-start | bytes 4456448 | tf_op jit(solution)/shard_map/all_to_all | solution.py:493
  235.9 112.9 %slice-start = ((s8[6291456]{0:T(1024)(128)(4,1)}), s8[4194304]{0:T(1024)(128)(4,1)S(1)}, s32[]{:S(2)}) async-start(s8[6291456]{0:T(1024)(128)(4,1)} %bitcast.28), calls=%async_computation.6 | async-start | bytes 8388608
  235.9 112.9 %slice-start.2 = ((s8[6291456]{0:T(1024)(128)(4,1)}), s8[4194304]{0:T(1024)(128)(4,1)S(1)}, s32[]{:S(2)}) async-start(s8[6291456]{0:T(1024)(128)(4,1)} %bitcast.30), calls=%async_computation.8 | async-start | bytes 8388608
  355.2 56.8 %all-to-all-start.5 = ((bf16[16,136,512]{2,1,0:T(8,128)(2,1)}), bf16[16,136,512]{2,1,0:T(8,128)(2,1)}, u32[]{:S(2)}, u32[]{:S(2)}) async-start(bf16[16,136,512]{2,1,0:T(8,128)(2,1)} %expert_backward.1), calls=%async_computation.5 | async-start | bytes 4456448 | tf_op jit(solution)/shard_map/all_to_all | solution.py:493
  360.9 13.6 %collective-permute-start.12 = (bf16[16,136,512]{2,1,0:T(8,128)(2,1)}, bf16[16,136,512]{2,1,0:T(8,128)(2,1)S(1)}, u32[]{:S(2)}, u32[]{:S(2)}) collective-permute-start(bf16[16,136,512]{2,1,0:T(8,128)(2,1)} %copy-done.11), channel_id=1, source_target_pairs={{0,16},{1,17},{2,18},{3,19},{4,20},{5,21},{6,22},{7,23},{8,24},{9,... | collective-permute-start | bytes 6684680 | tf_op jit(solution)/shard_map/ppermute | solution.py:597
  362.5 12.8 %collective-permute-start.10 = (bf16[16,136,512]{2,1,0:T(8,128)(2,1)S(1)}, bf16[16,136,512]{2,1,0:T(8,128)(2,1)S(1)}, u32[]{:S(2)}, u32[]{:S(2)}) collective-permute-start(bf16[16,136,512]{2,1,0:T(8,128)(2,1)S(1)} %all_to_all.31.refs_1_.received), channel_id=1, source_target_pairs={{16,0},{17,1},{18,2},{19,3},{20,4},{21,5},{22,6},{23,7},{24,8},{25... | collective-permute-start | bytes 6684680 | tf_op jit(solution)/shard_map/ppermute | solution.py:597
  367.0 5.7 %collective-permute-start.13 = (bf16[112,4096]{1,0:T(8,128)(2,1)S(1)}, bf16[112,4096]{1,0:T(8,128)(2,1)S(1)}, u32[]{:S(2)}, u32[]{:S(2)}) collective-permute-start(bf16[112,4096]{1,0:T(8,128)(2,1)S(1)} %get-tuple-element.67.grad.incoming), channel_id=1, source_target_pairs={{0,16},{1,17},{2,18},{3,19},{4,20},{5,21},{6,22},{7,23},{8,24},{9,... | collective-permute-start | bytes 2752520 | tf_op jit(solution)/shard_map/ppermute | solution.py:603
  368.3 6.2 %collective-permute-start.9 = (bf16[272,768]{1,0:T(8,128)(2,1)}, bf16[272,768]{1,0:T(8,128)(2,1)S(1)}, u32[]{:S(2)}, u32[]{:S(2)}) collective-permute-start(bf16[272,768]{1,0:T(8,128)(2,1)} %copy-done.20), channel_id=1, source_target_pairs={{16,0},{17,1},{18,2},{19,3},{20,4},{21,5},{22,6},{23,7},{24,8},{25... | collective-permute-start | bytes 1253384 | tf_op jit(solution)/shard_map/ppermute | solution.py:597
  371.4 3.9 collective-permute-start.11
  416.9 6.0 %collective-permute-start.14 = (bf16[112,4096]{1,0:T(8,128)(2,1)}, bf16[112,4096]{1,0:T(8,128)(2,1)S(1)}, u32[]{:S(2)}, u32[]{:S(2)}) collective-permute-start(bf16[112,4096]{1,0:T(8,128)(2,1)} %get-tuple-element.75), channel_id=1, source_target_pairs={{16,0},{17,1},{18,2},{19,3},{20,4},{21,5},{22,6},{23,7},{24,8},{25... | collective-permute-start | bytes 2752520 | tf_op jit(solution)/shard_map/ppermute | solution.py:617
  (43 other events, 647.3 us)

commit v6 on v5

--- a/solution.py
+++ b/solution.py
@@ -400,7 +400,8 @@
         copy.wait()
     for sender in range(sizes.experts):
         partner = pick[1] ^ sender
-        received[sender] = here[(partner % count) * PLANES + partner // count]
+        plane = partner // count
+        received[sender] = here[(partner % count) * PLANES + (plane ^ plane // 2)]
     back_out[...] = through_down_back(sizes, received, down)
 
 
@@ -549,7 +550,11 @@
         [plane] * PLANES, (), [SMEM, VMEM, VMEM],
     )
     last = PLANES - 1
-    near = [to_partner(planes[number], number * sizes.in_plane) for number in range(last)]
+    planes = [planes[number ^ number // 2] for number in range(PLANES)]
+    near = [
+        to_partner(planes[number], (number ^ number // 2) * sizes.in_plane)
+        for number in range(last)
+    ]
     hidden_0, activated_0, answer_0 = call(
         kernel(forward_kernel), "expert_forward", [in_0, up_0, down_0],
         [wide_hidden, activated, message],
@@ -562,7 +567,7 @@
     places = [to_partner(piece, number) for number, piece in enumerate(places)]
     (far,) = call(far_kernel, "far_plane", places, [plane])
     _, returned_0 = lax.optimization_barrier((far, returned_0))
-    far = to_partner(far, last * sizes.in_plane)
+    far = to_partner(far, (last ^ last // 2) * sizes.in_plane)
     carried_1, out_1 = call(
         kernel(middle_kernel), "combine_send", [clip, returned_0, table_0, across_1],
         [home_rows, message],

time: 426 us -> 422 us (level)
    all_to_all x4, waiting for transfers between devices: 77.4 us -> 86 us  [exchange(): lax.all_to_all(message, 'expert', split_axis=0, concat_axis=0, tiled=True)]
    ppermute x6, waiting for transfers between devices: 64.6 us -> 56.5 us  [to_partner(): lax.ppermute(piece, 'expert', [(source, source ^ number) for source in ra...]
  transfers between devices with their start and end apart: 19 -> 19, of which waited for: 13 -> 14; matrix products, arithmetic and copies ran while one was open for 1% -> 1% of each run, Pallas kernels for 9% -> 10%
where the time goes in v6:
time: 422 us; the launch traced here: 421 us
  waiting for transfers between devices  154 us (36%)
  blocking collectives  110 us (26%)
  Pallas kernels  60.3 us (14%)
  starting transfers between devices  50.6 us (12%)
  local copies, waits for them, and re-layouts  44 us (10%)
    all_to_all x2, blocking collectives, exchange(): lax.all_to_all(message, 'expert', split_axis=0, concat_axis=0, tiled=True)  110 us
    all_to_all x4, waiting for transfers between devices, exchange(): lax.all_to_all(message, 'expert', split_axis=0, concat_axis=0, tiled=True)  86 us
    pallas_call x15, Pallas kernels, call(): pl.pallas_call(kernel, name=name, in_specs=specs or [VMEM] * len(operands...  60.3 us
    ppermute x6, waiting for transfers between devices, to_partner(): lax.ppermute(piece, 'expert', [(source, source ^ number) for source in ra...  56.5 us
    unnamed x98, local copies, waits for them, and re-layouts  41.5 us
    all_to_all x4, starting transfers between devices, exchange(): lax.all_to_all(message, 'expert', split_axis=0, concat_axis=0, tiled=True)  25.1 us
    ppermute x4, starting transfers between devices, shards(): operands += near + [lax.ppermute(array, 'pipe', way) for array in near]  10.5 us
    ppermute x6, starting transfers between devices, to_partner(): lax.ppermute(piece, 'expert', [(source, source ^ number) for source in ra...  8.66 us
  transfers between devices with their start and end apart: 19, of which 14 were waited for; matrix products, arithmetic and copies ran while one was open for 1% of the time, Pallas kernels for 10%

profile of v6, /device:TPU:13, one launch (start us, length us, event | category | flops | bytes accessed | tf_op | source)
XLA Modules:
  0.0 420.8 jit_solution(12248332229079171123)
XLA Ops:
  7.3 6.6 %all-to-all-start = ((bf16[16,136,512]{2,1,0:T(8,128)(2,1)}), bf16[16,136,512]{2,1,0:T(8,128)(2,1)S(1)}, u32[]{:S(2)}, u32[]{:S(2)}) async-start(bf16[16,136,512]{2,1,0:T(8,128)(2,1)} %copy-done.2), calls=%async_computation | async-start | bytes 4456448 | tf_op jit(solution)/shard_map/all_to_all | solution.py:494
  16.2 7.2 %collective-permute-done.2.down_other = bf16[768,4096]{1,0:T(8,128)(2,1)} collective-permute-done((bf16[768,4096]{1,0:T(8,128)(2,1)}, bf16[768,4096]{1,0:T(8,128)(2,1)}, u32[]{:S(2)}, u32[]{:S(2)}) %collective-permute-start.2) | collective-permute-done | bytes 6291488 | tf_op jit(solution)/shard_map/ppermute | solution.py:523
  26.2 7.1 %weights.1 = (bf16[4096,768]{1,0:T(8,128)(2,1)S(1)}, bf16[768,4096]{1,0:T(8,128)(2,1)S(1)}, bf16[4096,768]{1,0:T(8,128)(2,1)S(1)}, bf16[768,4096]{1,0:T(8,128)(2,1)S(1)}) custom-call(s32[2]{0:T(128)S(1)} %pad_add_fusion.pick, bf16[4096,768]{1,0:T(8,128)(2,1)S(1)} %bitcast.27, bf16[768,4096]{1,0:T(8,128)(2,1)} %bitcast.36, ...), custom_call_target="tpu_custom_call" | custom-call | flops 8049999872 | tf_op jit(solution)/shard_map/weights/pallas_call | solution.py:476
  52.8 11.8 %all-to-all-done.received = bf16[16,136,512]{2,1,0:T(8,128)(2,1)S(1)} async-done(((bf16[16,136,512]{2,1,0:T(8,128)(2,1)}), bf16[16,136,512]{2,1,0:T(8,128)(2,1)S(1)}, u32[]{:S(2)}, u32[]{:S(2)}) %all-to-all-start) | async-done | bytes 2228256 | tf_op jit(solution)/shard_map/all_to_all | solution.py:494
  70.1 6.4 %expert_forward.1 = (f32[272,768]{1,0:T(8,128)S(1)}, bf16[272,768]{1,0:T(8,128)(2,1)S(1)}, bf16[16,136,512]{2,1,0:T(8,128)(2,1)}) custom-call(bf16[16,136,512]{2,1,0:T(8,128)(2,1)S(1)} %all-to-all-done.received, bf16[4096,768]{1,0:T(8,128)(2,1)S(1)} %copy-done.25, bf16[768,4096]{1,0:T(8,128)(2,1)S(1)} %copy-done.27), custom_call_target="tpu_custom_call" | custom-call | flops 6899999744 | tf_op jit(solution)/shard_map/expert_forward/pallas_call | solution.py:476
  82.3 6.4 %collective-permute-done.4.refs_2_ = bf16[4,136,512]{2,1,0:T(8,128)(2,1)} collective-permute-done((bf16[4,136,512]{2,1,0:T(8,128)(2,1)}, bf16[4,136,512]{2,1,0:T(8,128)(2,1)}, u32[]{:S(2)}, u32[]{:S(2)}) %collective-permute-start.4) | collective-permute-done | bytes 557088 | tf_op jit(solution)/shard_map/ppermute | solution.py:501
  88.7 4.2 %all-to-all-start.1 = ((bf16[16,136,512]{2,1,0:T(8,128)(2,1)}), bf16[16,136,512]{2,1,0:T(8,128)(2,1)S(1)}, u32[]{:S(2)}, u32[]{:S(2)}) async-start(bf16[16,136,512]{2,1,0:T(8,128)(2,1)} %get-tuple-element.58), calls=%async_computation.1 | async-start | bytes 4456448 | tf_op jit(solution)/shard_map/all_to_all | solution.py:494
  99.1 13.6 %collective-permute-done.5.refs_1_ = bf16[4,136,512]{2,1,0:T(8,128)(2,1)S(1)} collective-permute-done((bf16[4,136,512]{2,1,0:T(8,128)(2,1)S(1)}, bf16[4,136,512]{2,1,0:T(8,128)(2,1)S(1)}, u32[]{:S(2)}, u32[]{:S(2)}) %collective-permute-start.5) | collective-permute-done | bytes 557088 | tf_op jit(solution)/shard_map/ppermute | solution.py:501
  112.7 15.6 %collective-permute-done.6.refs_2_ = bf16[4,136,512]{2,1,0:T(8,128)(2,1)S(1)} collective-permute-done((bf16[4,136,512]{2,1,0:T(8,128)(2,1)S(1)}, bf16[4,136,512]{2,1,0:T(8,128)(2,1)S(1)}, u32[]{:S(2)}, u32[]{:S(2)}) %collective-permute-start.6) | collective-permute-done | bytes 557088 | tf_op jit(solution)/shard_map/ppermute | solution.py:501
  128.3 7.3 %collective-permute-done.7.refs_3_ = bf16[4,136,512]{2,1,0:T(8,128)(2,1)S(1)} collective-permute-done((bf16[4,136,512]{2,1,0:T(8,128)(2,1)S(1)}, bf16[4,136,512]{2,1,0:T(8,128)(2,1)S(1)}, u32[]{:S(2)}, u32[]{:S(2)}) %collective-permute-start.7) | collective-permute-done | bytes 557088 | tf_op jit(solution)/shard_map/ppermute | solution.py:501
  140.0 11.0 %all-to-all-done.1.answer = bf16[16,136,512]{2,1,0:T(8,128)(2,1)S(1)} async-done(((bf16[16,136,512]{2,1,0:T(8,128)(2,1)}), bf16[16,136,512]{2,1,0:T(8,128)(2,1)S(1)}, u32[]{:S(2)}, u32[]{:S(2)}) %all-to-all-start.1) | async-done | bytes 2228256 | tf_op jit(solution)/shard_map/all_to_all | solution.py:494
  154.5 9.7 %collective-permute-done.8.refs_4_ = bf16[4,136,512]{2,1,0:T(8,128)(2,1)} collective-permute-done((bf16[4,136,512]{2,1,0:T(8,128)(2,1)}, bf16[4,136,512]{2,1,0:T(8,128)(2,1)}, u32[]{:S(2)}, u32[]{:S(2)}) %collective-permute-start.8) | collective-permute-done | bytes 557088 | tf_op jit(solution)/shard_map/ppermute | solution.py:501
  164.2 8.6 %all-to-all-start.2 = ((bf16[16,136,512]{2,1,0:T(8,128)(2,1)}), bf16[16,136,512]{2,1,0:T(8,128)(2,1)S(1)}, u32[]{:S(2)}, u32[]{:S(2)}) async-start(bf16[16,136,512]{2,1,0:T(8,128)(2,1)} %copy-done.3), calls=%async_computation.2 | async-start | bytes 4456448 | tf_op jit(solution)/shard_map/all_to_all | solution.py:494
  178.7 4.6 %hidden_back.1 = (f32[272,768]{1,0:T(8,128)S(1)}, bf16[16,136,512]{2,1,0:T(8,128)(2,1)S(1)}) custom-call(s32[2]{0:T(128)S(1)} %pad_add_fusion.pick, bf16[768,4096]{1,0:T(8,128)(2,1)S(1)} %copy-done.31, bf16[4,136,512]{2,1,0:T(8,128)(2,1)S(1)} %copy-done.33, bf16[4,136,512]{2,1,0:T(8,128)(2,1)S(1)} %copy-done.15, bf16[4,136,512]{2,1,0:T(8,128)(2,1)S(1)} %copy-done.17, ...), custom_call_target="tpu_custom_call" | custom-call | flops 5750000128 | tf_op jit(solution)/shard_map/hidden_back/pallas_call | solution.py:476
  185.6 37.7 %all-to-all-done.2.received = bf16[16,136,512]{2,1,0:T(8,128)(2,1)S(1)} async-done(((bf16[16,136,512]{2,1,0:T(8,128)(2,1)}), bf16[16,136,512]{2,1,0:T(8,128)(2,1)S(1)}, u32[]{:S(2)}, u32[]{:S(2)}) %all-to-all-start.2) | async-done | bytes 2228256 | tf_op jit(solution)/shard_map/all_to_all | solution.py:494
  227.2 5.0 %expert_turn.1 = (bf16[272,768]{1,0:T(8,128)(2,1)S(1)}, bf16[16,136,512]{2,1,0:T(8,128)(2,1)S(1)}) custom-call(bf16[16,136,512]{2,1,0:T(8,128)(2,1)S(1)} %all-to-all-done.2.received, f32[272,768]{1,0:T(8,128)S(1)} %copy-done.41, bf16[4096,768]{1,0:T(8,128)(2,1)S(1)} %copy-done.29), custom_call_target="tpu_custom_call" | custom-call | flops 6899999744 | tf_op jit(solution)/shard_map/expert_turn/pallas_call | solution.py:476
  232.3 54.5 %all_to_all.30.answer = bf16[16,136,512]{2,1,0:T(8,128)(2,1)S(1)} all-to-all(bf16[16,136,512]{2,1,0:T(8,128)(2,1)S(1)} %get-tuple-element.66), channel_id=1, replica_groups=mesh['pipe'=2,'expert'=16] {'expert'}, dimensions={0} | all-to-all | bytes 4456448 | tf_op jit(solution)/shard_map/all_to_all | solution.py:494
  290.0 55.1 %all_to_all.31.refs_1_.received = bf16[16,136,512]{2,1,0:T(8,128)(2,1)S(1)} all-to-all(bf16[16,136,512]{2,1,0:T(8,128)(2,1)S(1)} %get-tuple-element.69), channel_id=1, replica_groups=mesh['pipe'=2,'expert'=16] {'expert'}, dimensions={0} | all-to-all | bytes 4456448 | tf_op jit(solution)/shard_map/all_to_all | solution.py:494
  345.2 6.3 %expert_backward.1 = bf16[16,136,512]{2,1,0:T(8,128)(2,1)} custom-call(bf16[16,136,512]{2,1,0:T(8,128)(2,1)S(1)} %all_to_all.31.refs_1_.received, f32[272,768]{1,0:T(8,128)S(1)} %copy-done.35, bf16[4096,768]{1,0:T(8,128)(2,1)S(1)} %bitcast.29, bf16[768,4096]{1,0:T(8,128)(2,1)S(1)} %bitcast.31), custom_call_target="tpu_custom_call" | custom-call | flops 6899999744 | tf_op jit(solution)/shard_map/expert_backward/pallas_call | solution.py:476
  351.6 5.7 %all-to-all-start.5 = ((bf16[16,136,512]{2,1,0:T(8,128)(2,1)}), bf16[16,136,512]{2,1,0:T(8,128)(2,1)}, u32[]{:S(2)}, u32[]{:S(2)}) async-start(bf16[16,136,512]{2,1,0:T(8,128)(2,1)} %expert_backward.1), calls=%async_computation.5 | async-start | bytes 4456448 | tf_op jit(solution)/shard_map/all_to_all | solution.py:494
  358.8 4.5 %collective-permute-start.10 = (bf16[16,136,512]{2,1,0:T(8,128)(2,1)S(1)}, bf16[16,136,512]{2,1,0:T(8,128)(2,1)S(1)}, u32[]{:S(2)}, u32[]{:S(2)}) collective-permute-start(bf16[16,136,512]{2,1,0:T(8,128)(2,1)S(1)} %all_to_all.31.refs_1_.received), channel_id=1, source_target_pairs={{16,0},{17,1},{18,2},{19,3},{20,4},{21,5},{22,6},{23,7},{24,8},{25... | collective-permute-start | bytes 6684680 | tf_op jit(solution)/shard_map/ppermute | solution.py:602
  371.7 11.1 %down_grad.1 = bf16[768,4096]{1,0:T(8,128)(2,1)} custom-call(s32[2]{0:T(128)S(1)} %pad_add_fusion.pick, bf16[272,768]{1,0:T(8,128)(2,1)S(1)} %copy-done.21, bf16[16,136,512]{2,1,0:T(8,128)(2,1)S(1)} %all_to_all.31.refs_1_.received, bf16[272,768]{1,0:T(8,128)(2,1)S(1)} %collective-permute-done.9.refs_2_, ...), custom_call_target="tpu_custom_call" | custom-call | flops 12650000384 | tf_op jit(solution)/shard_map/down_grad/pallas_call | solution.py:476
  382.8 25.6 %all-to-all-done.5.answer_far = bf16[16,136,512]{2,1,0:T(8,128)(2,1)} async-done(((bf16[16,136,512]{2,1,0:T(8,128)(2,1)}), bf16[16,136,512]{2,1,0:T(8,128)(2,1)}, u32[]{:S(2)}, u32[]{:S(2)}) %all-to-all-start.5) | async-done | bytes 2228256 | tf_op jit(solution)/shard_map/all_to_all | solution.py:494
  408.3 4.9 %norm_back_last.1 = (bf16[112,4096]{1,0:T(8,128)(2,1)}, bf16[2,112,4096]{2,1,0:T(8,128)(2,1)}) custom-call(s32[2]{0:T(128)} %copy-done.8, bf16[112,4096]{1,0:T(8,128)(2,1)} %copy-done.4, bf16[112,4096]{1,0:T(8,128)(2,1)} %copy-done.13, bf16[16,136,512]{2,1,0:T(8,128)(2,1)} %all-to-all-done.5.answer_far, ...), custom_call_target="tpu_custom_call", output_to_operand_aliasing={{1}: (5, {})} | custom-call | flops 6899999744 | tf_op jit(solution)/shard_map/norm_back_last/pallas_call | solution.py:476
  (140 shorter events, 89.2 us)
Async XLA Ops:
  2.3 1.6 collective-permute-start
  3.9 12.3 %collective-permute-start.1 = (bf16[4096,768]{1,0:T(8,128)(2,1)}, bf16[4096,768]{1,0:T(8,128)(2,1)}, u32[]{:S(2)}, u32[]{:S(2)}) collective-permute-start(bf16[4096,768]{1,0:T(8,128)(2,1)} %bitcast.26), channel_id=1, source_target_pairs={{0,16},{16,0},{1,17},{17,1},{2,18},{18,2},{3,19},{19,3},{4,20},{20... | collective-permute-start | bytes 18874376 | tf_op jit(solution)/shard_map/ppermute | solution.py:522
  4.3 19.1 %collective-permute-start.2 = (bf16[768,4096]{1,0:T(8,128)(2,1)}, bf16[768,4096]{1,0:T(8,128)(2,1)}, u32[]{:S(2)}, u32[]{:S(2)}) collective-permute-start(bf16[768,4096]{1,0:T(8,128)(2,1)} %bitcast.35), channel_id=1, source_target_pairs={{0,16},{16,0},{1,17},{17,1},{2,18},{18,2},{3,19},{19,3},{4,20},{20... | collective-permute-start | bytes 18874376 | tf_op jit(solution)/shard_map/ppermute | solution.py:523
  4.6 146.4 %copy-start.4 = (bf16[112,4096]{1,0:T(8,128)(2,1)}, bf16[112,4096]{1,0:T(8,128)(2,1)S(1)}, u32[]{:S(2)}) copy-start(bf16[112,4096]{1,0:T(8,128)(2,1)S(1)} %dynamic-slice_bitcast_fusion.1.carried.before) | copy-start | bytes 2752516
  4.6 146.3 %copy-start.7 = (f32[4,112]{0,1:T(8,128)}, f32[4,112]{0,1:T(8,128)S(1)}, u32[]{:S(2)}) copy-start(f32[4,112]{0,1:T(8,128)S(1)} %get-tuple-element.78) | copy-start | bytes 5380
  7.3 57.2 %all-to-all-start = ((bf16[16,136,512]{2,1,0:T(8,128)(2,1)}), bf16[16,136,512]{2,1,0:T(8,128)(2,1)S(1)}, u32[]{:S(2)}, u32[]{:S(2)}) async-start(bf16[16,136,512]{2,1,0:T(8,128)(2,1)} %copy-done.2), calls=%async_computation | async-start | bytes 4456448 | tf_op jit(solution)/shard_map/all_to_all | solution.py:494
  14.0 357.6 %copy-start.8 = (s32[2]{0:T(128)}, s32[2]{0:T(128)S(1)}, u32[]{:S(2)}) copy-start(s32[2]{0:T(128)S(1)} %pad_add_fusion.pick) | copy-start | bytes 28
  50.2 32.1 %collective-permute-start.3 = (bf16[4,136,512]{2,1,0:T(8,128)(2,1)}, bf16[4,136,512]{2,1,0:T(8,128)(2,1)}, u32[]{:S(2)}, u32[]{:S(2)}) collective-permute-start(bf16[4,136,512]{2,1,0:T(8,128)(2,1)} %get-tuple-element.45), channel_id=1, source_target_pairs={{0,4},{1,5},{2,6},{3,7},{4,0},{5,1},{6,2},{7,3},{8,12},{9,13},{10,... | collective-permute-start | bytes 1671176 | tf_op jit(solution)/shard_map/ppermute | solution.py:501
  50.4 38.3 %collective-permute-start.4 = (bf16[4,136,512]{2,1,0:T(8,128)(2,1)}, bf16[4,136,512]{2,1,0:T(8,128)(2,1)}, u32[]{:S(2)}, u32[]{:S(2)}) collective-permute-start(bf16[4,136,512]{2,1,0:T(8,128)(2,1)} %get-tuple-element.46), channel_id=1, source_target_pairs={{0,12},{1,13},{2,14},{3,15},{4,8},{5,9},{6,10},{7,11},{8,4},{9,5},... | collective-permute-start | bytes 1671176 | tf_op jit(solution)/shard_map/ppermute | solution.py:501
  88.7 62.3 %all-to-all-start.1 = ((bf16[16,136,512]{2,1,0:T(8,128)(2,1)}), bf16[16,136,512]{2,1,0:T(8,128)(2,1)S(1)}, u32[]{:S(2)}, u32[]{:S(2)}) async-start(bf16[16,136,512]{2,1,0:T(8,128)(2,1)} %get-tuple-element.58), calls=%async_computation.1 | async-start | bytes 4456448 | tf_op jit(solution)/shard_map/all_to_all | solution.py:494
  96.4 16.3 %collective-permute-start.5 = (bf16[4,136,512]{2,1,0:T(8,128)(2,1)S(1)}, bf16[4,136,512]{2,1,0:T(8,128)(2,1)S(1)}, u32[]{:S(2)}, u32[]{:S(2)}) collective-permute-start(bf16[4,136,512]{2,1,0:T(8,128)(2,1)S(1)} %get-tuple-element.55), channel_id=1, source_target_pairs={{0,1},{1,0},{2,3},{3,2},{4,5},{5,4},{6,7},{7,6},{8,9},{9,8},{10,11... | collective-permute-start | bytes 1671176 | tf_op jit(solution)/shard_map/ppermute | solution.py:501
  97.6 30.6 %collective-permute-start.6 = (bf16[4,136,512]{2,1,0:T(8,128)(2,1)S(1)}, bf16[4,136,512]{2,1,0:T(8,128)(2,1)S(1)}, u32[]{:S(2)}, u32[]{:S(2)}) collective-permute-start(bf16[4,136,512]{2,1,0:T(8,128)(2,1)S(1)} %get-tuple-element.56), channel_id=1, source_target_pairs={{0,2},{1,3},{2,0},{3,1},{4,6},{5,7},{6,4},{7,5},{8,10},{9,11},{10,... | collective-permute-start | bytes 1671176 | tf_op jit(solution)/shard_map/ppermute | solution.py:501
  97.9 37.6 %collective-permute-start.7 = (bf16[4,136,512]{2,1,0:T(8,128)(2,1)S(1)}, bf16[4,136,512]{2,1,0:T(8,128)(2,1)S(1)}, u32[]{:S(2)}, u32[]{:S(2)}) collective-permute-start(bf16[4,136,512]{2,1,0:T(8,128)(2,1)S(1)} %get-tuple-element.57), channel_id=1, source_target_pairs={{0,3},{1,2},{2,1},{3,0},{4,7},{5,6},{6,5},{7,4},{8,11},{9,10},{10,... | collective-permute-start | bytes 1671176 | tf_op jit(solution)/shard_map/ppermute | solution.py:501
  136.5 27.6 %collective-permute-start.8 = (bf16[4,136,512]{2,1,0:T(8,128)(2,1)}, bf16[4,136,512]{2,1,0:T(8,128)(2,1)}, u32[]{:S(2)}, u32[]{:S(2)}) collective-permute-start(bf16[4,136,512]{2,1,0:T(8,128)(2,1)} %far_plane.1), channel_id=1, source_target_pairs={{0,8},{1,9},{2,10},{3,11},{4,12},{5,13},{6,14},{7,15},{8,0},{9,1},... | collective-permute-start | bytes 1671176 | tf_op jit(solution)/shard_map/ppermute | solution.py:501
  164.2 59.1 %all-to-all-start.2 = ((bf16[16,136,512]{2,1,0:T(8,128)(2,1)}), bf16[16,136,512]{2,1,0:T(8,128)(2,1)S(1)}, u32[]{:S(2)}, u32[]{:S(2)}) async-start(bf16[16,136,512]{2,1,0:T(8,128)(2,1)} %copy-done.3), calls=%async_computation.2 | async-start | bytes 4456448 | tf_op jit(solution)/shard_map/all_to_all | solution.py:494
  232.3 112.9 %slice-start = ((s8[6291456]{0:T(1024)(128)(4,1)}), s8[4194304]{0:T(1024)(128)(4,1)S(1)}, s32[]{:S(2)}) async-start(s8[6291456]{0:T(1024)(128)(4,1)} %bitcast.28), calls=%async_computation.6 | async-start | bytes 8388608
  232.3 112.9 %slice-start.2 = ((s8[6291456]{0:T(1024)(128)(4,1)}), s8[4194304]{0:T(1024)(128)(4,1)S(1)}, s32[]{:S(2)}) async-start(s8[6291456]{0:T(1024)(128)(4,1)} %bitcast.30), calls=%async_computation.8 | async-start | bytes 8388608
  351.6 56.8 %all-to-all-start.5 = ((bf16[16,136,512]{2,1,0:T(8,128)(2,1)}), bf16[16,136,512]{2,1,0:T(8,128)(2,1)}, u32[]{:S(2)}, u32[]{:S(2)}) async-start(bf16[16,136,512]{2,1,0:T(8,128)(2,1)} %expert_backward.1), calls=%async_computation.5 | async-start | bytes 4456448 | tf_op jit(solution)/shard_map/all_to_all | solution.py:494
  357.3 13.6 %collective-permute-start.12 = (bf16[16,136,512]{2,1,0:T(8,128)(2,1)}, bf16[16,136,512]{2,1,0:T(8,128)(2,1)S(1)}, u32[]{:S(2)}, u32[]{:S(2)}) collective-permute-start(bf16[16,136,512]{2,1,0:T(8,128)(2,1)} %copy-done.11), channel_id=1, source_target_pairs={{0,16},{1,17},{2,18},{3,19},{4,20},{5,21},{6,22},{7,23},{8,24},{9,... | collective-permute-start | bytes 6684680 | tf_op jit(solution)/shard_map/ppermute | solution.py:602
  358.8 12.8 %collective-permute-start.10 = (bf16[16,136,512]{2,1,0:T(8,128)(2,1)S(1)}, bf16[16,136,512]{2,1,0:T(8,128)(2,1)S(1)}, u32[]{:S(2)}, u32[]{:S(2)}) collective-permute-start(bf16[16,136,512]{2,1,0:T(8,128)(2,1)S(1)} %all_to_all.31.refs_1_.received), channel_id=1, source_target_pairs={{16,0},{17,1},{18,2},{19,3},{20,4},{21,5},{22,6},{23,7},{24,8},{25... | collective-permute-start | bytes 6684680 | tf_op jit(solution)/shard_map/ppermute | solution.py:602
  363.4 5.7 %collective-permute-start.13 = (bf16[112,4096]{1,0:T(8,128)(2,1)S(1)}, bf16[112,4096]{1,0:T(8,128)(2,1)S(1)}, u32[]{:S(2)}, u32[]{:S(2)}) collective-permute-start(bf16[112,4096]{1,0:T(8,128)(2,1)S(1)} %get-tuple-element.67.grad.incoming), channel_id=1, source_target_pairs={{0,16},{1,17},{2,18},{3,19},{4,20},{5,21},{6,22},{7,23},{8,24},{9,... | collective-permute-start | bytes 2752520 | tf_op jit(solution)/shard_map/ppermute | solution.py:608
  364.7 6.2 %collective-permute-start.9 = (bf16[272,768]{1,0:T(8,128)(2,1)}, bf16[272,768]{1,0:T(8,128)(2,1)S(1)}, u32[]{:S(2)}, u32[]{:S(2)}) collective-permute-start(bf16[272,768]{1,0:T(8,128)(2,1)} %copy-done.20), channel_id=1, source_target_pairs={{16,0},{17,1},{18,2},{19,3},{20,4},{21,5},{22,6},{23,7},{24,8},{25... | collective-permute-start | bytes 1253384 | tf_op jit(solution)/shard_map/ppermute | solution.py:602
  367.8 3.9 collective-permute-start.11
  413.3 6.0 %collective-permute-start.14 = (bf16[112,4096]{1,0:T(8,128)(2,1)}, bf16[112,4096]{1,0:T(8,128)(2,1)S(1)}, u32[]{:S(2)}, u32[]{:S(2)}) collective-permute-start(bf16[112,4096]{1,0:T(8,128)(2,1)} %get-tuple-element.75), channel_id=1, source_target_pairs={{16,0},{17,1},{18,2},{19,3},{20,4},{21,5},{22,6},{23,7},{24,8},{25... | collective-permute-start | bytes 2752520 | tf_op jit(solution)/shard_map/ppermute | solution.py:622
  (43 other events, 636.3 us)

commit v7 on v6

--- a/solution.py
+++ b/solution.py
@@ -270,19 +270,24 @@
 def send_weighted(sizes, incoming, across, pieces, base=0):
     high, low = slots_by_token(sizes, across[...], True, base)
 
+    both = jnp.concatenate([high, low], axis=1)
+
     def values(block):
         rows = incoming[:, span(sizes, block)]
-        return dot(high, rows) + dot(low, rows)
+        return dot(both, jnp.concatenate([rows, rows], axis=0))
 
     write_pieces(sizes, pieces, values)
 
 
 def middle_kernel(sizes, before, answer, table, across, carried, message):
-    high, low = tokens_by_slot(sizes, table[...], True)
+    both = jnp.concatenate(tokens_by_slot(sizes, table[...], True), axis=0)
     rest = read_rest(sizes, answer)
     for block in range(FEATURE_BLOCKS):
         rows = read_block(sizes, answer, rest, block)
-        mixed = before[:, span(sizes, block)].astype(F32) + (dot(high, rows) + dot(low, rows))
+        parts = dot(both, rows)
+        mixed = before[:, span(sizes, block)].astype(F32) + (
+            parts[: sizes.rows] + parts[sizes.rows :]
+        )
         carried[:, span(sizes, block)] = mixed.astype(BF16)
     send_normed(sizes, carried, across, message)
 

time: 422 us -> 421 us (level)
  transfers between devices with their start and end apart: 19 -> 19, of which waited for: 14 -> 14; matrix products, arithmetic and copies ran while one was open for 1% -> 1% of each run, Pallas kernels for 10% -> 9%
where the time goes in v7:
time: 421 us; the launch traced here: 420 us
  waiting for transfers between devices  154 us (37%)
  blocking collectives  110 us (26%)
  Pallas kernels  59.2 us (14%)
  starting transfers between devices  50.4 us (12%)
  local copies, waits for them, and re-layouts  44 us (10%)
    all_to_all x2, blocking collectives, exchange(): lax.all_to_all(message, 'expert', split_axis=0, concat_axis=0, tiled=True)  110 us
    all_to_all x4, waiting for transfers between devices, exchange(): lax.all_to_all(message, 'expert', split_axis=0, concat_axis=0, tiled=True)  86.2 us
    pallas_call x15, Pallas kernels, call(): pl.pallas_call(kernel, name=name, in_specs=specs or [VMEM] * len(operands...  59.2 us
    ppermute x6, waiting for transfers between devices, to_partner(): lax.ppermute(piece, 'expert', [(source, source ^ number) for source in ra...  56.7 us
    unnamed x98, local copies, waits for them, and re-layouts  41.5 us
    all_to_all x4, starting transfers between devices, exchange(): lax.all_to_all(message, 'expert', split_axis=0, concat_axis=0, tiled=True)  24.6 us
    ppermute x4, starting transfers between devices, shards(): operands += near + [lax.ppermute(array, 'pipe', way) for array in near]  10.7 us
    ppermute x6, starting transfers between devices, to_partner(): lax.ppermute(piece, 'expert', [(source, source ^ number) for source in ra...  8.87 us
  transfers between devices with their start and end apart: 19, of which 14 were waited for; matrix products, arithmetic and copies ran while one was open for 1% of the time, Pallas kernels for 9%

profile of v7, /device:TPU:13, one launch (start us, length us, event | category | flops | bytes accessed | tf_op | source)
XLA Modules:
  0.0 420.0 jit_solution(15894370496809060579)
XLA Ops:
  7.3 6.6 %all-to-all-start = ((bf16[16,136,512]{2,1,0:T(8,128)(2,1)}), bf16[16,136,512]{2,1,0:T(8,128)(2,1)S(1)}, u32[]{:S(2)}, u32[]{:S(2)}) async-start(bf16[16,136,512]{2,1,0:T(8,128)(2,1)} %copy-done.2), calls=%async_computation | async-start | bytes 4456448 | tf_op jit(solution)/shard_map/all_to_all | solution.py:499
  16.2 7.2 %collective-permute-done.2.down_other = bf16[768,4096]{1,0:T(8,128)(2,1)} collective-permute-done((bf16[768,4096]{1,0:T(8,128)(2,1)}, bf16[768,4096]{1,0:T(8,128)(2,1)}, u32[]{:S(2)}, u32[]{:S(2)}) %collective-permute-start.2) | collective-permute-done | bytes 6291488 | tf_op jit(solution)/shard_map/ppermute | solution.py:528
  26.2 7.1 %weights.1 = (bf16[4096,768]{1,0:T(8,128)(2,1)S(1)}, bf16[768,4096]{1,0:T(8,128)(2,1)S(1)}, bf16[4096,768]{1,0:T(8,128)(2,1)S(1)}, bf16[768,4096]{1,0:T(8,128)(2,1)S(1)}) custom-call(s32[2]{0:T(128)S(1)} %pad_add_fusion.pick, bf16[4096,768]{1,0:T(8,128)(2,1)S(1)} %bitcast.27, bf16[768,4096]{1,0:T(8,128)(2,1)} %bitcast.36, ...), custom_call_target="tpu_custom_call" | custom-call | flops 8049999872 | tf_op jit(solution)/shard_map/weights/pallas_call | solution.py:481
  52.3 12.3 %all-to-all-done.received = bf16[16,136,512]{2,1,0:T(8,128)(2,1)S(1)} async-done(((bf16[16,136,512]{2,1,0:T(8,128)(2,1)}), bf16[16,136,512]{2,1,0:T(8,128)(2,1)S(1)}, u32[]{:S(2)}, u32[]{:S(2)}) %all-to-all-start) | async-done | bytes 2228256 | tf_op jit(solution)/shard_map/all_to_all | solution.py:499
  70.2 6.4 %expert_forward.1 = (f32[272,768]{1,0:T(8,128)S(1)}, bf16[272,768]{1,0:T(8,128)(2,1)S(1)}, bf16[16,136,512]{2,1,0:T(8,128)(2,1)}) custom-call(bf16[16,136,512]{2,1,0:T(8,128)(2,1)S(1)} %all-to-all-done.received, bf16[4096,768]{1,0:T(8,128)(2,1)S(1)} %copy-done.25, bf16[768,4096]{1,0:T(8,128)(2,1)S(1)} %copy-done.27), custom_call_target="tpu_custom_call" | custom-call | flops 6899999744 | tf_op jit(solution)/shard_map/expert_forward/pallas_call | solution.py:481
  82.1 6.4 %collective-permute-done.4.refs_2_ = bf16[4,136,512]{2,1,0:T(8,128)(2,1)} collective-permute-done((bf16[4,136,512]{2,1,0:T(8,128)(2,1)}, bf16[4,136,512]{2,1,0:T(8,128)(2,1)}, u32[]{:S(2)}, u32[]{:S(2)}) %collective-permute-start.4) | collective-permute-done | bytes 557088 | tf_op jit(solution)/shard_map/ppermute | solution.py:506
  88.5 4.4 %all-to-all-start.1 = ((bf16[16,136,512]{2,1,0:T(8,128)(2,1)}), bf16[16,136,512]{2,1,0:T(8,128)(2,1)S(1)}, u32[]{:S(2)}, u32[]{:S(2)}) async-start(bf16[16,136,512]{2,1,0:T(8,128)(2,1)} %get-tuple-element.58), calls=%async_computation.1 | async-start | bytes 4456448 | tf_op jit(solution)/shard_map/all_to_all | solution.py:499
  99.1 13.4 %collective-permute-done.5.refs_1_ = bf16[4,136,512]{2,1,0:T(8,128)(2,1)S(1)} collective-permute-done((bf16[4,136,512]{2,1,0:T(8,128)(2,1)S(1)}, bf16[4,136,512]{2,1,0:T(8,128)(2,1)S(1)}, u32[]{:S(2)}, u32[]{:S(2)}) %collective-permute-start.5) | collective-permute-done | bytes 557088 | tf_op jit(solution)/shard_map/ppermute | solution.py:506
  112.5 15.9 %collective-permute-done.6.refs_2_ = bf16[4,136,512]{2,1,0:T(8,128)(2,1)S(1)} collective-permute-done((bf16[4,136,512]{2,1,0:T(8,128)(2,1)S(1)}, bf16[4,136,512]{2,1,0:T(8,128)(2,1)S(1)}, u32[]{:S(2)}, u32[]{:S(2)}) %collective-permute-start.6) | collective-permute-done | bytes 557088 | tf_op jit(solution)/shard_map/ppermute | solution.py:506
  128.4 6.9 %collective-permute-done.7.refs_3_ = bf16[4,136,512]{2,1,0:T(8,128)(2,1)S(1)} collective-permute-done((bf16[4,136,512]{2,1,0:T(8,128)(2,1)S(1)}, bf16[4,136,512]{2,1,0:T(8,128)(2,1)S(1)}, u32[]{:S(2)}, u32[]{:S(2)}) %collective-permute-start.7) | collective-permute-done | bytes 557088 | tf_op jit(solution)/shard_map/ppermute | solution.py:506
  140.0 11.0 %all-to-all-done.1.answer = bf16[16,136,512]{2,1,0:T(8,128)(2,1)S(1)} async-done(((bf16[16,136,512]{2,1,0:T(8,128)(2,1)}), bf16[16,136,512]{2,1,0:T(8,128)(2,1)S(1)}, u32[]{:S(2)}, u32[]{:S(2)}) %all-to-all-start.1) | async-done | bytes 2228256 | tf_op jit(solution)/shard_map/all_to_all | solution.py:499
  154.4 10.3 %collective-permute-done.8.refs_4_ = bf16[4,136,512]{2,1,0:T(8,128)(2,1)} collective-permute-done((bf16[4,136,512]{2,1,0:T(8,128)(2,1)}, bf16[4,136,512]{2,1,0:T(8,128)(2,1)}, u32[]{:S(2)}, u32[]{:S(2)}) %collective-permute-start.8) | collective-permute-done | bytes 557088 | tf_op jit(solution)/shard_map/ppermute | solution.py:506
  164.7 8.1 %all-to-all-start.2 = ((bf16[16,136,512]{2,1,0:T(8,128)(2,1)}), bf16[16,136,512]{2,1,0:T(8,128)(2,1)S(1)}, u32[]{:S(2)}, u32[]{:S(2)}) async-start(bf16[16,136,512]{2,1,0:T(8,128)(2,1)} %copy-done.3), calls=%async_computation.2 | async-start | bytes 4456448 | tf_op jit(solution)/shard_map/all_to_all | solution.py:499
  178.7 4.6 %hidden_back.1 = (f32[272,768]{1,0:T(8,128)S(1)}, bf16[16,136,512]{2,1,0:T(8,128)(2,1)S(1)}) custom-call(s32[2]{0:T(128)S(1)} %pad_add_fusion.pick, bf16[768,4096]{1,0:T(8,128)(2,1)S(1)} %copy-done.31, bf16[4,136,512]{2,1,0:T(8,128)(2,1)S(1)} %copy-done.33, bf16[4,136,512]{2,1,0:T(8,128)(2,1)S(1)} %copy-done.15, bf16[4,136,512]{2,1,0:T(8,128)(2,1)S(1)} %copy-done.17, ...), custom_call_target="tpu_custom_call" | custom-call | flops 5750000128 | tf_op jit(solution)/shard_map/hidden_back/pallas_call | solution.py:481
  185.5 37.6 %all-to-all-done.2.received = bf16[16,136,512]{2,1,0:T(8,128)(2,1)S(1)} async-done(((bf16[16,136,512]{2,1,0:T(8,128)(2,1)}), bf16[16,136,512]{2,1,0:T(8,128)(2,1)S(1)}, u32[]{:S(2)}, u32[]{:S(2)}) %all-to-all-start.2) | async-done | bytes 2228256 | tf_op jit(solution)/shard_map/all_to_all | solution.py:499
  227.1 5.0 %expert_turn.1 = (bf16[272,768]{1,0:T(8,128)(2,1)S(1)}, bf16[16,136,512]{2,1,0:T(8,128)(2,1)S(1)}) custom-call(bf16[16,136,512]{2,1,0:T(8,128)(2,1)S(1)} %all-to-all-done.2.received, f32[272,768]{1,0:T(8,128)S(1)} %copy-done.41, bf16[4096,768]{1,0:T(8,128)(2,1)S(1)} %copy-done.29), custom_call_target="tpu_custom_call" | custom-call | flops 6899999744 | tf_op jit(solution)/shard_map/expert_turn/pallas_call | solution.py:481
  232.2 54.7 %all_to_all.30.answer = bf16[16,136,512]{2,1,0:T(8,128)(2,1)S(1)} all-to-all(bf16[16,136,512]{2,1,0:T(8,128)(2,1)S(1)} %get-tuple-element.66), channel_id=1, replica_groups=mesh['pipe'=2,'expert'=16] {'expert'}, dimensions={0} | all-to-all | bytes 4456448 | tf_op jit(solution)/shard_map/all_to_all | solution.py:499
  289.6 55.1 %all_to_all.31.refs_1_.received = bf16[16,136,512]{2,1,0:T(8,128)(2,1)S(1)} all-to-all(bf16[16,136,512]{2,1,0:T(8,128)(2,1)S(1)} %get-tuple-element.69), channel_id=1, replica_groups=mesh['pipe'=2,'expert'=16] {'expert'}, dimensions={0} | all-to-all | bytes 4456448 | tf_op jit(solution)/shard_map/all_to_all | solution.py:499
  344.7 6.3 %expert_backward.1 = bf16[16,136,512]{2,1,0:T(8,128)(2,1)} custom-call(bf16[16,136,512]{2,1,0:T(8,128)(2,1)S(1)} %all_to_all.31.refs_1_.received, f32[272,768]{1,0:T(8,128)S(1)} %copy-done.35, bf16[4096,768]{1,0:T(8,128)(2,1)S(1)} %bitcast.29, bf16[768,4096]{1,0:T(8,128)(2,1)S(1)} %bitcast.31), custom_call_target="tpu_custom_call" | custom-call | flops 6899999744 | tf_op jit(solution)/shard_map/expert_backward/pallas_call | solution.py:481
  351.1 5.5 %all-to-all-start.5 = ((bf16[16,136,512]{2,1,0:T(8,128)(2,1)}), bf16[16,136,512]{2,1,0:T(8,128)(2,1)}, u32[]{:S(2)}, u32[]{:S(2)}) async-start(bf16[16,136,512]{2,1,0:T(8,128)(2,1)} %expert_backward.1), calls=%async_computation.5 | async-start | bytes 4456448 | tf_op jit(solution)/shard_map/all_to_all | solution.py:499
  358.3 4.5 %collective-permute-start.10 = (bf16[16,136,512]{2,1,0:T(8,128)(2,1)S(1)}, bf16[16,136,512]{2,1,0:T(8,128)(2,1)S(1)}, u32[]{:S(2)}, u32[]{:S(2)}) collective-permute-start(bf16[16,136,512]{2,1,0:T(8,128)(2,1)S(1)} %all_to_all.31.refs_1_.received), channel_id=1, source_target_pairs={{16,0},{17,1},{18,2},{19,3},{20,4},{21,5},{22,6},{23,7},{24,8},{25... | collective-permute-start | bytes 6684680 | tf_op jit(solution)/shard_map/ppermute | solution.py:607
  371.1 11.1 %down_grad.1 = bf16[768,4096]{1,0:T(8,128)(2,1)} custom-call(s32[2]{0:T(128)S(1)} %pad_add_fusion.pick, bf16[272,768]{1,0:T(8,128)(2,1)S(1)} %copy-done.21, bf16[16,136,512]{2,1,0:T(8,128)(2,1)S(1)} %all_to_all.31.refs_1_.received, bf16[272,768]{1,0:T(8,128)(2,1)S(1)} %collective-permute-done.9.refs_2_, ...), custom_call_target="tpu_custom_call" | custom-call | flops 12650000384 | tf_op jit(solution)/shard_map/down_grad/pallas_call | solution.py:481
  382.3 25.3 %all-to-all-done.5.answer_far = bf16[16,136,512]{2,1,0:T(8,128)(2,1)} async-done(((bf16[16,136,512]{2,1,0:T(8,128)(2,1)}), bf16[16,136,512]{2,1,0:T(8,128)(2,1)}, u32[]{:S(2)}, u32[]{:S(2)}) %all-to-all-start.5) | async-done | bytes 2228256 | tf_op jit(solution)/shard_map/all_to_all | solution.py:499
  407.6 4.9 %norm_back_last.1 = (bf16[112,4096]{1,0:T(8,128)(2,1)}, bf16[2,112,4096]{2,1,0:T(8,128)(2,1)}) custom-call(s32[2]{0:T(128)} %copy-done.8, bf16[112,4096]{1,0:T(8,128)(2,1)} %copy-done.4, bf16[112,4096]{1,0:T(8,128)(2,1)} %copy-done.13, bf16[16,136,512]{2,1,0:T(8,128)(2,1)} %all-to-all-done.5.answer_far, ...), custom_call_target="tpu_custom_call", output_to_operand_aliasing={{1}: (5, {})} | custom-call | flops 6899999744 | tf_op jit(solution)/shard_map/norm_back_last/pallas_call | solution.py:481
  (140 shorter events, 88.4 us)
Async XLA Ops:
  2.3 1.6 collective-permute-start
  3.9 12.3 %collective-permute-start.1 = (bf16[4096,768]{1,0:T(8,128)(2,1)}, bf16[4096,768]{1,0:T(8,128)(2,1)}, u32[]{:S(2)}, u32[]{:S(2)}) collective-permute-start(bf16[4096,768]{1,0:T(8,128)(2,1)} %bitcast.26), channel_id=1, source_target_pairs={{0,16},{16,0},{1,17},{17,1},{2,18},{18,2},{3,19},{19,3},{4,20},{20... | collective-permute-start | bytes 18874376 | tf_op jit(solution)/shard_map/ppermute | solution.py:527
  4.3 19.1 %collective-permute-start.2 = (bf16[768,4096]{1,0:T(8,128)(2,1)}, bf16[768,4096]{1,0:T(8,128)(2,1)}, u32[]{:S(2)}, u32[]{:S(2)}) collective-permute-start(bf16[768,4096]{1,0:T(8,128)(2,1)} %bitcast.35), channel_id=1, source_target_pairs={{0,16},{16,0},{1,17},{17,1},{2,18},{18,2},{3,19},{19,3},{4,20},{20... | collective-permute-start | bytes 18874376 | tf_op jit(solution)/shard_map/ppermute | solution.py:528
  4.6 146.3 %copy-start.4 = (bf16[112,4096]{1,0:T(8,128)(2,1)}, bf16[112,4096]{1,0:T(8,128)(2,1)S(1)}, u32[]{:S(2)}) copy-start(bf16[112,4096]{1,0:T(8,128)(2,1)S(1)} %dynamic-slice_bitcast_fusion.1.carried.before) | copy-start | bytes 2752516
  4.6 146.3 %copy-start.7 = (f32[4,112]{0,1:T(8,128)}, f32[4,112]{0,1:T(8,128)S(1)}, u32[]{:S(2)}) copy-start(f32[4,112]{0,1:T(8,128)S(1)} %get-tuple-element.78) | copy-start | bytes 5380
  7.3 57.2 %all-to-all-start = ((bf16[16,136,512]{2,1,0:T(8,128)(2,1)}), bf16[16,136,512]{2,1,0:T(8,128)(2,1)S(1)}, u32[]{:S(2)}, u32[]{:S(2)}) async-start(bf16[16,136,512]{2,1,0:T(8,128)(2,1)} %copy-done.2), calls=%async_computation | async-start | bytes 4456448 | tf_op jit(solution)/shard_map/all_to_all | solution.py:499
  14.0 357.1 %copy-start.8 = (s32[2]{0:T(128)}, s32[2]{0:T(128)S(1)}, u32[]{:S(2)}) copy-start(s32[2]{0:T(128)S(1)} %pad_add_fusion.pick) | copy-start | bytes 28
  49.7 32.4 %collective-permute-start.3 = (bf16[4,136,512]{2,1,0:T(8,128)(2,1)}, bf16[4,136,512]{2,1,0:T(8,128)(2,1)}, u32[]{:S(2)}, u32[]{:S(2)}) collective-permute-start(bf16[4,136,512]{2,1,0:T(8,128)(2,1)} %get-tuple-element.45), channel_id=1, source_target_pairs={{0,4},{1,5},{2,6},{3,7},{4,0},{5,1},{6,2},{7,3},{8,12},{9,13},{10,... | collective-permute-start | bytes 1671176 | tf_op jit(solution)/shard_map/ppermute | solution.py:506
  49.9 38.6 %collective-permute-start.4 = (bf16[4,136,512]{2,1,0:T(8,128)(2,1)}, bf16[4,136,512]{2,1,0:T(8,128)(2,1)}, u32[]{:S(2)}, u32[]{:S(2)}) collective-permute-start(bf16[4,136,512]{2,1,0:T(8,128)(2,1)} %get-tuple-element.46), channel_id=1, source_target_pairs={{0,12},{1,13},{2,14},{3,15},{4,8},{5,9},{6,10},{7,11},{8,4},{9,5},... | collective-permute-start | bytes 1671176 | tf_op jit(solution)/shard_map/ppermute | solution.py:506
  88.5 62.4 %all-to-all-start.1 = ((bf16[16,136,512]{2,1,0:T(8,128)(2,1)}), bf16[16,136,512]{2,1,0:T(8,128)(2,1)S(1)}, u32[]{:S(2)}, u32[]{:S(2)}) async-start(bf16[16,136,512]{2,1,0:T(8,128)(2,1)} %get-tuple-element.58), calls=%async_computation.1 | async-start | bytes 4456448 | tf_op jit(solution)/shard_map/all_to_all | solution.py:499
  96.4 16.1 %collective-permute-start.5 = (bf16[4,136,512]{2,1,0:T(8,128)(2,1)S(1)}, bf16[4,136,512]{2,1,0:T(8,128)(2,1)S(1)}, u32[]{:S(2)}, u32[]{:S(2)}) collective-permute-start(bf16[4,136,512]{2,1,0:T(8,128)(2,1)S(1)} %get-tuple-element.55), channel_id=1, source_target_pairs={{0,1},{1,0},{2,3},{3,2},{4,5},{5,4},{6,7},{7,6},{8,9},{9,8},{10,11... | collective-permute-start | bytes 1671176 | tf_op jit(solution)/shard_map/ppermute | solution.py:506
  97.6 30.7 %collective-permute-start.6 = (bf16[4,136,512]{2,1,0:T(8,128)(2,1)S(1)}, bf16[4,136,512]{2,1,0:T(8,128)(2,1)S(1)}, u32[]{:S(2)}, u32[]{:S(2)}) collective-permute-start(bf16[4,136,512]{2,1,0:T(8,128)(2,1)S(1)} %get-tuple-element.56), channel_id=1, source_target_pairs={{0,2},{1,3},{2,0},{3,1},{4,6},{5,7},{6,4},{7,5},{8,10},{9,11},{10,... | collective-permute-start | bytes 1671176 | tf_op jit(solution)/shard_map/ppermute | solution.py:506
  97.9 37.4 %collective-permute-start.7 = (bf16[4,136,512]{2,1,0:T(8,128)(2,1)S(1)}, bf16[4,136,512]{2,1,0:T(8,128)(2,1)S(1)}, u32[]{:S(2)}, u32[]{:S(2)}) collective-permute-start(bf16[4,136,512]{2,1,0:T(8,128)(2,1)S(1)} %get-tuple-element.57), channel_id=1, source_target_pairs={{0,3},{1,2},{2,1},{3,0},{4,7},{5,6},{6,5},{7,4},{8,11},{9,10},{10,... | collective-permute-start | bytes 1671176 | tf_op jit(solution)/shard_map/ppermute | solution.py:506
  136.3 28.3 %collective-permute-start.8 = (bf16[4,136,512]{2,1,0:T(8,128)(2,1)}, bf16[4,136,512]{2,1,0:T(8,128)(2,1)}, u32[]{:S(2)}, u32[]{:S(2)}) collective-permute-start(bf16[4,136,512]{2,1,0:T(8,128)(2,1)} %far_plane.1), channel_id=1, source_target_pairs={{0,8},{1,9},{2,10},{3,11},{4,12},{5,13},{6,14},{7,15},{8,0},{9,1},... | collective-permute-start | bytes 1671176 | tf_op jit(solution)/shard_map/ppermute | solution.py:506
  164.7 58.5 %all-to-all-start.2 = ((bf16[16,136,512]{2,1,0:T(8,128)(2,1)}), bf16[16,136,512]{2,1,0:T(8,128)(2,1)S(1)}, u32[]{:S(2)}, u32[]{:S(2)}) async-start(bf16[16,136,512]{2,1,0:T(8,128)(2,1)} %copy-done.3), calls=%async_computation.2 | async-start | bytes 4456448 | tf_op jit(solution)/shard_map/all_to_all | solution.py:499
  232.2 112.5 %slice-start = ((s8[6291456]{0:T(1024)(128)(4,1)}), s8[4194304]{0:T(1024)(128)(4,1)S(1)}, s32[]{:S(2)}) async-start(s8[6291456]{0:T(1024)(128)(4,1)} %bitcast.28), calls=%async_computation.6 | async-start | bytes 8388608
  232.2 112.5 %slice-start.2 = ((s8[6291456]{0:T(1024)(128)(4,1)}), s8[4194304]{0:T(1024)(128)(4,1)S(1)}, s32[]{:S(2)}) async-start(s8[6291456]{0:T(1024)(128)(4,1)} %bitcast.30), calls=%async_computation.8 | async-start | bytes 8388608
  351.1 56.5 %all-to-all-start.5 = ((bf16[16,136,512]{2,1,0:T(8,128)(2,1)}), bf16[16,136,512]{2,1,0:T(8,128)(2,1)}, u32[]{:S(2)}, u32[]{:S(2)}) async-start(bf16[16,136,512]{2,1,0:T(8,128)(2,1)} %expert_backward.1), calls=%async_computation.5 | async-start | bytes 4456448 | tf_op jit(solution)/shard_map/all_to_all | solution.py:499
  356.5 13.8 %collective-permute-start.12 = (bf16[16,136,512]{2,1,0:T(8,128)(2,1)}, bf16[16,136,512]{2,1,0:T(8,128)(2,1)S(1)}, u32[]{:S(2)}, u32[]{:S(2)}) collective-permute-start(bf16[16,136,512]{2,1,0:T(8,128)(2,1)} %copy-done.11), channel_id=1, source_target_pairs={{0,16},{1,17},{2,18},{3,19},{4,20},{5,21},{6,22},{7,23},{8,24},{9,... | collective-permute-start | bytes 6684680 | tf_op jit(solution)/shard_map/ppermute | solution.py:607
  358.3 12.8 %collective-permute-start.10 = (bf16[16,136,512]{2,1,0:T(8,128)(2,1)S(1)}, bf16[16,136,512]{2,1,0:T(8,128)(2,1)S(1)}, u32[]{:S(2)}, u32[]{:S(2)}) collective-permute-start(bf16[16,136,512]{2,1,0:T(8,128)(2,1)S(1)} %all_to_all.31.refs_1_.received), channel_id=1, source_target_pairs={{16,0},{17,1},{18,2},{19,3},{20,4},{21,5},{22,6},{23,7},{24,8},{25... | collective-permute-start | bytes 6684680 | tf_op jit(solution)/shard_map/ppermute | solution.py:607
  362.8 5.7 %collective-permute-start.13 = (bf16[112,4096]{1,0:T(8,128)(2,1)S(1)}, bf16[112,4096]{1,0:T(8,128)(2,1)S(1)}, u32[]{:S(2)}, u32[]{:S(2)}) collective-permute-start(bf16[112,4096]{1,0:T(8,128)(2,1)S(1)} %get-tuple-element.67.grad.incoming), channel_id=1, source_target_pairs={{0,16},{1,17},{2,18},{3,19},{4,20},{5,21},{6,22},{7,23},{8,24},{9,... | collective-permute-start | bytes 2752520 | tf_op jit(solution)/shard_map/ppermute | solution.py:613
  364.1 6.2 %collective-permute-start.9 = (bf16[272,768]{1,0:T(8,128)(2,1)}, bf16[272,768]{1,0:T(8,128)(2,1)S(1)}, u32[]{:S(2)}, u32[]{:S(2)}) collective-permute-start(bf16[272,768]{1,0:T(8,128)(2,1)} %copy-done.20), channel_id=1, source_target_pairs={{16,0},{17,1},{18,2},{19,3},{20,4},{21,5},{22,6},{23,7},{24,8},{25... | collective-permute-start | bytes 1253384 | tf_op jit(solution)/shard_map/ppermute | solution.py:607
  367.3 3.9 collective-permute-start.11
  412.5 6.0 %collective-permute-start.14 = (bf16[112,4096]{1,0:T(8,128)(2,1)}, bf16[112,4096]{1,0:T(8,128)(2,1)S(1)}, u32[]{:S(2)}, u32[]{:S(2)}) collective-permute-start(bf16[112,4096]{1,0:T(8,128)(2,1)} %get-tuple-element.75), channel_id=1, source_target_pairs={{16,0},{17,1},{18,2},{19,3},{20,4},{21,5},{22,6},{23,7},{24,8},{25... | collective-permute-start | bytes 2752520 | tf_op jit(solution)/shard_map/ppermute | solution.py:627
  (43 other events, 635.4 us)
